TPU v7x, 32 devices: a whole 2x2x4 slice. The times are simulated.
32 devices in a mesh: dp: 4 (over y, core), seq: 8 (over z, x).
Axes of the slice: x: 2, y: 2, z: 4, core: 2. Of those that a mesh axis runs over, the one named last changes fastest.
Arguments:
- tokens: bfloat16 [8, 2048, 1024], P('dp', 'seq'), may hold values from -6 to 6
- first_gain: float32 [1024], replicated, may hold values from 0.25 to 1.75
- first_shift: float32 [1024], replicated, may hold values from -1.5 to 1.5
- project_weight: bfloat16 [1024, 3072], replicated, may hold values from -0.1875 to 0.1875
- query_bias: float32 [1024], replicated, may hold values from -1.5 to 1.5
- value_bias: float32 [1024], replicated, may hold values from -1.5 to 1.5
- output_weight: bfloat16 [1024, 1024], replicated, may hold values from -1 to 1
- output_bias: float32 [1024], replicated, may hold values from -1.5 to 1.5
- second_gain: float32 [1024], replicated, may hold values from 0.25 to 1.75
- second_shift: float32 [1024], replicated, may hold values from -1.5 to 1.5
- up_weight: bfloat16 [1024, 4096], replicated, may hold values from -0.1875 to 0.1875
- up_bias: float32 [4096], replicated, may hold values from -1.5 to 1.5
- down_weight: bfloat16 [4096, 1024], replicated, may hold values from -0.09375 to 0.09375
- down_bias: float32 [1024], replicated, may hold values from -1.5 to 1.5
- doc_offsets: int32 [8, 4], P('dp'), may hold values from 0 to 2048, as said below
- exit_layers: int32 [8, 2048], P('dp'), may hold values from 1 to 24, as said below
- layer_index: int32 [1], replicated, may hold values from 6 to 11
- upstream: bfloat16 [8, 2048, 1024], P('dp', 'seq'), may hold values from -6 to 6
Outputs:
- result: bfloat16 [8, 2048, 1024], P('dp', 'seq')
- token_grad: bfloat16 [8, 2048, 1024], P('dp', 'seq')
- first_gain_grad: float32 [1024], P(('dp', 'seq'))
- first_shift_grad: float32 [1024], P(('dp', 'seq'))
- project_weight_grad: float32 [1024, 3072], P(('dp', 'seq'))
- query_bias_grad: float32 [1024], P(('dp', 'seq'))
- value_bias_grad: float32 [1024], P(('dp', 'seq'))
- output_weight_grad: float32 [1024, 1024], P(('dp', 'seq'))
- output_bias_grad: float32 [1024], P(('dp', 'seq'))
- second_gain_grad: float32 [1024], P(('dp', 'seq'))
- second_shift_grad: float32 [1024], P(('dp', 'seq'))
- up_weight_grad: float32 [1024, 4096], P(('dp', 'seq'))
- up_bias_grad: float32 [4096], P(('dp', 'seq'))
- down_weight_grad: float32 [4096, 1024], P(('dp', 'seq'))
- down_bias_grad: float32 [1024], P(('dp', 'seq'))
Inputs may be any that keep to these rules, and one draw needn't show every extreme that they name: `doc_offsets`: each row's offsets start at 0 and never fall; document j runs from offset j to offset j + 1 (the last to 2048); an offset of 2048 marks an empty document. In every aligned group of 2 rows one row has a document that begins within the first device's tokens of the row and ends within the last device's tokens. `exit_layers`: the first token of every document has exit layer 24.
All inputs are finite; a program needn't handle non-finite values.
Results may differ from a plain program's by a relative error of at most 0.011.
Values may be sent and summed in bfloat16 or wider, within the bound.
A program may use at most 192 MiB of HBM per device.

v0:
```python
import jax
import jax.numpy as jnp
from jax import lax
from jax.sharding import PartitionSpec as P

HEAD_DIM = 64


NEG_FILL = -1e30


def layer_norm(inputs, gain_vec, bias_vec):
    average = jnp.mean(inputs, axis=-1, keepdims=True)
    centred = inputs - average
    spread = jnp.mean(centred * centred, axis=-1, keepdims=True)
    return centred * lax.rsqrt(spread + 1e-05) * gain_vec + bias_vec


def gelu_tanh(inputs):
    return jax.nn.gelu(inputs, approximate=True)


def token_sum(values):
    return jnp.sum(values.astype(jnp.float32), axis=(0, 1))


def per_device(
    tokens,
    first_gain,
    first_shift,
    project_weight,
    query_bias,
    value_bias,
    output_weight,
    output_bias,
    second_gain,
    second_shift,
    up_weight,
    up_bias,
    down_weight,
    down_bias,
    doc_offsets,
    exit_layers,
    layer_index,
    upstream,
):
    group_size = lax.axis_size("seq")
    row_count, shard_len, model_width = tokens.shape
    seq_length = exit_layers.shape[1]
    local_width = model_width // group_size
    heads_here = local_width // HEAD_DIM
    score_scale = HEAD_DIM ** (-0.5)
    block_len = min(512, seq_length)
    block_count = seq_length // block_len
    first_here = lax.axis_index("seq") * shard_len
    key_pos = jnp.arange(seq_length, dtype=jnp.int32)
    doc_ids = jnp.sum(
        (doc_offsets[:, 1:, None] <= key_pos[None, None, :]).astype(jnp.int32), axis=1
    )
    active = exit_layers > layer_index[0]
    keep_mask = lax.dynamic_slice_in_dim(active, first_here, shard_len, 1).astype(jnp.float32)[
        :, :, None
    ]
    head_shape = (seq_length, heads_here, HEAD_DIM)
    residual = tokens.astype(jnp.float32)
    normed_full, first_back = jax.vjp(layer_norm, residual, first_gain, first_shift)
    normed = normed_full.astype(jnp.bfloat16)
    biases = jnp.stack([query_bias, jnp.zeros_like(query_bias), value_bias])
    mixed = jnp.einsum("rsd,df->rsf", normed, project_weight, preferred_element_type=jnp.float32)
    packed_qkv = (mixed.reshape(row_count, shard_len, 3, model_width) + biases).astype(jnp.bfloat16)
    head_rows = lax.all_to_all(packed_qkv, "seq", split_axis=3, concat_axis=1, tiled=True)

    def block_mask(doc_row, live_row, block_index):
        query_pos = block_index * block_len + jnp.arange(block_len, dtype=jnp.int32)
        query_docs = lax.dynamic_slice_in_dim(doc_row, block_index * block_len, block_len, 0)
        same_doc = query_docs[:, None] == doc_row[None, :]
        return same_doc & (key_pos[None, :] <= query_pos[:, None]) & live_row[None, :]

    def row_forward(packed):
        heads_row, doc_row, live_row = packed
        queries = heads_row[:, 0].reshape(head_shape)
        key_rows = heads_row[:, 1].reshape(head_shape)
        value_rows = heads_row[:, 2].reshape(head_shape)

        def block_forward(block_index):
            query_block = lax.dynamic_slice_in_dim(queries, block_index * block_len, block_len, 0)
            scores = (
                jnp.einsum(
                    "qhd,khd->hqk", query_block, key_rows, preferred_element_type=jnp.float32
                )
                * score_scale
            )
            masked = jnp.where(block_mask(doc_row, live_row, block_index)[None], scores, NEG_FILL)
            highest = jnp.max(masked, axis=2, keepdims=True)
            weights = jnp.exp(masked - highest)
            totals = jnp.sum(weights, axis=2, keepdims=True)
            weights_low = (weights / totals).astype(jnp.bfloat16)
            context = jnp.einsum(
                "hqk,khd->qhd", weights_low, value_rows, preferred_element_type=jnp.float32
            )
            return (context.astype(jnp.bfloat16), (highest + jnp.log(totals))[:, :, 0])

        contexts, logsums = lax.map(block_forward, jnp.arange(block_count))
        return (contexts.reshape(seq_length, local_width), logsums)

    head_context, logsums = lax.map(row_forward, (head_rows, doc_ids, active))
    context = lax.all_to_all(head_context, "seq", split_axis=1, concat_axis=2, tiled=True)
    attended = (
        jnp.einsum("rsd,de->rse", context, output_weight, preferred_element_type=jnp.float32)
        + output_bias
    )
    middle = residual + keep_mask * attended
    normed_two_full, second_back = jax.vjp(layer_norm, middle, second_gain, second_shift)
    normed_two = normed_two_full.astype(jnp.bfloat16)
    raised = (
        jnp.einsum("rsd,df->rsf", normed_two, up_weight, preferred_element_type=jnp.float32)
        + up_bias
    )
    activated, gelu_back = jax.vjp(gelu_tanh, raised)
    hidden = activated.astype(jnp.bfloat16)
    lowered = (
        jnp.einsum("rsf,fd->rsd", hidden, down_weight, preferred_element_type=jnp.float32)
        + down_bias
    )
    result = (middle + keep_mask * lowered).astype(jnp.bfloat16)
    incoming = upstream.astype(jnp.float32)
    down_in = (keep_mask * incoming).astype(jnp.bfloat16)
    grad_down_weight = jnp.einsum(
        "rsf,rsd->fd", hidden, down_in, preferred_element_type=jnp.float32
    )
    grad_down_bias = token_sum(down_in)
    hidden_grad = jnp.einsum(
        "rsd,fd->rsf", down_in, down_weight, preferred_element_type=jnp.float32
    )
    raised_grad = gelu_back(hidden_grad)[0].astype(jnp.bfloat16)
    grad_up_weight = jnp.einsum(
        "rsd,rsf->df", normed_two, raised_grad, preferred_element_type=jnp.float32
    )
    grad_up_bias = token_sum(raised_grad)
    normed_two_grad = jnp.einsum(
        "rsf,df->rsd", raised_grad, up_weight, preferred_element_type=jnp.float32
    )
    middle_part, grad_second_gain, grad_second_shift = second_back(normed_two_grad)
    middle_grad = incoming + middle_part
    attended_grad = (keep_mask * middle_grad).astype(jnp.bfloat16)
    grad_output_weight = jnp.einsum(
        "rsd,rse->de", context, attended_grad, preferred_element_type=jnp.float32
    )
    grad_output_bias = token_sum(attended_grad)
    context_grad = jnp.einsum(
        "rse,de->rsd", attended_grad, output_weight, preferred_element_type=jnp.float32
    ).astype(jnp.bfloat16)
    head_grad = lax.all_to_all(context_grad, "seq", split_axis=2, concat_axis=1, tiled=True)

    def row_backward(packed):
        heads_row, doc_row, live_row, row_sums, grad_row = packed
        queries = heads_row[:, 0].reshape(head_shape)
        key_rows = heads_row[:, 1].reshape(head_shape)
        value_rows = heads_row[:, 2].reshape(head_shape)
        grad_heads = grad_row.reshape(head_shape)

        def block_backward(carry, block_index):
            key_total, value_total = carry
            query_block = lax.dynamic_slice_in_dim(queries, block_index * block_len, block_len, 0)
            grad_block = lax.dynamic_slice_in_dim(grad_heads, block_index * block_len, block_len, 0)
            block_sums = lax.dynamic_index_in_dim(row_sums, block_index, 0, keepdims=False)
            scores = (
                jnp.einsum(
                    "qhd,khd->hqk", query_block, key_rows, preferred_element_type=jnp.float32
                )
                * score_scale
            )
            allowed = block_mask(doc_row, live_row, block_index)[None]
            weights = jnp.where(allowed, jnp.exp(scores - block_sums[:, :, None]), 0.0)
            weights_low = weights.astype(jnp.bfloat16)
            value_total = value_total + jnp.einsum(
                "hqk,qhd->khd", weights_low, grad_block, preferred_element_type=jnp.float32
            )
            weight_grad = jnp.einsum(
                "qhd,khd->hqk", grad_block, value_rows, preferred_element_type=jnp.float32
            )
            centre = jnp.sum(weights * weight_grad, axis=2, keepdims=True)
            score_grad = (weights * (weight_grad - centre)).astype(jnp.bfloat16)
            query_grad = (
                jnp.einsum("hqk,khd->qhd", score_grad, key_rows, preferred_element_type=jnp.float32)
                * score_scale
            )
            key_total = (
                key_total
                + jnp.einsum(
                    "hqk,qhd->khd", score_grad, query_block, preferred_element_type=jnp.float32
                )
                * score_scale
            )
            return ((key_total, value_total), query_grad)

        zeros = jnp.zeros(head_shape, jnp.float32)
        totals, query_grads = lax.scan(block_backward, (zeros, zeros), jnp.arange(block_count))
        stacked = jnp.stack(
            [
                query_grads.reshape(seq_length, local_width),
                totals[0].reshape(seq_length, local_width),
                totals[1].reshape(seq_length, local_width),
            ],
            axis=1,
        )
        return stacked.astype(jnp.bfloat16)

    head_qkv_grad = lax.map(row_backward, (head_rows, doc_ids, active, logsums, head_grad))
    qkv_grad = lax.all_to_all(head_qkv_grad, "seq", split_axis=1, concat_axis=3, tiled=True)
    flat_grad = qkv_grad.reshape(row_count, shard_len, 3 * model_width)
    grad_project = jnp.einsum("rsd,rsf->df", normed, flat_grad, preferred_element_type=jnp.float32)
    grad_query_bias = token_sum(qkv_grad[:, :, 0])
    grad_value_bias = token_sum(qkv_grad[:, :, 2])
    normed_grad = jnp.einsum(
        "rsf,df->rsd", flat_grad, project_weight, preferred_element_type=jnp.float32
    )
    input_part, grad_first_gain, grad_first_shift = first_back(normed_grad)
    token_grad = (middle_grad + input_part).astype(jnp.bfloat16)
    shares = (
        lax.psum_scatter(grad_first_gain, ("dp", "seq"), scatter_dimension=0, tiled=True),
        lax.psum_scatter(grad_first_shift, ("dp", "seq"), scatter_dimension=0, tiled=True),
        lax.psum_scatter(grad_project, ("dp", "seq"), scatter_dimension=0, tiled=True),
        lax.psum_scatter(grad_query_bias, ("dp", "seq"), scatter_dimension=0, tiled=True),
        lax.psum_scatter(grad_value_bias, ("dp", "seq"), scatter_dimension=0, tiled=True),
        lax.psum_scatter(grad_output_weight, ("dp", "seq"), scatter_dimension=0, tiled=True),
        lax.psum_scatter(grad_output_bias, ("dp", "seq"), scatter_dimension=0, tiled=True),
        lax.psum_scatter(grad_second_gain, ("dp", "seq"), scatter_dimension=0, tiled=True),
        lax.psum_scatter(grad_second_shift, ("dp", "seq"), scatter_dimension=0, tiled=True),
        lax.psum_scatter(grad_up_weight, ("dp", "seq"), scatter_dimension=0, tiled=True),
        lax.psum_scatter(grad_up_bias, ("dp", "seq"), scatter_dimension=0, tiled=True),
        lax.psum_scatter(grad_down_weight, ("dp", "seq"), scatter_dimension=0, tiled=True),
        lax.psum_scatter(grad_down_bias, ("dp", "seq"), scatter_dimension=0, tiled=True),
    )
    return (result, token_grad) + tuple(shares)


def solution(mesh):
    in_specs = (
        P("dp", "seq", None),
        P(),
        P(),
        P(),
        P(),
        P(),
        P(),
        P(),
        P(),
        P(),
        P(),
        P(),
        P(),
        P(),
        P("dp", None),
        P("dp", None),
        P(),
        P("dp", "seq", None),
    )
    out_specs = (
        P("dp", "seq", None),
        P("dp", "seq", None),
        P(("dp", "seq")),
        P(("dp", "seq")),
        P(("dp", "seq"), None),
        P(("dp", "seq")),
        P(("dp", "seq")),
        P(("dp", "seq"), None),
        P(("dp", "seq")),
        P(("dp", "seq")),
        P(("dp", "seq")),
        P(("dp", "seq"), None),
        P(("dp", "seq")),
        P(("dp", "seq"), None),
        P(("dp", "seq")),
    )
    return jax.shard_map(
        per_device, mesh=mesh, in_specs=in_specs, out_specs=out_specs, check_vma=False
    )
```

profile of v0, /device:TPU:0, one launch (start us, length us, event | category | flops | bytes accessed | tf_op | source)
XLA Modules:
  0.0 1589.4 jit_solution(17249946269366915103)
XLA Ops:
  11.8 6.2 fusion.58
  23.6 7.6 all-to-all-start
  32.2 69.8 %all-to-all-done = bf16[2,256,3,1024]{1,0,2,3:T(2,128)(2,1)} async-done(((bf16[2,256,3,1024]{1,0,2,3:T(2,128)(2,1)}), bf16[2,256,3,1024]{1,0,2,3:T(2,128)(2,1)}, u32[]{:S(2)}, u32[]{:S(2)}) %all-to-all-start) | async-done | bytes 3145760 | tf_op jit(solution)/shard_map/all_to_all | solution.py:71
  115.4 94.5 %while.54 = (s32[]{:T(128)}, bf16[2,2048,128]{1,2,0:T(8,128)(2,1)}, f32[2,4,2,512]{3,2,1,0:T(2,128)S(1)}, bf16[2,2048,3,128]{1,3,2,0:T(8,128)(2,1)}, s32[2,2048]...) while((s32[]{:T(128)}, bf16[2,2048,128]{1,2,0:T(8,128)(2,1)}, ...), condition=%wide.region_8.9_spmd.clone, body=%wide.region_3.8_spmd.clone.sunk | while | flops 566296064 | bytes 40231904 | solution.py:106
  118.1 42.9 %while.57 = (s32[]{:T(128)}, bf16[4,512,2,64]{1,3,2,0:T(8,128)(2,1)S(1)}, f32[4,2,512]{2,1,0:T(2,128)S(1)}, s32[4]{0:T(128)S(1)}, s32[2048]{0:T(1024)S(1)}, /*in...) while((s32[]{:T(128)}, ...), condition=%wide.region_7.7_spmd, body=%wide.region_4.6_spmd.sunk | while | flops 566296064 | bytes 30732500 | solution.py:103
  165.3 42.9 %while.57 = (s32[]{:T(128)}, bf16[4,512,2,64]{1,3,2,0:T(8,128)(2,1)S(1)}, f32[4,2,512]{2,1,0:T(2,128)S(1)}, s32[4]{0:T(128)S(1)}, s32[2048]{0:T(1024)S(1)}, /*in...) while((s32[]{:T(128)}, ...), condition=%wide.region_7.7_spmd, body=%wide.region_4.6_spmd.sunk | while | flops 566296064 | bytes 30732500 | solution.py:103
  218.2 25.6 %all-to-all-done.1 = bf16[2,2048,128]{2,0,1:T(2,128)(2,1)} async-done(((bf16[2,2048,128]{2,0,1:T(2,128)(2,1)}), bf16[2,2048,128]{2,0,1:T(2,128)(2,1)}, u32[]{:S(2)}, u32[]{:S(2)}) %all-to-all-start.1) | async-done | bytes 1048608 | tf_op jit(solution)/shard_map/all_to_all | solution.py:107
  252.1 10.6 fusion.54
  262.8 14.4 convert_reduce_fusion
  298.9 26.1 %all-to-all-done.2 = bf16[2,256,1024]{1,0,2:T(2,128)(2,1)S(1)} async-done(((bf16[2,256,1024]{1,0,2:T(2,128)(2,1)}), bf16[2,256,1024]{1,0,2:T(2,128)(2,1)S(1)}, u32[]{:S(2)}, u32[]{:S(2)}) %all-to-all-start.2) | async-done | bytes 1048608 | tf_op jit(solution)/shard_map/all_to_all | solution.py:153
  327.1 275.7 %while.56 = (s32[]{:T(128)}, bf16[2,2048,3,128]{1,3,2,0:T(8,128)(2,1)}, bf16[2,2048,3,128]{1,3,2,0:T(8,128)(2,1)}, bf16[2,2048,128]{1,2,0:T(8,128)(2,1)}, f32[2,...) while((s32[]{:T(128)}, ...), condition=%wide.region_17.18_spmd.clone, body=%wide.region_13.17_spmd.clone.sunk | while | flops 1384447488 | bytes 148231872 | solution.py:209
  331.5 129.1 %while.58 = (s32[]{:T(128)}, f32[2048,2,64]{0,2,1:T(8,128)S(1)}, f32[2048,2,64]{0,2,1:T(8,128)}, bf16[4,512,2,64]{1,3,2,0:T(8,128)(2,1)}, s32[4]{0:T(128)S(1)}, ...) while((s32[]{:T(128)}, f32[2048,2,64]{0,2,1:T(8,128)S(1)}, ...), condition=%wide.region_16.16_spmd.clone, body=%wide.region_14.15_spmd.clone.sunk | while | flops 1379204608 | bytes 132440952 | solution.py:198
  373.3 5.9 multiply_reduce_fusion.5
  405.6 5.9 multiply_reduce_fusion.5
  438.1 5.8 multiply_reduce_fusion.5
  469.6 128.7 %while.58 = (s32[]{:T(128)}, f32[2048,2,64]{0,2,1:T(8,128)S(1)}, f32[2048,2,64]{0,2,1:T(8,128)}, bf16[4,512,2,64]{1,3,2,0:T(8,128)(2,1)}, s32[4]{0:T(128)S(1)}, ...) while((s32[]{:T(128)}, f32[2048,2,64]{0,2,1:T(8,128)S(1)}, ...), condition=%wide.region_16.16_spmd.clone, body=%wide.region_14.15_spmd.clone.sunk | while | flops 1379204608 | bytes 132440952 | solution.py:198
  479.4 5.8 multiply_reduce_fusion.5
  511.3 5.8 multiply_reduce_fusion.5
  543.6 5.8 multiply_reduce_fusion.5
  575.8 5.8 multiply_reduce_fusion.5
  602.8 8.7 copy.121
  611.6 74.6 %all_to_all.72 = bf16[2,2048,3,128]{3,0,2,1:T(2,128)(2,1)S(1)} all-to-all(bf16[2,2048,3,128]{3,0,2,1:T(2,128)(2,1)} %copy.121), channel_id=1, replica_groups=mesh['dp'=4,'seq'=8] {'seq'}, dimensions={1} | all-to-all | bytes 6291456 | tf_op jit(solution)/shard_map/all_to_all | solution.py:210
  692.0 5.9 reshape.347
  697.9 8.4 convolution_bitcast_fusion.2
  708.0 11.1 convolution_bitcast_fusion.1
  719.8 17.3 %convolution_bitcast_fusion = f32[4096,1024]{1,0:T(8,128)} fusion(bf16[2,256,1024]{2,1,0:T(8,128)(2,1)} %param.43, f32[2,256]{1,0:T(2,128)S(1)} %copy-done.28, f32[2,256,4096]{2,1,0:T(8,128)} %fusion.54, f32[4096]{0:T(1024)S(1)} %copy-done.37), kind=kOutput, calls=%fused_computation.61 | convolution fusion | flops 4317511680 | bytes 26232832 | tf_op jit(solution)/shard_map/rsf,rsd->fd/dot_general | solution.py:128
  737.8 13.1 add_convert_fusion.2
  757.8 6.8 fusion.93
  767.0 42.4 %all-reduce.9 = (f32[1024]{0:T(1024)S(1)}, f32[1024]{0:T(1024)S(1)}, f32[1024]{0:T(1024)S(1)}, f32[1024]{0:T(1024)S(1)}, f32[1024]{0:T(1024)S(1)}, /*index=5*/f3...) all-reduce(f32[1024]{0:T(1024)S(1)} %get-tuple-element.364, ...), channel_id=2, replica_groups=mesh['dp'=4,'seq'=8] {'dp','seq'}, use_global_device_ids=true, to_apply=%region_21.22.clone | all-reduce | flops 12288 | bytes 98304
  818.6 43.4 %reduce-scatter.5.cloned.1.call-done = f32[32,3072]{1,0:T(8,128)} async-done(((f32[1024,3072]{1,0:T(8,128)}), f32[32,3072]{1,0:T(8,128)}) %reduce-scatter.5.cloned.1.call-update) | async-done | bytes 393232 | tf_op jit(solution)/shard_map/reduce_scatter | solution.py:223
  862.0 360.1 %reduce-scatter.9.cloned.1.call-done = f32[32,4096]{1,0:T(8,128)} async-done(((f32[1024,4096]{1,0:T(8,128)}), f32[32,4096]{1,0:T(8,128)}) %reduce-scatter.9.cloned.1.call-update) | async-done | bytes 524304 | tf_op jit(solution)/shard_map/reduce_scatter | solution.py:230
  1222.1 360.3 %reduce-scatter.11.cloned.1.call-done = f32[128,1024]{1,0:T(8,128)} async-done(((f32[4096,1024]{1,0:T(8,128)}), f32[128,1024]{1,0:T(8,128)}) %reduce-scatter.11.cloned.1.call-update) | async-done | bytes 524304 | tf_op jit(solution)/shard_map/reduce_scatter | solution.py:232
  (412 shorter events, 393.5 us)
Async XLA Ops:
  7.2 241.8 %copy-start = (bf16[1024,1024]{1,0:T(8,128)(2,1)S(1)}, bf16[1024,1024]{1,0:T(8,128)(2,1)}, u32[]{:S(2)}) copy-start(bf16[1024,1024]{1,0:T(8,128)(2,1)} %param.32) | copy-start | bytes 6291460
  8.8 9.3 copy-start.12
  10.5 7.6 copy-start.16
  23.6 8.3 copy-start.35
  23.6 8.6 copy-start.26
  23.6 78.4 %all-to-all-start = ((bf16[2,256,3,1024]{1,0,2,3:T(2,128)(2,1)}), bf16[2,256,3,1024]{1,0,2,3:T(2,128)(2,1)}, u32[]{:S(2)}, u32[]{:S(2)}) async-start(bf16[2,256,3,1024]{1,0,2,3:T(2,128)(2,1)} %copy.111), calls=%async_computation | async-start | bytes 6291456 | tf_op jit(solution)/shard_map/all_to_all | solution.py:71
  213.6 35.4 %copy-start.5 = (bf16[2,256,1024]{2,1,0:T(8,128)(2,1)S(1)}, bf16[2,256,1024]{2,1,0:T(8,128)(2,1)}, u32[]{:S(2)}) copy-start(bf16[2,256,1024]{2,1,0:T(8,128)(2,1)} %param.26) | copy-start | bytes 3145732
  213.6 35.4 %copy-start.38 = (f32[1024]{0:T(1024)S(1)}, f32[1024]{0:T(1024)}, u32[]{:S(2)}) copy-start(f32[1024]{0:T(1024)} %param.33) | copy-start | bytes 12292
  213.6 30.3 %all-to-all-start.1 = ((bf16[2,2048,128]{2,0,1:T(2,128)(2,1)}), bf16[2,2048,128]{2,0,1:T(2,128)(2,1)}, u32[]{:S(2)}, u32[]{:S(2)}) async-start(bf16[2,2048,128]{2,0,1:T(2,128)(2,1)} %copy.116), calls=%async_computation.1 | async-start | bytes 2097152 | tf_op jit(solution)/shard_map/all_to_all | solution.py:107
  218.2 65.2 %copy-start.27 = (f32[2,256]{1,0:T(2,128)}, f32[2,256]{1,0:T(2,128)S(1)}, u32[]{:S(2)}) copy-start(f32[2,256]{1,0:T(2,128)S(1)} %dynamic-slice_convert_fusion) | copy-start | bytes 6148
  251.7 31.0 %copy-start.8 = (f32[2,256,1024]{2,1,0:T(8,128)}, f32[2,256,1024]{2,1,0:T(8,128)S(1)}, u32[]{:S(2)}) copy-start(f32[2,256,1024]{2,1,0:T(8,128)S(1)} %get-tuple-element.468) | copy-start | bytes 6291460
  251.7 30.9 %copy-start.20 = (f32[2,256]{1,0:T(2,128)}, f32[2,256]{1,0:T(2,128)S(1)}, u32[]{:S(2)}) copy-start(f32[2,256]{1,0:T(2,128)S(1)} %broadcast_multiply_fusion) | copy-start | bytes 6148
  252.1 30.6 %copy-start.29 = (f32[2,256]{1,0:T(2,128)}, f32[2,256]{1,0:T(2,128)S(1)}, u32[]{:S(2)}) copy-start(f32[2,256]{1,0:T(2,128)S(1)} %fusion.92) | copy-start | bytes 6148
  252.1 10.7 copy-start.10
  252.1 10.7 copy-start.36
  252.1 25.0 %slice-start.2 = ((s8[8388608]{0:T(1024)(128)(4,1)}), s8[4194304]{0:T(1024)(128)(4,1)S(1)}, s32[]{:S(2)}) async-start(s8[8388608]{0:T(1024)(128)(4,1)} %bitcast.220), calls=%async_computation.14 | async-start | bytes 8388608
  262.8 14.4 slice-start.3
  292.0 33.1 %all-to-all-start.2 = ((bf16[2,256,1024]{1,0,2:T(2,128)(2,1)}), bf16[2,256,1024]{1,0,2:T(2,128)(2,1)S(1)}, u32[]{:S(2)}, u32[]{:S(2)}) async-start(bf16[2,256,1024]{1,0,2:T(2,128)(2,1)} %copy.118), calls=%async_computation.2 | async-start | bytes 2097152 | tf_op jit(solution)/shard_map/all_to_all | solution.py:153
  295.5 523.1 %reduce-scatter.7.cloned.1.call-start = ((), (), s32[]{:S(2)}) async-start(), calls=%async_computation.9 | async-start | bytes 4325376 | tf_op jit(solution)/shard_map/reduce_scatter | solution.py:226
  298.9 563.1 %reduce-scatter.5.cloned.1.call-start = ((), (), s32[]{:S(2)}) async-start(), calls=%async_computation.8 | async-start | bytes 12976128 | tf_op jit(solution)/shard_map/reduce_scatter | solution.py:223
  351.1 8.0 copy-start.2
  383.1 8.0 copy-start.2
  415.5 8.0 copy-start.2
  447.9 8.0 copy-start.2
  489.2 8.0 copy-start.2
  521.0 8.0 copy-start.2
  553.3 8.0 copy-start.2
  585.6 8.0 copy-start.2
  706.4 515.6 %reduce-scatter.9.cloned.1.call-start = ((), (), s32[]{:S(2)}) async-start(), calls=%async_computation.10 | async-start | bytes 17301504 | tf_op jit(solution)/shard_map/reduce_scatter | solution.py:230
  719.1 863.2 %reduce-scatter.11.cloned.1.call-start = ((), (), s32[]{:S(2)}) async-start(), calls=%async_computation.11 | async-start | bytes 17301504 | tf_op jit(solution)/shard_map/reduce_scatter | solution.py:232
  764.6 50.0 %copy-start.15 = (f32[2,256]{1,0:T(2,128)S(1)}, f32[2,256]{1,0:T(2,128)}, u32[]{:S(2)}) copy-start(f32[2,256]{1,0:T(2,128)} %copy-done.14) | copy-start | bytes 6148
  814.6 767.7 %copy-start.1 = (bf16[1024,1024]{1,0:T(8,128)(2,1)S(1)}, bf16[1024,1024]{1,0:T(8,128)(2,1)}, u32[]{:S(2)}) copy-start(bf16[1024,1024]{1,0:T(8,128)(2,1)} %param.32) | copy-start | bytes 6291460
  (44 other events, 182.0 us)
Sparse Core Ops, SparseCore 0:
  299.2 150.0 reduce-scatter.6
  706.6 155.3 reduce-scatter.4
  864.9 357.0 reduce-scatter.8
  1224.9 357.3 reduce-scatter.10
where the time goes:
time: 1600 us; the launch traced here: 1590 us
  waiting for transfers between devices  885 us (55%)
  matrix products  339 us (21%)
  blocking collectives  117 us (7%)
  local copies, waits for them, and re-layouts  103 us (6%)
  other arithmetic  87.1 us (5%)
  loops' own time  27.1 us (2%)
  starting transfers between devices  16.2 us (1%)
    reduce_scatter x1, waiting for transfers between devices, per_device(): lax.psum_scatter(grad_down_weight, ('dp', 'seq'), scatter_dimension=0, ti...  360 us
    reduce_scatter x1, waiting for transfers between devices, per_device(): lax.psum_scatter(grad_up_weight, ('dp', 'seq'), scatter_dimension=0, tile...  360 us
    all_to_all x1, blocking collectives, per_device(): lax.all_to_all(head_qkv_grad, 'seq', split_axis=1, concat_axis=3, tiled=T...  74.6 us
    all_to_all x1, waiting for transfers between devices, per_device(): lax.all_to_all(packed_qkv, 'seq', split_axis=3, concat_axis=1, tiled=True)  69.8 us
    dot_general x8, matrix products, block_backward(): jnp.einsum('qhd,khd->hqk', grad_block, value_rows, preferred_element_type...  46.7 us
    reduce_scatter x1, waiting for transfers between devices, per_device(): lax.psum_scatter(grad_project, ('dp', 'seq'), scatter_dimension=0, tiled=...  43.4 us
    dot_general x8, matrix products, block_backward(): jnp.einsum('qhd,khd->hqk', query_block, key_rows, preferred_element_type=...  43.4 us
    unnamed x1, blocking collectives  42.4 us
  transfers between devices with their start and end apart: 7, of which 6 were waited for; matrix products, arithmetic and copies ran while one was open for 22% of the time, Pallas kernels for 0%

commit v1 on v0

v1 whole, which is shorter than its diff:
```python
import functools

import jax
import jax.numpy as jnp
from jax import lax
from jax.experimental import pallas as pl
from jax.experimental.pallas import tpu as pltpu
from jax.sharding import PartitionSpec as P

HEAD_DIM = 64
SCALE = HEAD_DIM**-0.5
TILE = 256
FAR = 2**30
NEG = -1e30
EPS = 1e-05
VMEM_LIMIT = 56 * 2**20
F32 = jnp.float32
BF16 = jnp.bfloat16

NT = (((1,), (1,)), ((), ()))
NN = (((1,), (0,)), ((), ()))


def dot(a, b, dims=NN):
    return lax.dot_general(a, b, dims, preferred_element_type=F32)


def any_spec():
    return pl.BlockSpec(memory_space=pltpu.VMEM)


def params(**kw):
    return pltpu.CompilerParams(vmem_limit_bytes=VMEM_LIMIT, **kw)


def centre_rows(x):
    centred = x - jnp.mean(x, axis=-1, keepdims=True)
    spread = jnp.mean(centred * centred, axis=-1, keepdims=True)
    rs = lax.rsqrt(spread + EPS)
    return centred * rs, rs


def qkv_kernel(group, me_ref, x_ref, gain_ref, shift_ref, w_ref, bias_ref, normed_ref, *outs):
    step = pl.program_id(0)

    @pl.when(step == 0)
    def _():
        n, _ = centre_rows(x_ref[...].astype(F32))
        normed_ref[...] = (n * gain_ref[...] + shift_ref[...]).astype(BF16)

    value = (dot(normed_ref[...], w_ref[0]) + bias_ref[0]).astype(BF16)
    for m in range(group):

        @pl.when(step == m)
        def _(m=m):
            outs[m][...] = value


def qkv_chunks(me, x, gain, shift, w_parts, bias_parts):
    group, width, cols = w_parts.shape
    rows = x.shape[0]
    whole = lambda m, me_ref: (0, 0)
    out = pl.pallas_call(
        functools.partial(qkv_kernel, group),
        grid_spec=pltpu.PrefetchScalarGridSpec(
            num_scalar_prefetch=1,
            grid=(group,),
            in_specs=[
                pl.BlockSpec((rows, width), whole),
                pl.BlockSpec((1, width), whole),
                pl.BlockSpec((1, width), whole),
                pl.BlockSpec((1, width, cols), lambda m, me_ref: (m ^ me_ref[0], 0, 0)),
                pl.BlockSpec((1, 1, cols), lambda m, me_ref: (m ^ me_ref[0], 0, 0)),
            ],
            out_specs=[pl.BlockSpec((rows, width), whole)]
            + [pl.BlockSpec((rows, cols), whole)] * group,
        ),
        out_shape=[jax.ShapeDtypeStruct((rows, width), BF16)]
        + [jax.ShapeDtypeStruct((rows, cols), BF16)] * group,
        compiler_params=params(),
        cost_estimate=pl.CostEstimate(
            flops=2 * rows * width * cols * group,
            bytes_accessed=2 * group * cols * (width + rows),
            transcendentals=0,
        ),
        name="norm_project",
    )(me, x, gain[None], shift[None], w_parts, bias_parts)
    return out[0], out[1:]


def head_mask(rows, wide, head):
    lane = lax.broadcasted_iota(jnp.int32, (rows, wide), 1)
    return lane // HEAD_DIM == head


def only_head(block, head, heads):
    if heads == 1:
        return block
    return jnp.where(head_mask(*block.shape, head), block, jnp.zeros_like(block))


def transposed(block):
    return block.astype(F32).T.astype(BF16)


def visible(key_pos, starts, spots, diagonal):
    seen = key_pos >= starts
    if diagonal:
        seen = seen & (key_pos <= spots)
    return seen


def attend_kernel(group, cap, tiles, heads, sc_ref, *refs):
    parts, refs = refs[:group], refs[group:]
    kp_ref, starts_ref, spots_ref = refs[:3]
    outs, refs = refs[3 : 3 + group], refs[3 + group :]
    lse_ref, q_s, k_s, v_s, vt_s, o_s = refs
    wide = heads * HEAD_DIM
    me = sc_ref[0]
    row = pl.program_id(0)
    for m in range(group):
        here = pl.ds(pl.multiple_of((me ^ m) * cap, cap), cap)
        q_s[here, :] = parts[m][:, :wide] * SCALE
        k_s[here, :] = parts[m][:, wide : 2 * wide]
        v_s[here, :] = parts[m][:, 2 * wide :]
    for t in range(tiles):
        vt_s[t] = transposed(v_s[t * TILE : (t + 1) * TILE, :])

    def one_tile(i, _):
        at = pl.ds(pl.multiple_of(i * TILE, TILE), TILE)
        queries = q_s[at, :]
        split = [only_head(queries, h, heads) for h in range(heads)]
        starts = starts_ref[0, i]
        spots = spots_ref[0, i]

        def step(j, carry, diagonal):
            there = pl.ds(pl.multiple_of(j * TILE, TILE), TILE)
            seen = visible(kp_ref[0, there, :], starts, spots, diagonal)
            keys = k_s[there, :]
            new = []
            for h in range(heads):
                top, total, acc = carry[h]
                s = jnp.where(seen, dot(keys, split[h], NT), NEG)
                top2 = jnp.maximum(top, jnp.max(s, axis=0, keepdims=True))
                p = jnp.exp(s - top2)
                fade = jnp.exp(top - top2)
                total = total * fade + jnp.sum(p, axis=0, keepdims=True)
                vt = vt_s[j, h * HEAD_DIM : (h + 1) * HEAD_DIM, :]
                acc = acc * fade + dot(vt, p.astype(BF16))
                new.append((top2, total, acc))
            return tuple(new)

        first = tuple(
            (
                jnp.full((1, TILE), NEG, F32),
                jnp.zeros((1, TILE), F32),
                jnp.zeros((HEAD_DIM, TILE), F32),
            )
            for _ in range(heads)
        )
        low = sc_ref[1 + row * tiles + i]
        carry = lax.fori_loop(low, i, lambda j, c: step(j, c, False), first)
        carry = step(i, carry, True)
        pieces = []
        for h in range(heads):
            top, total, acc = carry[h]
            pieces.append(acc * (1.0 / total))
            lse_ref[0, i, h : h + 1, :] = top + jnp.log(total)
        o_s[at, :] = jnp.concatenate(pieces, axis=0).T.astype(BF16)
        return 0

    lax.fori_loop(0, tiles, one_tile, 0)
    for m in range(group):
        outs[m][...] = o_s[pl.ds(pl.multiple_of((me ^ m) * cap, cap), cap), :]


def attend(scalars, parts, key_pos, starts, spots, cap, heads):
    group = len(parts)
    rows = parts[0].shape[0] // cap
    cols = parts[0].shape[1]
    length = group * cap
    tiles = length // TILE
    wide = heads * HEAD_DIM
    pair = rows * heads * length * length // 2 * HEAD_DIM
    by_row = lambda r, sc: (r, 0)
    out = pl.pallas_call(
        functools.partial(attend_kernel, group, cap, tiles, heads),
        grid_spec=pltpu.PrefetchScalarGridSpec(
            num_scalar_prefetch=1,
            grid=(rows,),
            in_specs=[pl.BlockSpec((cap, cols), by_row)] * group
            + [
                pl.BlockSpec((1, length, 1), lambda r, sc: (r, 0, 0)),
                pl.BlockSpec((1, tiles, 1, TILE), lambda r, sc: (r, 0, 0, 0)),
                pl.BlockSpec((1, tiles, 1, TILE), lambda r, sc: (r, 0, 0, 0)),
            ],
            out_specs=[pl.BlockSpec((cap, wide), by_row)] * group
            + [pl.BlockSpec((1, tiles, heads, TILE), lambda r, sc: (r, 0, 0, 0))],
            scratch_shapes=[
                pltpu.VMEM((length, wide), BF16),
                pltpu.VMEM((length, wide), BF16),
                pltpu.VMEM((length, wide), BF16),
                pltpu.VMEM((tiles, wide, TILE), BF16),
                pltpu.VMEM((length, wide), BF16),
            ],
        ),
        out_shape=[jax.ShapeDtypeStruct((rows * cap, wide), BF16)] * group
        + [jax.ShapeDtypeStruct((rows, tiles, heads, TILE), F32)],
        compiler_params=params(),
        cost_estimate=pl.CostEstimate(
            flops=4 * 4 * pair, bytes_accessed=8 * rows * length * wide, transcendentals=pair // 32
        ),
        name="attend",
    )(scalars, *parts, key_pos, starts, spots)
    return out[:group], out[group]


def attend_back_kernel(group, cap, tiles, heads, sc_ref, *refs):
    parts, refs = refs[:group], refs[group:]
    ctx, refs = refs[:group], refs[group:]
    grads, refs = refs[:group], refs[group:]
    kp_ref, starts_ref, spots_ref, lse_ref = refs[:4]
    outs, refs = refs[4 : 4 + group], refs[4 + group :]
    q_s, k_s, v_s, kt_s, g_s, o_s, dq_s, dk_s, dv_s = refs
    wide = heads * HEAD_DIM
    me = sc_ref[0]
    row = pl.program_id(0)
    for m in range(group):
        here = pl.ds(pl.multiple_of((me ^ m) * cap, cap), cap)
        q_s[here, :] = parts[m][:, :wide] * SCALE
        k_s[here, :] = parts[m][:, wide : 2 * wide]
        v_s[here, :] = parts[m][:, 2 * wide :]
        g_s[here, :] = grads[m][...]
        o_s[here, :] = ctx[m][...]
    for t in range(tiles):
        kt_s[t] = transposed(k_s[t * TILE : (t + 1) * TILE, :])
    dk_s[...] = jnp.zeros_like(dk_s)
    dv_s[...] = jnp.zeros_like(dv_s)

    def one_tile(i, _):
        at = pl.ds(pl.multiple_of(i * TILE, TILE), TILE)
        queries = q_s[at, :]
        grad = g_s[at, :]
        starts = starts_ref[0, i]
        spots = spots_ref[0, i]
        product = (grad.astype(F32) * o_s[at, :].astype(F32)).T
        split_q = [only_head(queries, h, heads) for h in range(heads)]
        split_g = [only_head(grad, h, heads) for h in range(heads)]
        delta = [
            jnp.sum(product[h * HEAD_DIM : (h + 1) * HEAD_DIM], axis=0, keepdims=True)
            for h in range(heads)
        ]
        lse = [lse_ref[0, i, h : h + 1, :] for h in range(heads)]

        def step(j, carry, diagonal):
            there = pl.ds(pl.multiple_of(j * TILE, TILE), TILE)
            seen = visible(kp_ref[0, there, :], starts, spots, diagonal)
            keys = k_s[there, :]
            values = v_s[there, :]
            new = []
            dk = dk_s[there, :]
            dv = dv_s[there, :]
            for h in range(heads):
                s = dot(keys, split_q[h], NT)
                p = jnp.where(seen, jnp.exp(s - lse[h]), 0.0)
                dp = dot(values, split_g[h], NT)
                ds = (p * (dp - delta[h])).astype(BF16)
                dv = dv + dot(p.astype(BF16), split_g[h])
                dk = dk + dot(ds, split_q[h])
                kt = kt_s[j, h * HEAD_DIM : (h + 1) * HEAD_DIM, :]
                new.append(carry[h] + dot(kt, ds))
            dk_s[there, :] = dk
            dv_s[there, :] = dv
            return tuple(new)

        first = tuple(jnp.zeros((HEAD_DIM, TILE), F32) for _ in range(heads))
        low = sc_ref[1 + row * tiles + i]
        carry = lax.fori_loop(low, i, lambda j, c: step(j, c, False), first)
        carry = step(i, carry, True)
        dq_s[at, :] = (jnp.concatenate(carry, axis=0).T * SCALE).astype(BF16)
        return 0

    lax.fori_loop(0, tiles, one_tile, 0)
    for m in range(group):
        here = pl.ds(pl.multiple_of((me ^ m) * cap, cap), cap)
        outs[m][:, :wide] = dq_s[here, :]
        outs[m][:, wide : 2 * wide] = dk_s[here, :].astype(BF16)
        outs[m][:, 2 * wide :] = dv_s[here, :].astype(BF16)


def attend_back(scalars, parts, ctx, grads, key_pos, starts, spots, lse, cap, heads):
    group = len(parts)
    rows = parts[0].shape[0] // cap
    cols = parts[0].shape[1]
    length = group * cap
    tiles = length // TILE
    wide = heads * HEAD_DIM
    pair = rows * heads * length * length // 2 * HEAD_DIM
    by_row = lambda r, sc: (r, 0)
    return pl.pallas_call(
        functools.partial(attend_back_kernel, group, cap, tiles, heads),
        grid_spec=pltpu.PrefetchScalarGridSpec(
            num_scalar_prefetch=1,
            grid=(rows,),
            in_specs=[pl.BlockSpec((cap, cols), by_row)] * group
            + [pl.BlockSpec((cap, wide), by_row)] * (2 * group)
            + [
                pl.BlockSpec((1, length, 1), lambda r, sc: (r, 0, 0)),
                pl.BlockSpec((1, tiles, 1, TILE), lambda r, sc: (r, 0, 0, 0)),
                pl.BlockSpec((1, tiles, 1, TILE), lambda r, sc: (r, 0, 0, 0)),
                pl.BlockSpec((1, tiles, heads, TILE), lambda r, sc: (r, 0, 0, 0)),
            ],
            out_specs=[pl.BlockSpec((cap, cols), by_row)] * group,
            scratch_shapes=[pltpu.VMEM((length, wide), BF16)] * 3
            + [pltpu.VMEM((tiles, wide, TILE), BF16)]
            + [pltpu.VMEM((length, wide), BF16)] * 3
            + [pltpu.VMEM((length, wide), F32)] * 2,
        ),
        out_shape=[jax.ShapeDtypeStruct((rows * cap, cols), BF16)] * group,
        compiler_params=params(),
        cost_estimate=pl.CostEstimate(
            flops=10 * 4 * pair, bytes_accessed=20 * rows * length * wide, transcendentals=pair // 32
        ),
        name="attend_back",
    )(scalars, *parts, *ctx, *grads, key_pos, starts, spots, lse)


def gather_parts(me, parts, ordered):
    for m in range(len(parts)):
        ordered[me ^ m] = parts[m][...]


def output_kernel(group, sc_ref, *refs):
    parts, refs = refs[:group], refs[group:]
    x_ref, w_ref, bias_ref, gain_ref, shift_ref, ctx_ref, mid_ref, normed_ref, ordered = refs
    wide = parts[0].shape[1]
    gather_parts(sc_ref[0], parts, ordered)
    for s in range(group):
        ctx_ref[:, s * wide : (s + 1) * wide] = ordered[s]
    mid = x_ref[...].astype(F32) + dot(ctx_ref[...], w_ref[...]) + bias_ref[...]
    mid_ref[...] = mid
    n, _ = centre_rows(mid)
    normed_ref[...] = (n * gain_ref[...] + shift_ref[...]).astype(BF16)


def output_project(me, parts, x, w, bias, gain, shift):
    group = len(parts)
    rows, width = x.shape
    wide = parts[0].shape[1]
    return pl.pallas_call(
        functools.partial(output_kernel, group),
        in_specs=[pl.BlockSpec(memory_space=pltpu.SMEM)] + [any_spec()] * (group + 5),
        out_specs=[any_spec()] * 3,
        out_shape=[
            jax.ShapeDtypeStruct((rows, width), BF16),
            jax.ShapeDtypeStruct((rows, width), F32),
            jax.ShapeDtypeStruct((rows, width), BF16),
        ],
        scratch_shapes=[pltpu.VMEM((group, rows, wide), BF16)],
        compiler_params=params(),
        cost_estimate=pl.CostEstimate(
            flops=2 * rows * width * width,
            bytes_accessed=2 * width * width + 12 * rows * width,
            transcendentals=0,
        ),
        name="output_project",
    )(me, *parts, x, w, bias[None], gain[None], shift[None])


def mid_back_kernel(
    group, sc_ref, n2_ref, mid_ref, g_ref, gain_ref, w_ref, mg_ref, ag_ref, gg_ref, gs_ref, bo_ref, *rest
):
    outs, ordered = rest[:group], rest[group]
    n, rs = centre_rows(mid_ref[...])
    n2 = n2_ref[...]
    gg_ref[...] = jnp.sum(n2 * n, axis=0, keepdims=True)
    gs_ref[...] = jnp.sum(n2, axis=0, keepdims=True)
    e = n2 * gain_ref[...]
    part = rs * (
        e - jnp.mean(e, axis=-1, keepdims=True) - n * jnp.mean(e * n, axis=-1, keepdims=True)
    )
    mid_grad = g_ref[...].astype(F32) + part
    mg_ref[...] = mid_grad
    attn = mid_grad.astype(BF16)
    ag_ref[...] = attn
    bo_ref[...] = jnp.sum(attn.astype(F32), axis=0, keepdims=True)
    full = dot(attn, w_ref[...], NT).astype(BF16)
    wide = outs[0].shape[1]
    for s in range(group):
        ordered[s] = full[:, s * wide : (s + 1) * wide]
    for m in range(group):
        outs[m][...] = ordered[sc_ref[0] ^ m]


def mid_back(me, n2_grad, mid, g, gain, w, group):
    rows, width = mid.shape
    wide = width // group
    vec = jax.ShapeDtypeStruct((1, width), F32)
    out = pl.pallas_call(
        functools.partial(mid_back_kernel, group),
        in_specs=[pl.BlockSpec(memory_space=pltpu.SMEM)] + [any_spec()] * 5,
        out_specs=[any_spec()] * (5 + group),
        out_shape=[
            jax.ShapeDtypeStruct((rows, width), F32),
            jax.ShapeDtypeStruct((rows, width), BF16),
            vec,
            vec,
            vec,
        ]
        + [jax.ShapeDtypeStruct((rows, wide), BF16)] * group,
        scratch_shapes=[pltpu.VMEM((group, rows, wide), BF16)],
        compiler_params=params(),
        cost_estimate=pl.CostEstimate(
            flops=2 * rows * width * width,
            bytes_accessed=2 * width * width + 18 * rows * width,
            transcendentals=0,
        ),
        name="mid_back",
    )(me, n2_grad, mid, g, gain[None], w)
    return out[0], out[1], out[2][0], out[3][0], out[4][0], out[5:]


def input_back_kernel(group, sc_ref, *refs):
    parts, refs = refs[:group], refs[group:]
    w_ref, x_ref, mg_ref, gain_ref, flat_ref, tg_ref, gg_ref, gs_ref, gb_ref, ordered, acc = refs
    s = pl.program_id(0)
    cols = parts[0].shape[1]

    @pl.when(s == 0)
    def _():
        gather_parts(sc_ref[0], parts, ordered)
        for k in range(group):
            flat_ref[:, k * cols : (k + 1) * cols] = ordered[k]
            gb_ref[:, k * cols : (k + 1) * cols] = jnp.sum(
                ordered[k].astype(F32), axis=0, keepdims=True
            )
        acc[...] = jnp.zeros_like(acc)

    acc[...] += dot(ordered[s], w_ref[0], NT)

    @pl.when(s == group - 1)
    def _():
        n, rs = centre_rows(x_ref[...].astype(F32))
        n1 = acc[...]
        gg_ref[...] = jnp.sum(n1 * n, axis=0, keepdims=True)
        gs_ref[...] = jnp.sum(n1, axis=0, keepdims=True)
        e = n1 * gain_ref[...]
        part = rs * (
            e - jnp.mean(e, axis=-1, keepdims=True) - n * jnp.mean(e * n, axis=-1, keepdims=True)
        )
        tg_ref[...] = (mg_ref[...] + part).astype(BF16)


def input_back(me, parts, w_parts, x, mid_grad, gain):
    group, width, cols = w_parts.shape
    rows = x.shape[0]
    whole = lambda s, sc: (0, 0)
    vec = jax.ShapeDtypeStruct((1, width), F32)
    out = pl.pallas_call(
        functools.partial(input_back_kernel, group),
        grid_spec=pltpu.PrefetchScalarGridSpec(
            num_scalar_prefetch=1,
            grid=(group,),
            in_specs=[pl.BlockSpec((rows, cols), whole)] * group
            + [
                pl.BlockSpec((1, width, cols), lambda s, sc: (s, 0, 0)),
                pl.BlockSpec((rows, width), whole),
                pl.BlockSpec((rows, width), whole),
                pl.BlockSpec((1, width), whole),
            ],
            out_specs=[
                pl.BlockSpec((rows, group * cols), whole),
                pl.BlockSpec((rows, width), whole),
                pl.BlockSpec((1, width), whole),
                pl.BlockSpec((1, width), whole),
                pl.BlockSpec((1, group * cols), whole),
            ],
            scratch_shapes=[
                pltpu.VMEM((group, rows, cols), BF16),
                pltpu.VMEM((rows, width), F32),
            ],
        ),
        out_shape=[
            jax.ShapeDtypeStruct((rows, group * cols), BF16),
            jax.ShapeDtypeStruct((rows, width), BF16),
            vec,
            vec,
            jax.ShapeDtypeStruct((1, group * cols), F32),
        ],
        compiler_params=params(),
        cost_estimate=pl.CostEstimate(
            flops=2 * rows * width * cols * group,
            bytes_accessed=2 * group * cols * (width + 2 * rows) + 8 * rows * width,
            transcendentals=0,
        ),
        name="input_back",
    )(me, *parts, w_parts, x, mid_grad, gain[None])
    return out[0], out[1], out[2][0], out[3][0], out[4][0]


def partner(axis, mask):
    return [(i, i ^ mask) for i in range(lax.axis_size(axis))]


def exchange(chunks):
    return [chunks[0]] + [
        lax.ppermute(chunks[m], "seq", partner("seq", m)) for m in range(1, len(chunks))
    ]


def bits_of(size):
    return size.bit_length() - 1


def halve(block, axis, bit, dim):
    mine = (lax.axis_index(axis) >> bit) & 1
    keep = lax.dynamic_index_in_dim(block, mine, dim, keepdims=False)
    send = lax.dynamic_index_in_dim(block, 1 - mine, dim, keepdims=False)
    got = lax.ppermute(send, axis, partner(axis, 1 << bit))
    return keep.astype(F32) + got.astype(F32)


def reduce_shares(a, b, order):
    tokens, rows = a.shape
    cols = b.shape[1]
    outer, inner = lax.axis_size("dp") // 2, lax.axis_size("seq")
    share = rows // (2 * outer * inner)
    split = a.reshape(tokens, outer, 2, inner * share)
    core = lax.axis_index("dp") & 1
    send = lax.dynamic_index_in_dim(split, 1 - core, 2, keepdims=False).reshape(tokens, rows // 2)
    keep = lax.dynamic_index_in_dim(split, core, 2, keepdims=False).reshape(tokens, rows // 2)
    got = lax.ppermute(
        dot(send, b, (((0,), (0,)), ((), ()))).astype(BF16), "dp", partner("dp", 1)
    )
    total = (dot(keep, b, (((0,), (0,)), ((), ()))) + got.astype(F32)).astype(BF16)
    return halving(total, order, share, cols)


def halving(total, order, share, cols):
    outer, inner = lax.axis_size("dp") // 2, lax.axis_size("seq")
    axes = [("dp", 1 + k) for k in reversed(range(bits_of(outer)))]
    axes += [("seq", k) for k in reversed(range(bits_of(inner)))]
    total = total.reshape((2,) * len(axes) + (share, cols))
    left = list(axes)
    for pick in order(axes):
        dim = left.index(pick)
        total = halve(total, *pick, dim).astype(F32 if len(left) == 1 else BF16)
        left.remove(pick)
    return total


def dp_first(axes):
    return sorted(axes, key=lambda a: (a[0] != "dp", a[1]))


def seq_first(axes):
    low = [a for a in axes if a == ("seq", 0)]
    rest = sorted((a for a in axes if a != ("seq", 0)), key=lambda a: (a[0] != "dp", a[1]))
    return low + rest


def reduce_vectors(vectors):
    outer, inner = lax.axis_size("dp") // 2, lax.axis_size("seq")
    devices = 2 * outer * inner
    flat = jnp.concatenate([v.reshape(devices, -1) for v in vectors], axis=1)
    axes = [("dp", k) for k in reversed(range(bits_of(2 * outer)))]
    axes += [("seq", k) for k in reversed(range(bits_of(inner)))]
    total = flat.reshape((2,) * len(axes) + flat.shape[1:])
    for axis, bit in axes:
        total = halve(total, axis, bit, 0)
    out, at = [], 0
    for v in vectors:
        wide = v.shape[0] // devices
        out.append(total[at : at + wide])
        at += wide
    return out


def gelu_tanh(inputs):
    return jax.nn.gelu(inputs, approximate=True)


def token_sum(values):
    return jnp.sum(values.astype(F32), axis=0)


def layer(
    cap,
    tokens,
    first_gain,
    first_shift,
    project_weight,
    query_bias,
    value_bias,
    output_weight,
    output_bias,
    second_gain,
    second_shift,
    up_weight,
    up_bias,
    down_weight,
    down_bias,
    doc_offsets,
    active,
    upstream,
):
    group = lax.axis_size("seq")
    rows, shard, width = tokens.shape
    length = active.shape[1]
    wide = width // group
    heads = wide // HEAD_DIM
    me = lax.axis_index("seq")
    me1 = me[None].astype(jnp.int32)
    count = rows * cap

    place = jnp.arange(length, dtype=jnp.int32)
    begun = jnp.where(doc_offsets[:, :, None] <= place, doc_offsets[:, :, None], 0)
    starts = jnp.max(begun, axis=1)
    live = active.reshape(rows, group, shard)
    rank = jnp.cumsum(live.astype(jnp.int32), axis=2) - 1
    slot = jnp.arange(cap, dtype=jnp.int32)[:, None]
    chosen = (rank[:, :, None, :] == slot) & live[:, :, None, :]
    filled = jnp.any(chosen, axis=3)
    place = place.reshape(1, group, 1, shard)
    key_pos = jnp.sum(jnp.where(chosen, place, 0), axis=3)
    key_pos = jnp.where(filled, key_pos, -1).reshape(rows, group * cap)
    begin = jnp.sum(jnp.where(chosen, starts.reshape(rows, group, 1, shard), 0), axis=3)
    begin = jnp.where(filled, begin, FAR).reshape(rows, group * cap)
    tiles = group * cap // TILE
    last_key = jnp.max(key_pos.reshape(rows, tiles, TILE), axis=2)
    first_start = jnp.min(begin.reshape(rows, tiles, TILE), axis=2)
    number = jnp.arange(tiles, dtype=jnp.int32)
    needed = (last_key[:, None, :] >= first_start[:, :, None]) & (number < number[:, None])
    low = jnp.min(jnp.where(needed, number, number[:, None]), axis=2)
    scalars = jnp.concatenate([me1, low.reshape(-1)])
    kp = key_pos[:, :, None]
    spots = key_pos.reshape(rows, tiles, 1, TILE)
    begin = begin.reshape(rows, tiles, 1, TILE)
    pick = lax.dynamic_index_in_dim(chosen, me, 1, keepdims=False).astype(BF16)
    live_here = lax.dynamic_index_in_dim(live, me, 1, keepdims=False)[:, :, None]

    def pack(values):
        return (
            jnp.einsum("rct,rtd->rcd", pick, values, preferred_element_type=F32)
            .astype(BF16)
            .reshape(count, width)
        )

    def unpack(packed, values):
        spread = jnp.einsum(
            "rct,rcd->rtd", pick, packed.reshape(rows, cap, width), preferred_element_type=F32
        ).astype(BF16)
        return jnp.where(live_here, spread, values)

    x = pack(tokens)
    g = pack(upstream)

    w_parts = project_weight.reshape(width, 3, group, wide).transpose(2, 0, 1, 3)
    w_parts = w_parts.reshape(group, width, 3 * wide)
    biases = jnp.stack([query_bias, jnp.zeros_like(query_bias), value_bias])
    bias_parts = biases.reshape(3, group, wide).transpose(1, 0, 2).reshape(group, 1, 3 * wide)

    normed, chunks = qkv_chunks(me1, x, first_gain, first_shift, w_parts, bias_parts)
    head_parts = exchange(chunks)
    ctx_chunks, lse = attend(scalars, head_parts, kp, begin, spots, cap, heads)
    ctx_parts = exchange(ctx_chunks)
    context, middle, normed_two = output_project(
        me1, ctx_parts, x, output_weight, output_bias, second_gain, second_shift
    )

    raised = dot(normed_two, up_weight) + up_bias
    activated, gelu_back = jax.vjp(gelu_tanh, raised)
    hidden = activated.astype(BF16)
    hidden_grad = dot(g, down_weight, NT)
    raised_grad = gelu_back(hidden_grad)[0].astype(BF16)
    normed_two_grad = dot(raised_grad, up_weight, NT)
    middle_grad, attended_grad, grad_second_gain, grad_second_shift, grad_output_bias, grads = (
        mid_back(me1, normed_two_grad, middle, g, second_gain, output_weight, group)
    )
    grad_parts = exchange(grads)
    down_share = reduce_shares(hidden, g, dp_first)
    up_share = reduce_shares(normed_two, raised_grad, seq_first)
    lowered = dot(hidden, down_weight) + down_bias
    result = unpack((middle + lowered).astype(BF16), tokens)
    output_share = reduce_shares(context, attended_grad, dp_first)

    back_chunks = attend_back(
        scalars, head_parts, ctx_chunks, grad_parts, kp, begin, spots, lse, cap, heads
    )
    back_parts = exchange(back_chunks)
    flat_grad, token_grad, grad_first_gain, grad_first_shift, grad_biases = input_back(
        me1, back_parts, w_parts, x, middle_grad, first_gain
    )
    project_share = reduce_shares(normed, flat_grad, seq_first)
    project_share = (
        project_share.reshape(-1, group, 3, wide).transpose(0, 2, 1, 3).reshape(-1, 3 * width)
    )
    grad_biases = grad_biases.reshape(group, 3, wide).transpose(1, 0, 2).reshape(3, width)
    (
        first_gain_share,
        first_shift_share,
        query_share,
        value_share,
        output_bias_share,
        second_gain_share,
        second_shift_share,
        up_bias_share,
        down_bias_share,
    ) = reduce_vectors(
        [
            grad_first_gain,
            grad_first_shift,
            grad_biases[0],
            grad_biases[2],
            grad_output_bias,
            grad_second_gain,
            grad_second_shift,
            token_sum(raised_grad),
            token_sum(g),
        ]
    )
    return (
        result,
        unpack(token_grad, upstream),
        first_gain_share,
        first_shift_share,
        project_share,
        query_share,
        value_share,
        output_share,
        output_bias_share,
        second_gain_share,
        second_shift_share,
        up_share,
        up_bias_share,
        down_share,
        down_bias_share,
    )


def per_device(*args):
    *most, doc_offsets, exit_layers, layer_index, upstream = args
    shard = most[0].shape[1]
    active = exit_layers > layer_index[0]
    return layer(shard, *most, doc_offsets, active, upstream)


def solution(mesh):
    rows = P("dp", "seq", None)
    shares = P(("dp", "seq"))
    wide_shares = P(("dp", "seq"), None)
    in_specs = (rows,) + (P(),) * 13 + (P("dp", None), P("dp", None), P(), rows)
    out_specs = (
        rows,
        rows,
        shares,
        shares,
        wide_shares,
        shares,
        shares,
        wide_shares,
        shares,
        shares,
        shares,
        wide_shares,
        shares,
        wide_shares,
        shares,
    )
    return jax.shard_map(
        per_device, mesh=mesh, in_specs=in_specs, out_specs=out_specs, check_vma=False
    )
```

time: 1600 us -> 662 us (0.41)
  waiting for transfers between devices: 885 us -> 198 us
  matrix products: 339 us -> 83.3 us
  Pallas kernels: 0 us -> 132 us
  blocking collectives: 117 us -> 0 us
  starting transfers between devices: 16.2 us -> 109 us
  other arithmetic: 87.1 us -> 23.5 us
  loops' own time: 27.1 us -> 0 us
    reduce_scatter x4 -> x0, waiting for transfers between devices: 764 us -> none  [the longest x1 360 us: per_device(): lax.psum_scatter(grad_down_weight, ('dp', 'seq'), scatter_dimension=0, ti...]
    dot_general x68 -> x16, matrix products: 339 us -> 83.3 us  [the longest x12 76.3 us: dot(): return lax.dot_general(a, b, dims, preferred_element_type=F32)]
    ppermute x0 -> x53, waiting for transfers between devices: none -> 198 us  [the longest x21 129 us: halve(): got = lax.ppermute(send, axis, partner(axis, 1 << bit))]
    pallas_call x0 -> x6, Pallas kernels: none -> 132 us  [the longest x1 46.3 us: attend(): pl.pallas_call(functools.partial(attend_kernel, group, cap, tiles, heads)...]
    all_to_all x3 -> x0, waiting for transfers between devices: 121 us -> none  [the longest x1 69.8 us: per_device(): lax.all_to_all(packed_qkv, 'seq', split_axis=3, concat_axis=1, tiled=True)]
    ppermute x0 -> x53, starting transfers between devices: none -> 109 us  [the longest x28 65.5 us: exchange(): lax.ppermute(chunks[m], 'seq', partner('seq', m))]
    all_to_all x1 -> x0, blocking collectives: 74.6 us -> none  [per_device(): lax.all_to_all(head_qkv_grad, 'seq', split_axis=1, concat_axis=3, tiled=T...]
    unnamed x1 -> x0, blocking collectives: 42.4 us -> none
  transfers between devices with their start and end apart: 7 -> 53, of which waited for: 6 -> 20; matrix products, arithmetic and copies ran while one was open for 22% -> 24% of each run, Pallas kernels for 0% -> 2%
where the time goes in v1:
time: 662 us; the launch traced here: 655 us
  waiting for transfers between devices  198 us (30%)
  Pallas kernels  132 us (20%)
  starting transfers between devices  109 us (16%)
  local copies, waits for them, and re-layouts  107 us (16%)
  matrix products  83.3 us (13%)
  other arithmetic  23.5 us (4%)
    ppermute x21, waiting for transfers between devices, halve(): got = lax.ppermute(send, axis, partner(axis, 1 << bit))  129 us
    dot_general x12, matrix products, dot(): return lax.dot_general(a, b, dims, preferred_element_type=F32)  76.3 us
    ppermute x28, waiting for transfers between devices, exchange(): lax.ppermute(chunks[m], 'seq', partner('seq', m))  68.3 us
    ppermute x28, starting transfers between devices, exchange(): lax.ppermute(chunks[m], 'seq', partner('seq', m))  65.5 us
    unnamed x108, local copies, waits for them, and re-layouts  46.5 us
    pallas_call x1, Pallas kernels, attend(): pl.pallas_call(functools.partial(attend_kernel, group, cap, tiles, heads)...  46.3 us
    pallas_call x1, Pallas kernels, attend_back(): pl.pallas_call(functools.partial(attend_back_kernel, group, cap, tiles, h...  45.6 us
    ppermute x21, starting transfers between devices, halve(): got = lax.ppermute(send, axis, partner(axis, 1 << bit))  43.4 us
  transfers between devices with their start and end apart: 53, of which 20 were waited for; matrix products, arithmetic and copies ran while one was open for 24% of the time, Pallas kernels for 2%

profile of v1, /device:TPU:0, one launch (start us, length us, event | category | flops | bytes accessed | tf_op | source)
XLA Modules:
  0.0 655.0 jit_solution(3390667527432291306)
XLA Ops:
  3.6 8.7 %copy.153 = bf16[1024,3072]{0,1:T(8,128)(2,1)} copy(bf16[1024,3072]{1,0:T(8,128)(2,1)} %param.21) | data formatting | bytes 12582912 | tf_op args[3]
  12.3 6.5 copy.154
  18.8 8.8 %copy.155.w_ref.refs_8_ = bf16[8,1024,384]{2,1,0:T(8,128)(2,1)} copy(bf16[8,1024,384]{1,2,0:T(8,128)(2,1)} %bitcast.203) | data formatting | bytes 12582912 | tf_op jit(solution)/shard_map/reshape | solution.py:659
  30.7 11.9 %norm_project.1 = (bf16[512,1024]{1,0:T(8,128)(2,1)}, bf16[512,384]{1,0:T(8,128)(2,1)}, bf16[512,384]{1,0:T(8,128)(2,1)}, bf16[512,384]{1,0:T(8,128)(2,1)}, bf16...) custom-call(s32[1]{0:T(128)} %bitcast.6.me_ref.sc_ref, ...), custom_call_target="tpu_custom_call" | custom-call | flops 3221225472 | bytes 9437184 | tf_op jit(solution)/shard_map/norm_project/pallas_call | solution.py:63
  58.8 15.0 %collective-permute-done.1.refs_2_ = bf16[512,384]{1,0:T(8,128)(2,1)S(1)} collective-permute-done((bf16[512,384]{1,0:T(8,128)(2,1)}, bf16[512,384]{1,0:T(8,128)(2,1)S(1)}, u32[]{:S(2)}, u32[]{:S(2)}) %collective-permute-start.1) | collective-permute-done | bytes 393248 | tf_op jit(solution)/shard_map/ppermute | solution.py:507
  80.4 23.4 %collective-permute-done.4.refs_5_ = bf16[512,384]{1,0:T(8,128)(2,1)S(1)} collective-permute-done((bf16[512,384]{1,0:T(8,128)(2,1)}, bf16[512,384]{1,0:T(8,128)(2,1)S(1)}, u32[]{:S(2)}, u32[]{:S(2)}) %collective-permute-start.4) | collective-permute-done | bytes 393248 | tf_op jit(solution)/shard_map/ppermute | solution.py:507
  104.6 46.3 %attend.1 = (bf16[512,128]{1,0:T(8,128)(2,1)}, bf16[512,128]{1,0:T(8,128)(2,1)}, bf16[512,128]{1,0:T(8,128)(2,1)}, bf16[512,128]{1,0:T(8,128)(2,1)}, bf16[512,12...) custom-call(s32[17]{0:T(128)} %pad_add_fusion.sc_ref, ...), custom_call_target="tpu_custom_call" | custom-call | flops 8589934592 | bytes 4194304 | tf_op jit(solution)/shard_map/attend/pallas_call | solution.py:186
  151.2 15.4 %collective-permute-start.8 = (bf16[512,128]{1,0:T(8,128)(2,1)}, bf16[512,128]{1,0:T(8,128)(2,1)S(1)}, u32[]{:S(2)}, u32[]{:S(2)}) collective-permute-start(bf16[512,128]{1,0:T(8,128)(2,1)} %get-tuple-element.72.refs_10_), channel_id=1, source_target_pairs={{0,2},{1,3},{2,0},{3,1},{4,6},{5,7},{6,4},{7,5},{8,10},{9,11},{10,... | collective-permute-start | bytes 393224 | tf_op jit(solution)/shard_map/ppermute | solution.py:507
  176.7 10.6 %fusion.52 = f32[512,4096]{1,0:T(8,128)} fusion(bf16[512,1024]{1,0:T(8,128)(2,1)S(1)} %bitcast.208, bf16[4096,1024]{1,0:T(8,128)(2,1)} %param.30), kind=kOutput, calls=%fused_computation.150 | convolution fusion | flops 4294967296 | bytes 17825792 | tf_op jit(solution)/shard_map/dot_general | solution.py:25
  195.3 16.5 %convert_reduce_fusion = (f32[4096]{0:T(1024)}, bf16[512,4096]{1,0:T(8,128)(2,1)S(1)}, bf16[512,4096]{1,0:T(8,128)(2,1)}) fusion(f32[512,4096]{1,0:T(8,128)} %fusion.52, f32[4096]{0:T(1024)S(1)} %copy-done.43, bf16[512,1024]{1,0:T(8,128)(2,1)} %get-tuple-element.79, bf16[1024,4096]{1,0:T(8,128)(2,1)} %param.28), kind=kOutput, calls=%fused_computation.11 | convolution fusion | flops 4347392000 | bytes 26247168 | tf_op jit(solution)/shard_map/dot_general | solution.py:25
  217.6 7.3 %mid_back.1 = (f32[512,1024]{1,0:T(8,128)}, bf16[512,1024]{1,0:T(8,128)(2,1)}, f32[1,1024]{1,0:T(1,128)}, f32[1,1024]{1,0:T(1,128)}, f32[1,1024]{1,0:T(1,128)}, ...) custom-call(s32[1]{0:T(128)} %bitcast.6.me_ref.sc_ref, ...), custom_call_target="tpu_custom_call" | custom-call | flops 1073741824 | bytes 11534336 | tf_op jit(solution)/shard_map/mid_back/pallas_call | solution.py:399
  252.0 45.6 %attend_back.1 = (bf16[512,384]{1,0:T(8,128)(2,1)}, bf16[512,384]{1,0:T(8,128)(2,1)}, bf16[512,384]{1,0:T(8,128)(2,1)}, bf16[512,384]{1,0:T(8,128)(2,1)}, bf16[5...) custom-call(s32[17]{0:T(128)} %pad_add_fusion.sc_ref, ...), custom_call_target="tpu_custom_call" | custom-call | flops 21474836480 | bytes 10485760 | tf_op jit(solution)/shard_map/attend_back/pallas_call | solution.py:300
  303.1 8.9 %add_convert_fusion.4 = bf16[512,1024]{1,0:T(8,128)(2,1)} fusion(f32[512,1024]{1,0:T(8,128)S(1)} %copy-done.10, bf16[512,4096]{1,0:T(8,128)(2,1)S(1)} %copy-done.8, bf16[4096,1024]{1,0:T(8,128)(2,1)} %param.30, f32[1024]{0:T(1024)S(1)} %copy-done.44), kind=kOutput, calls=%fused_computation.37 | convolution fusion | flops 4296540160 | bytes 15732736 | tf_op jit(solution)/shard_map/dot_general | solution.py:25
  330.2 6.5 convolution_convert_fusion
  336.7 8.0 %reshape.320 = bf16[512,2,2,1024]{3,2,1,0:T(2,128)(2,1)} reshape(bf16[512,4096]{1,0:T(8,128)(2,1)} %get-tuple-element.123) | data formatting | bytes 8388608 | tf_op jit(solution)/shard_map/reshape | solution.py:528
  356.7 12.4 %collective-permute-done.24.refs_4_ = bf16[512,384]{1,0:T(8,128)(2,1)} collective-permute-done((bf16[512,384]{1,0:T(8,128)(2,1)}, bf16[512,384]{1,0:T(8,128)(2,1)}, u32[]{:S(2)}, u32[]{:S(2)}) %collective-permute-start.24) | collective-permute-done | bytes 393248 | tf_op jit(solution)/shard_map/ppermute | solution.py:507
  369.1 8.8 %collective-permute-done.25.refs_5_ = bf16[512,384]{1,0:T(8,128)(2,1)} collective-permute-done((bf16[512,384]{1,0:T(8,128)(2,1)}, bf16[512,384]{1,0:T(8,128)(2,1)}, u32[]{:S(2)}, u32[]{:S(2)}) %collective-permute-start.25) | collective-permute-done | bytes 393248 | tf_op jit(solution)/shard_map/ppermute | solution.py:507
  377.9 15.2 %input_back.1 = (bf16[512,3072]{1,0:T(8,128)(2,1)}, bf16[512,1024]{1,0:T(8,128)(2,1)}, f32[1,1024]{1,0:T(1,128)}, f32[1,1024]{1,0:T(1,128)}, f32[1,3072]{1,0:T(1,128)}) custom-call(s32[1]{0:T(128)} %bitcast.6.me_ref.sc_ref, bf16[512,384]{1,0:T(8,128)(2,1)} %get-tuple-element.89.refs_0_, bf16[512,384]{1,0:T(8,128)(2,1)} %copy-done.21, ...), custom_call_target="tpu_custom_call" | custom-call | flops 3221225472 | bytes 16777216 | tf_op jit(solution)/shard_map/input_back/pallas_call | solution.py:459
  397.9 6.2 collective-permute-start.28
  404.0 11.3 %constant_dynamic-slice_fusion.2 = (bf16[512,2,1,1024]{3,2,1,0:T(2,128)(2,1)}, bf16[512,2,1,1024]{3,2,1,0:T(2,128)(2,1)}) fusion(bf16[512,2,2,1024]{3,2,1,0:T(2,128)(2,1)} %reshape.320, s32[]{:T(128)S(6)} %select_n.186, s32[]{:T(128)S(6)} %select_n.185), kind=kLoop, calls=%fused_computation.101 | loop fusion | bytes 8388616 | tf_op jit(solution)/shard_map/jit(dynamic_index_in_dim)/dynamic_slice | solution.py:530
  415.3 10.6 %copy.191 = bf16[512,2,1,1024]{0,3,1,2:T(8,128)(2,1)} copy(bf16[512,2,1,1024]{3,2,1,0:T(2,128)(2,1)} %get-tuple-element.126) | data formatting | bytes 4194304
  426.0 6.7 %collective-permute-start.29 = (f32[2,2,2,384]{3,2,1,0:T(2,128)S(1)}, f32[2,2,2,384]{3,2,1,0:T(2,128)S(1)}, u32[]{:S(2)}, u32[]{:S(2)}) collective-permute-start(f32[2,2,2,384]{3,2,1,0:T(2,128)S(1)} %fusion.36), channel_id=1, source_target_pairs={{0,8},{8,0},{16,24},{24,16},{1,9},{9,1},{17,25},{25,17},{2,10},{10... | collective-permute-start | bytes 36872 | tf_op jit(solution)/shard_map/ppermute | solution.py:519
  438.3 14.3 %collective-permute-start.30 = (f32[2,2,384]{2,1,0:T(2,128)S(1)}, f32[2,2,384]{2,1,0:T(2,128)S(1)}, u32[]{:S(2)}, u32[]{:S(2)}) collective-permute-start(f32[2,2,384]{2,1,0:T(2,128)S(1)} %fusion.39), channel_id=1, source_target_pairs={{0,4},{1,5},{2,6},{3,7},{4,0},{5,1},{6,2},{7,3},{8,12},{9,13},{10,... | collective-permute-start | bytes 18440 | tf_op jit(solution)/shard_map/ppermute | solution.py:519
  459.7 9.1 %collective-permute-done.39 = bf16[2,2,2,32,1024]{4,3,0,1,2:T(8,128)(2,1)S(1)} collective-permute-done((bf16[2,2,2,32,1024]{4,3,0,1,2:T(8,128)(2,1)S(1)}, bf16[2,2,2,32,1024]{4,3,0,1,2:T(8,128)(2,1)S(1)}, u32[]{:S(2)}, u32[]{:S(2)}) %collective-permute-start.39) | collective-permute-done | bytes 524320 | tf_op jit(solution)/shard_map/ppermute | solution.py:519
  475.4 10.7 %copy.190 = bf16[512,2,1,1024]{0,3,1,2:T(8,128)(2,1)} copy(bf16[512,2,1,1024]{3,2,1,0:T(2,128)(2,1)} %get-tuple-element.127) | data formatting | bytes 4194304
  507.8 28.0 %collective-permute-done.34 = bf16[2,2,2,32,3072]{4,3,1,2,0:T(8,128)(2,1)S(1)} collective-permute-done((bf16[2,2,2,32,3072]{4,3,1,2,0:T(8,128)(2,1)S(1)}, bf16[2,2,2,32,3072]{4,3,1,2,0:T(8,128)(2,1)S(1)}, u32[]{:S(2)}, u32[]{:S(2)}) %collective-permute-start.34) | collective-permute-done | bytes 1572896 | tf_op jit(solution)/shard_map/ppermute | solution.py:519
  544.1 12.9 %collective-permute-done.35 = bf16[2,2,32,3072]{3,2,0,1:T(8,128)(2,1)S(1)} collective-permute-done((bf16[2,2,32,3072]{3,2,0,1:T(8,128)(2,1)S(1)}, bf16[2,2,32,3072]{3,2,0,1:T(8,128)(2,1)S(1)}, u32[]{:S(2)}, u32[]{:S(2)}) %collective-permute-start.35) | collective-permute-done | bytes 786464 | tf_op jit(solution)/shard_map/ppermute | solution.py:519
  559.2 18.6 %collective-permute-done.44 = bf16[2,2,2,32,4096]{4,3,1,2,0:T(8,128)(2,1)S(1)} collective-permute-done((bf16[2,2,2,32,4096]{4,3,1,2,0:T(8,128)(2,1)S(1)}, bf16[2,2,2,32,4096]{4,3,1,2,0:T(8,128)(2,1)S(1)}, u32[]{:S(2)}, u32[]{:S(2)}) %collective-permute-start.44) | collective-permute-done | bytes 2097184 | tf_op jit(solution)/shard_map/ppermute | solution.py:519
  579.0 22.9 %collective-permute-done.49 = bf16[2,2,2,128,1024]{4,3,0,1,2:T(8,128)(2,1)S(1)} collective-permute-done((bf16[2,2,2,128,1024]{4,3,0,1,2:T(8,128)(2,1)S(1)}, bf16[2,2,2,128,1024]{4,3,0,1,2:T(8,128)(2,1)S(1)}, u32[]{:S(2)}, u32[]{:S(2)}) %collective-permute-start.49) | collective-permute-done | bytes 2097184 | tf_op jit(solution)/shard_map/ppermute | solution.py:519
  607.4 10.2 %collective-permute-done.45 = bf16[2,2,32,4096]{3,2,0,1:T(8,128)(2,1)S(1)} collective-permute-done((bf16[2,2,32,4096]{3,2,0,1:T(8,128)(2,1)S(1)}, bf16[2,2,32,4096]{3,2,0,1:T(8,128)(2,1)S(1)}, u32[]{:S(2)}, u32[]{:S(2)}) %collective-permute-start.45) | collective-permute-done | bytes 1048608 | tf_op jit(solution)/shard_map/ppermute | solution.py:519
  625.4 9.1 %collective-permute-done.46 = bf16[2,32,4096]{2,1,0:T(8,128)(2,1)} collective-permute-done((bf16[2,32,4096]{2,1,0:T(8,128)(2,1)}, bf16[2,32,4096]{2,1,0:T(8,128)(2,1)}, u32[]{:S(2)}, u32[]{:S(2)}) %collective-permute-start.46) | collective-permute-done | bytes 524320 | tf_op jit(solution)/shard_map/ppermute | solution.py:519
  636.1 8.3 %collective-permute-done.51 = bf16[2,128,1024]{2,1,0:T(8,128)(2,1)S(1)} collective-permute-done((bf16[2,128,1024]{2,1,0:T(8,128)(2,1)S(1)}, bf16[2,128,1024]{2,1,0:T(8,128)(2,1)S(1)}, u32[]{:S(2)}, u32[]{:S(2)}) %collective-permute-start.51) | collective-permute-done | bytes 524320 | tf_op jit(solution)/shard_map/ppermute | solution.py:519
  (307 shorter events, 197.8 us)
Async XLA Ops:
  45.6 28.1 %collective-permute-start.1 = (bf16[512,384]{1,0:T(8,128)(2,1)}, bf16[512,384]{1,0:T(8,128)(2,1)S(1)}, u32[]{:S(2)}, u32[]{:S(2)}) collective-permute-start(bf16[512,384]{1,0:T(8,128)(2,1)} %get-tuple-element.64), channel_id=1, source_target_pairs={{0,2},{1,3},{2,0},{3,1},{4,6},{5,7},{6,4},{7,5},{8,10},{9,11},{10,... | collective-permute-start | bytes 1179656 | tf_op jit(solution)/shard_map/ppermute | solution.py:507
  47.2 33.2 %collective-permute-start.2 = (bf16[512,384]{1,0:T(8,128)(2,1)}, bf16[512,384]{1,0:T(8,128)(2,1)S(1)}, u32[]{:S(2)}, u32[]{:S(2)}) collective-permute-start(bf16[512,384]{1,0:T(8,128)(2,1)} %get-tuple-element.65), channel_id=1, source_target_pairs={{0,3},{1,2},{2,1},{3,0},{4,7},{5,6},{6,5},{7,4},{8,11},{9,10},{10,... | collective-permute-start | bytes 1179656 | tf_op jit(solution)/shard_map/ppermute | solution.py:507
  47.2 33.2 %collective-permute-start.3 = (bf16[512,384]{1,0:T(8,128)(2,1)}, bf16[512,384]{1,0:T(8,128)(2,1)S(1)}, u32[]{:S(2)}, u32[]{:S(2)}) collective-permute-start(bf16[512,384]{1,0:T(8,128)(2,1)} %get-tuple-element.66), channel_id=1, source_target_pairs={{0,4},{1,5},{2,6},{3,7},{4,0},{5,1},{6,2},{7,3},{8,12},{9,13},{10,... | collective-permute-start | bytes 1179656 | tf_op jit(solution)/shard_map/ppermute | solution.py:507
  50.2 53.6 %collective-permute-start.4 = (bf16[512,384]{1,0:T(8,128)(2,1)}, bf16[512,384]{1,0:T(8,128)(2,1)S(1)}, u32[]{:S(2)}, u32[]{:S(2)}) collective-permute-start(bf16[512,384]{1,0:T(8,128)(2,1)} %get-tuple-element.67), channel_id=1, source_target_pairs={{0,5},{1,4},{2,7},{3,6},{4,1},{5,0},{6,3},{7,2},{8,13},{9,12},{10,... | collective-permute-start | bytes 1179656 | tf_op jit(solution)/shard_map/ppermute | solution.py:507
  55.0 48.9 %collective-permute-start.5 = (bf16[512,384]{1,0:T(8,128)(2,1)}, bf16[512,384]{1,0:T(8,128)(2,1)}, u32[]{:S(2)}, u32[]{:S(2)}) collective-permute-start(bf16[512,384]{1,0:T(8,128)(2,1)} %get-tuple-element.68), channel_id=1, source_target_pairs={{0,6},{1,7},{2,4},{3,5},{4,2},{5,3},{6,0},{7,1},{8,14},{9,15},{10,... | collective-permute-start | bytes 1179656 | tf_op jit(solution)/shard_map/ppermute | solution.py:507
  73.8 30.1 %collective-permute-start.6 = (bf16[512,384]{1,0:T(8,128)(2,1)}, bf16[512,384]{1,0:T(8,128)(2,1)}, u32[]{:S(2)}, u32[]{:S(2)}) collective-permute-start(bf16[512,384]{1,0:T(8,128)(2,1)} %get-tuple-element.69), channel_id=1, source_target_pairs={{0,7},{1,6},{2,5},{3,4},{4,3},{5,2},{6,1},{7,0},{8,15},{9,14},{10,... | collective-permute-start | bytes 1179656 | tf_op jit(solution)/shard_map/ppermute | solution.py:507
  150.9 21.1 %collective-permute-start.7 = (bf16[512,128]{1,0:T(8,128)(2,1)}, bf16[512,128]{1,0:T(8,128)(2,1)S(1)}, u32[]{:S(2)}, u32[]{:S(2)}) collective-permute-start(bf16[512,128]{1,0:T(8,128)(2,1)} %get-tuple-element.71.refs_9_), channel_id=1, source_target_pairs={{0,1},{1,0},{2,3},{3,2},{4,5},{5,4},{6,7},{7,6},{8,9},{9,8},{10,11... | collective-permute-start | bytes 393224 | tf_op jit(solution)/shard_map/ppermute | solution.py:507
  151.2 23.3 %collective-permute-start.8 = (bf16[512,128]{1,0:T(8,128)(2,1)}, bf16[512,128]{1,0:T(8,128)(2,1)S(1)}, u32[]{:S(2)}, u32[]{:S(2)}) collective-permute-start(bf16[512,128]{1,0:T(8,128)(2,1)} %get-tuple-element.72.refs_10_), channel_id=1, source_target_pairs={{0,2},{1,3},{2,0},{3,1},{4,6},{5,7},{6,4},{7,5},{8,10},{9,11},{10,... | collective-permute-start | bytes 393224 | tf_op jit(solution)/shard_map/ppermute | solution.py:507
  167.1 20.2 %collective-permute-start.9 = (bf16[512,128]{1,0:T(8,128)(2,1)}, bf16[512,128]{1,0:T(8,128)(2,1)S(1)}, u32[]{:S(2)}, u32[]{:S(2)}) collective-permute-start(bf16[512,128]{1,0:T(8,128)(2,1)} %get-tuple-element.73.refs_11_), channel_id=1, source_target_pairs={{0,3},{1,2},{2,1},{3,0},{4,7},{5,6},{6,5},{7,4},{8,11},{9,10},{10,... | collective-permute-start | bytes 393224 | tf_op jit(solution)/shard_map/ppermute | solution.py:507
  167.8 19.5 %collective-permute-start.10 = (bf16[512,128]{1,0:T(8,128)(2,1)}, bf16[512,128]{1,0:T(8,128)(2,1)S(1)}, u32[]{:S(2)}, u32[]{:S(2)}) collective-permute-start(bf16[512,128]{1,0:T(8,128)(2,1)} %get-tuple-element.74.refs_12_), channel_id=1, source_target_pairs={{0,4},{1,5},{2,6},{3,7},{4,0},{5,1},{6,2},{7,3},{8,12},{9,13},{10,... | collective-permute-start | bytes 393224 | tf_op jit(solution)/shard_map/ppermute | solution.py:507
  297.7 28.6 %collective-permute-start.21 = (bf16[512,384]{1,0:T(8,128)(2,1)}, bf16[512,384]{1,0:T(8,128)(2,1)S(1)}, u32[]{:S(2)}, u32[]{:S(2)}) collective-permute-start(bf16[512,384]{1,0:T(8,128)(2,1)} %get-tuple-element.90), channel_id=1, source_target_pairs={{0,1},{1,0},{2,3},{3,2},{4,5},{5,4},{6,7},{7,6},{8,9},{9,8},{10,11... | collective-permute-start | bytes 1179656 | tf_op jit(solution)/shard_map/ppermute | solution.py:507
  299.1 28.7 %collective-permute-start.22 = (bf16[512,384]{1,0:T(8,128)(2,1)}, bf16[512,384]{1,0:T(8,128)(2,1)}, u32[]{:S(2)}, u32[]{:S(2)}) collective-permute-start(bf16[512,384]{1,0:T(8,128)(2,1)} %get-tuple-element.91), channel_id=1, source_target_pairs={{0,2},{1,3},{2,0},{3,1},{4,6},{5,7},{6,4},{7,5},{8,10},{9,11},{10,... | collective-permute-start | bytes 1179656 | tf_op jit(solution)/shard_map/ppermute | solution.py:507
  322.4 34.3 %collective-permute-start.23 = (bf16[512,384]{1,0:T(8,128)(2,1)}, bf16[512,384]{1,0:T(8,128)(2,1)}, u32[]{:S(2)}, u32[]{:S(2)}) collective-permute-start(bf16[512,384]{1,0:T(8,128)(2,1)} %get-tuple-element.92), channel_id=1, source_target_pairs={{0,3},{1,2},{2,1},{3,0},{4,7},{5,6},{6,5},{7,4},{8,11},{9,10},{10,... | collective-permute-start | bytes 1179656 | tf_op jit(solution)/shard_map/ppermute | solution.py:507
  322.6 46.5 %collective-permute-start.24 = (bf16[512,384]{1,0:T(8,128)(2,1)}, bf16[512,384]{1,0:T(8,128)(2,1)}, u32[]{:S(2)}, u32[]{:S(2)}) collective-permute-start(bf16[512,384]{1,0:T(8,128)(2,1)} %get-tuple-element.93), channel_id=1, source_target_pairs={{0,4},{1,5},{2,6},{3,7},{4,0},{5,1},{6,2},{7,3},{8,12},{9,13},{10,... | collective-permute-start | bytes 1179656 | tf_op jit(solution)/shard_map/ppermute | solution.py:507
  325.3 52.7 %collective-permute-start.25 = (bf16[512,384]{1,0:T(8,128)(2,1)}, bf16[512,384]{1,0:T(8,128)(2,1)}, u32[]{:S(2)}, u32[]{:S(2)}) collective-permute-start(bf16[512,384]{1,0:T(8,128)(2,1)} %get-tuple-element.94), channel_id=1, source_target_pairs={{0,5},{1,4},{2,7},{3,6},{4,1},{5,0},{6,3},{7,2},{8,13},{9,12},{10,... | collective-permute-start | bytes 1179656 | tf_op jit(solution)/shard_map/ppermute | solution.py:507
  326.3 51.6 %collective-permute-start.26 = (bf16[512,384]{1,0:T(8,128)(2,1)}, bf16[512,384]{1,0:T(8,128)(2,1)}, u32[]{:S(2)}, u32[]{:S(2)}) collective-permute-start(bf16[512,384]{1,0:T(8,128)(2,1)} %get-tuple-element.95), channel_id=1, source_target_pairs={{0,6},{1,7},{2,4},{3,5},{4,2},{5,3},{6,0},{7,1},{8,14},{9,15},{10,... | collective-permute-start | bytes 1179656 | tf_op jit(solution)/shard_map/ppermute | solution.py:507
  327.8 50.1 %collective-permute-start.27 = (bf16[512,384]{1,0:T(8,128)(2,1)}, bf16[512,384]{1,0:T(8,128)(2,1)}, u32[]{:S(2)}, u32[]{:S(2)}) collective-permute-start(bf16[512,384]{1,0:T(8,128)(2,1)} %get-tuple-element.96), channel_id=1, source_target_pairs={{0,7},{1,6},{2,5},{3,4},{4,3},{5,2},{6,1},{7,0},{8,15},{9,14},{10,... | collective-permute-start | bytes 1179656 | tf_op jit(solution)/shard_map/ppermute | solution.py:507
  356.7 95.9 %collective-permute-start.38 = (bf16[512,1024]{1,0:T(8,128)(2,1)}, bf16[512,1024]{1,0:T(8,128)(2,1)}, u32[]{:S(2)}, u32[]{:S(2)}) collective-permute-start(bf16[512,1024]{1,0:T(8,128)(2,1)} %convolution_convert_fusion.7), channel_id=1, source_target_pairs={{0,8},{8,0},{16,24},{24,16},{1,9},{9,1},{17,25},{25,17},{2,10},{10... | collective-permute-start | bytes 3145736 | tf_op jit(solution)/shard_map/ppermute | solution.py:532
  369.1 132.2 %collective-permute-start.43 = (bf16[512,4096]{1,0:T(8,128)(2,1)}, bf16[512,4096]{1,0:T(8,128)(2,1)}, u32[]{:S(2)}, u32[]{:S(2)}) collective-permute-start(bf16[512,4096]{1,0:T(8,128)(2,1)} %convolution_convert_fusion), channel_id=1, source_target_pairs={{0,8},{8,0},{16,24},{24,16},{1,9},{9,1},{17,25},{25,17},{2,10},{10... | collective-permute-start | bytes 12582920 | tf_op jit(solution)/shard_map/ppermute | solution.py:532
  397.9 28.1 %collective-permute-start.28 = (f32[2,2,2,2,384]{4,3,2,1,0:T(2,128)S(1)}, f32[2,2,2,2,384]{4,3,2,1,0:T(2,128)S(1)}, u32[]{:S(2)}, u32[]{:S(2)}) collective-permute-start(f32[2,2,2,2,384]{4,3,2,1,0:T(2,128)S(1)} %dynamic-slice_bitcast_fusion.12), channel_id=1, source_target_pairs={{0,16},{8,24},{16,0},{24,8},{1,17},{9,25},{17,1},{25,9},{2,18},{10... | collective-permute-start | bytes 73736 | tf_op jit(solution)/shard_map/ppermute | solution.py:519
  438.2 56.1 %collective-permute-start.33 = (bf16[512,3072]{1,0:T(8,128)(2,1)}, bf16[512,3072]{1,0:T(8,128)(2,1)}, u32[]{:S(2)}, u32[]{:S(2)}) collective-permute-start(bf16[512,3072]{1,0:T(8,128)(2,1)} %convolution_convert_fusion.1), channel_id=1, source_target_pairs={{0,8},{8,0},{16,24},{24,16},{1,9},{9,1},{17,25},{25,17},{2,10},{10... | collective-permute-start | bytes 9437192 | tf_op jit(solution)/shard_map/ppermute | solution.py:532
  438.3 21.2 %collective-permute-start.30 = (f32[2,2,384]{2,1,0:T(2,128)S(1)}, f32[2,2,384]{2,1,0:T(2,128)S(1)}, u32[]{:S(2)}, u32[]{:S(2)}) collective-permute-start(f32[2,2,384]{2,1,0:T(2,128)S(1)} %fusion.39), channel_id=1, source_target_pairs={{0,4},{1,5},{2,6},{3,7},{4,0},{5,1},{6,2},{7,3},{8,12},{9,13},{10,... | collective-permute-start | bytes 18440 | tf_op jit(solution)/shard_map/ppermute | solution.py:519
  459.5 77.4 %collective-permute-start.48 = (bf16[2048,1024]{1,0:T(8,128)(2,1)}, bf16[2048,1024]{1,0:T(8,128)(2,1)}, u32[]{:S(2)}, u32[]{:S(2)}) collective-permute-start(bf16[2048,1024]{1,0:T(8,128)(2,1)} %convolution_convert_fusion.2), channel_id=1, source_target_pairs={{0,8},{8,0},{16,24},{24,16},{1,9},{9,1},{17,25},{25,17},{2,10},{10... | collective-permute-start | bytes 12582920 | tf_op jit(solution)/shard_map/ppermute | solution.py:532
  459.5 26.6 %collective-permute-start.31 = (f32[2,384]{1,0:T(2,128)S(1)}, f32[2,384]{1,0:T(2,128)S(1)}, u32[]{:S(2)}, u32[]{:S(2)}) collective-permute-start(f32[2,384]{1,0:T(2,128)S(1)} %fusion.43), channel_id=1, source_target_pairs={{0,2},{1,3},{2,0},{3,1},{4,6},{5,7},{6,4},{7,5},{8,10},{9,11},{10,... | collective-permute-start | bytes 9224 | tf_op jit(solution)/shard_map/ppermute | solution.py:519
  498.4 37.4 %collective-permute-start.34 = (bf16[2,2,2,32,3072]{4,3,1,2,0:T(8,128)(2,1)S(1)}, bf16[2,2,2,32,3072]{4,3,1,2,0:T(8,128)(2,1)S(1)}, u32[]{:S(2)}, u32[]{:S(2)}) collective-permute-start(bf16[2,2,2,32,3072]{4,3,1,2,0:T(8,128)(2,1)S(1)} %bitcast.220), channel_id=1, source_target_pairs={{0,1},{1,0},{2,3},{3,2},{4,5},{5,4},{6,7},{7,6},{8,9},{9,8},{10,11... | collective-permute-start | bytes 4718600 | tf_op jit(solution)/shard_map/ppermute | solution.py:519
  506.6 71.1 %collective-permute-start.44 = (bf16[2,2,2,32,4096]{4,3,1,2,0:T(8,128)(2,1)S(1)}, bf16[2,2,2,32,4096]{4,3,1,2,0:T(8,128)(2,1)S(1)}, u32[]{:S(2)}, u32[]{:S(2)}) collective-permute-start(bf16[2,2,2,32,4096]{4,3,1,2,0:T(8,128)(2,1)S(1)} %bitcast.218), channel_id=1, source_target_pairs={{0,1},{1,0},{2,3},{3,2},{4,5},{5,4},{6,7},{7,6},{8,9},{9,8},{10,11... | collective-permute-start | bytes 6291464 | tf_op jit(solution)/shard_map/ppermute | solution.py:519
  536.5 20.5 %collective-permute-start.35 = (bf16[2,2,32,3072]{3,2,0,1:T(8,128)(2,1)S(1)}, bf16[2,2,32,3072]{3,2,0,1:T(8,128)(2,1)S(1)}, u32[]{:S(2)}, u32[]{:S(2)}) collective-permute-start(bf16[2,2,32,3072]{3,2,0,1:T(8,128)(2,1)S(1)} %dynamic-slice_bitcast_fusion.2), channel_id=1, source_target_pairs={{0,16},{8,24},{16,0},{24,8},{1,17},{9,25},{17,1},{25,9},{2,18},{10... | collective-permute-start | bytes 2359304 | tf_op jit(solution)/shard_map/ppermute | solution.py:519
  542.3 59.7 %collective-permute-start.49 = (bf16[2,2,2,128,1024]{4,3,0,1,2:T(8,128)(2,1)S(1)}, bf16[2,2,2,128,1024]{4,3,0,1,2:T(8,128)(2,1)S(1)}, u32[]{:S(2)}, u32[]{:S(2)}) collective-permute-start(bf16[2,2,2,128,1024]{4,3,0,1,2:T(8,128)(2,1)S(1)} %bitcast.219), channel_id=1, source_target_pairs={{0,16},{8,24},{16,0},{24,8},{1,17},{9,25},{17,1},{25,9},{2,18},{10... | collective-permute-start | bytes 6291464 | tf_op jit(solution)/shard_map/ppermute | solution.py:519
  557.2 47.6 %collective-permute-start.36 = (bf16[2,32,3072]{2,1,0:T(8,128)(2,1)S(1)}, bf16[2,32,3072]{2,1,0:T(8,128)(2,1)S(1)}, u32[]{:S(2)}, u32[]{:S(2)}) collective-permute-start(bf16[2,32,3072]{2,1,0:T(8,128)(2,1)S(1)} %dynamic-slice_bitcast_fusion.5), channel_id=1, source_target_pairs={{0,2},{1,3},{2,0},{3,1},{4,6},{5,7},{6,4},{7,5},{8,10},{9,11},{10,... | collective-permute-start | bytes 1179656 | tf_op jit(solution)/shard_map/ppermute | solution.py:519
  578.7 38.9 %collective-permute-start.45 = (bf16[2,2,32,4096]{3,2,0,1:T(8,128)(2,1)S(1)}, bf16[2,2,32,4096]{3,2,0,1:T(8,128)(2,1)S(1)}, u32[]{:S(2)}, u32[]{:S(2)}) collective-permute-start(bf16[2,2,32,4096]{3,2,0,1:T(8,128)(2,1)S(1)} %dynamic-slice_bitcast_fusion.1), channel_id=1, source_target_pairs={{0,16},{8,24},{16,0},{24,8},{1,17},{9,25},{17,1},{25,9},{2,18},{10... | collective-permute-start | bytes 3145736 | tf_op jit(solution)/shard_map/ppermute | solution.py:519
  604.0 18.3 %collective-permute-start.50 = (bf16[2,2,128,1024]{3,2,0,1:T(8,128)(2,1)}, bf16[2,2,128,1024]{3,2,0,1:T(8,128)(2,1)}, u32[]{:S(2)}, u32[]{:S(2)}) collective-permute-start(bf16[2,2,128,1024]{3,2,0,1:T(8,128)(2,1)} %dynamic-slice_bitcast_fusion), channel_id=1, source_target_pairs={{0,1},{1,0},{2,3},{3,2},{4,5},{5,4},{6,7},{7,6},{8,9},{9,8},{10,11... | collective-permute-start | bytes 3145736 | tf_op jit(solution)/shard_map/ppermute | solution.py:519
  624.0 20.3 %collective-permute-start.51 = (bf16[2,128,1024]{2,1,0:T(8,128)(2,1)S(1)}, bf16[2,128,1024]{2,1,0:T(8,128)(2,1)S(1)}, u32[]{:S(2)}, u32[]{:S(2)}) collective-permute-start(bf16[2,128,1024]{2,1,0:T(8,128)(2,1)S(1)} %dynamic-slice_bitcast_fusion.3), channel_id=1, source_target_pairs={{0,2},{1,3},{2,0},{3,1},{4,6},{5,7},{6,4},{7,5},{8,10},{9,11},{10,... | collective-permute-start | bytes 1572872 | tf_op jit(solution)/shard_map/ppermute | solution.py:519
  (70 other events, 1235.2 us)

commit v2 on v0

v2 whole, which is shorter than its diff:
```python
import functools
import math

import jax
import jax.numpy as jnp
from jax import lax
from jax.experimental import pallas as pl
from jax.experimental.pallas import tpu as pltpu
from jax.sharding import PartitionSpec as P

HEAD_DIM = 64
SCALE = HEAD_DIM**-0.5
TILE = 256
PAIR = 2 * TILE
NEG = -1e30
EPS = 1e-05
VMEM_LIMIT = 60 * 2**20
F32 = jnp.float32
BF16 = jnp.bfloat16

NT = (((1,), (1,)), ((), ()))
NN = (((1,), (0,)), ((), ()))
TN = (((0,), (0,)), ((), ()))


def dot(a, b, dims=NN):
    return lax.dot_general(a, b, dims, preferred_element_type=F32)


def any_spec():
    return pl.BlockSpec(memory_space=pltpu.VMEM)


def params(**kw):
    return pltpu.CompilerParams(vmem_limit_bytes=VMEM_LIMIT, **kw)


def centre_rows(x):
    centred = x - jnp.mean(x, axis=-1, keepdims=True)
    spread = jnp.mean(centred * centred, axis=-1, keepdims=True)
    rs = lax.rsqrt(spread + EPS)
    return centred * rs, rs


def smem():
    return pl.BlockSpec(memory_space=pltpu.SMEM)


def flip(index, mask):
    bit = 1
    out = index
    while bit <= mask:
        if mask & bit:
            out = out + bit * (1 - 2 * ((index // bit) % 2))
        bit *= 2
    return out


class Links:
    def __init__(self, send_sem, recv_sem):
        self.send_sem, self.recv_sem, self.used, self.sent = send_sem, recv_sem, 0, []

    def reserve(self, count):
        first, self.used = self.used, self.used + count
        return first

    def start(self, src, dst, slot, there, device):
        copy = pltpu.make_async_remote_copy(
            src_ref=src,
            dst_ref=dst,
            send_sem=self.send_sem.at[slot],
            recv_sem=self.recv_sem.at[there],
            device_id=device,
            device_id_type=pl.DeviceIdType.MESH,
        )
        copy.start()
        self.sent.append(copy)

    def arrived(self, ref, slot, device):
        pltpu.make_async_remote_copy(
            src_ref=ref,
            dst_ref=ref,
            send_sem=self.send_sem.at[slot],
            recv_sem=self.recv_sem.at[slot],
            device_id=device,
            device_id_type=pl.DeviceIdType.MESH,
        ).wait_recv()

    def drain(self):
        for copy in self.sent:
            copy.wait_send()


def greet(seq_masks, dp_masks):
    me, dp = lax.axis_index("seq"), lax.axis_index("dp")
    barrier = pltpu.get_barrier_semaphore()
    others = [{"seq": flip(me, m)} for m in seq_masks] + [{"dp": flip(dp, m)} for m in dp_masks]
    for device in others:
        pl.semaphore_signal(barrier, inc=1, device_id=device, device_id_type=pl.DeviceIdType.MESH)
    pl.semaphore_wait(barrier, len(others))


class Grid:
    def __init__(self):
        self.dp, self.seq = lax.axis_size("dp"), lax.axis_size("seq")
        self.y = self.dp // 2
        self.x = min(self.y, self.seq)
        self.z = self.seq // self.x
        self.size = {"y": self.y, "x": self.x, "z": self.z}

    def device(self, axis, r):
        me, dp = lax.axis_index("seq"), lax.axis_index("dp")
        if axis == "y":
            return {"dp": flip(dp, 2 * r)}
        return {"seq": flip(me, self.mask(axis, r))}

    def mask(self, axis, r):
        return {"y": 0, "x": r, "z": r * self.x}[axis]


def total_of(first, others, kind):
    total = first.astype(F32)
    for other in others:
        total = total + other.astype(F32)
    return total.astype(kind)


def add_into(total, others):
    for i in range(total.shape[0]):
        for j in range(total.shape[1]):
            total[i, j] = total_of(total[i, j], [other[i, j] for other in others], total.dtype)


class Summed:
    def __init__(self, links, grid, axis, block, got):
        self.links, self.grid, self.axis, self.block, self.got = links, grid, axis, block, got
        self.size = grid.size[axis]
        self.slot = links.reserve(self.size - 1)

    def send(self):
        for r in range(1, self.size):
            slot = self.slot + r - 1
            self.links.start(
                self.block.at[r], self.got.at[r - 1], slot, slot, self.grid.device(self.axis, r)
            )

    def receive(self, store, kind=BF16):
        for r in range(1, self.size):
            self.links.arrived(
                self.got.at[r - 1], self.slot + r - 1, self.grid.device(self.axis, r)
            )
        for i in range(store.shape[0]):
            store[i] = total_of(
                self.block[0, i], [self.got[r - 1, i] for r in range(1, self.size)], kind
            )

    def receive_last(self, store):
        for r in range(1, self.size):
            self.links.arrived(
                self.got.at[r - 1], self.slot + r - 1, self.grid.device(self.axis, r)
            )
        store[...] = total_of(self.block[0], [self.got[r - 1] for r in range(1, self.size)], F32)


class LineSum:
    def __init__(self, links, grid, block, right, left):
        self.links, self.grid, self.block = links, grid, block
        self.got = {1: right, -1: left}
        self.size = grid.z
        self.place = lax.axis_index("seq") // grid.x
        self.slot = {1: links.reserve(self.size), -1: links.reserve(self.size)}

    def next(self, way):
        return {"seq": lax.axis_index("seq") + way * self.grid.x}

    def copy(self, way, goal, src):
        slot = self.slot[way] + goal
        return pltpu.make_async_remote_copy(
            src_ref=src,
            dst_ref=self.got[way].at[goal],
            send_sem=self.links.send_sem.at[slot],
            recv_sem=self.links.recv_sem.at[slot],
            device_id=self.next(way),
            device_id_type=pl.DeviceIdType.MESH,
        )

    def source(self, way, goal, first):
        if first:
            return self.block.at[flip(self.place, goal)]
        return self.got[way].at[goal]

    def hop(self, k):
        for way, at in ((1, k), (-1, self.size - 1 - k)):
            goals = range(at + 1, self.size) if way == 1 else range(at - 1, -1, -1)

            @pl.when(self.place == at)
            def _(way=way, goals=goals):
                for goal in goals:
                    if k:
                        self.arrived(way, goal)
                        got = self.got[way]
                        own = self.block.at[flip(self.place, goal)]
                        for i in range(got.shape[1]):
                            got[goal, i] = total_of(own[i], [got[goal, i]], BF16)
                    self.copy(way, goal, self.source(way, goal, k == 0)).start()

    def arrived(self, way, goal):
        self.copy(way, goal, self.got[way].at[goal]).wait_recv()

    def finish(self, store, cols):
        for at in range(self.size):

            @pl.when(self.place == at)
            def _(at=at):
                ways = [way for way in (1, -1) if (at > 0 if way == 1 else at < self.size - 1)]
                for way in ways:
                    self.arrived(way, at)
                store[:, cols] = total_of(self.block[0], [self.got[w][at] for w in ways], F32)
                for way, k in ((1, at), (-1, self.size - 1 - at)):
                    goals = range(at + 1, self.size) if way == 1 else range(at - 1, -1, -1)
                    for goal in goals:
                        self.copy(way, goal, self.source(way, goal, k == 0)).wait_send()


class SlotSum:
    def __init__(self, links, grid, axis, slots, block, got, inner=False):
        self.links, self.grid, self.axis, self.got = links, grid, axis, got
        self.block = (lambda m, r: block.at[m, :, r]) if inner else (lambda m, r: block.at[m, r])
        self.size = grid.size[axis]
        self.first = links.reserve(slots * (self.size - 1))

    def id(self, m, r):
        return self.first + m * (self.size - 1) + r - 1

    def send(self, m):
        for r in range(1, self.size):
            there = m ^ self.grid.mask(self.axis, r)
            self.links.start(
                self.block(m, r),
                self.got.at[there, r - 1],
                self.id(m, r),
                self.id(there, r),
                self.grid.device(self.axis, r),
            )

    def receive(self, m):
        for r in range(1, self.size):
            self.links.arrived(
                self.got.at[m, r - 1], self.id(m, r), self.grid.device(self.axis, r)
            )
        return total_of(
            self.block(m, 0)[...], [self.got[m, r - 1] for r in range(1, self.size)], F32
        )


def split_weight(weight, group):
    width = weight.shape[0]
    wide = width // group
    if wide % 128 == 0:
        return weight
    return weight.reshape(width, 3, group, wide).transpose(1, 2, 0, 3)


def weight_view(weight, part, source, width, wide):
    if wide % 128 == 0:
        return weight.at[:, pl.ds(pl.multiple_of(part * width + source * wide, 128), wide)]
    return weight.at[part, source]


def first_kernel(wide, *refs):
    x_ref, gain_ref, shift_ref, weight, bias_ref, normed_ref, landed = refs[:7]
    w_s, stage, send_sem, recv_sem, load_sem, own_sem = refs[7:]
    group = lax.axis_size("seq")
    me = lax.axis_index("seq")
    width = x_ref.shape[1]
    links = Links(send_sem, recv_sem)
    first = links.reserve(group)
    order = list(range(group - 1, -1, -1))
    loads = {}
    for m in order:
        source = flip(me, m)
        loads[m] = []
        for part in range(3):
            loads[m].append(
                pltpu.make_async_copy(
                    weight_view(weight, part, source, width, wide),
                    w_s.at[m, part],
                    load_sem.at[3 * m + part],
                )
            )
            loads[m][-1].start()
    n, _ = centre_rows(x_ref[...].astype(F32))
    normed_ref[...] = (n * gain_ref[...] + shift_ref[...]).astype(BF16)
    greet(range(1, group), [])
    own = pltpu.make_async_copy(stage.at[0], landed.at[0], own_sem)
    for m in order:
        for copy in loads[m]:
            copy.wait()
        joined = jnp.concatenate([w_s[m, part] for part in range(3)], axis=1)
        stage[m] = (dot(normed_ref[...], joined) + bias_ref[flip(me, m)]).astype(BF16)
        if m:
            links.start(stage.at[m], landed.at[m], first + m, first + m, {"seq": flip(me, m)})
        else:
            own.start()
    for m in range(1, group):
        links.arrived(landed.at[m], first + m, {"seq": flip(me, m)})
    links.drain()
    own.wait()


def project(x, gain, shift, weight, bias_parts):
    rows, width = x.shape
    group = bias_parts.shape[0]
    wide = width // group
    cols = 3 * wide
    here = any_spec()
    anywhere = pl.BlockSpec(memory_space=pl.ANY)
    return pl.pallas_call(
        functools.partial(first_kernel, wide),
        in_specs=[here, here, here, anywhere, here],
        out_specs=[here, anywhere],
        out_shape=[
            jax.ShapeDtypeStruct((rows, width), BF16),
            jax.ShapeDtypeStruct((group, rows, cols), BF16),
        ],
        scratch_shapes=[
            pltpu.VMEM((group, 3, width, wide), BF16),
            pltpu.VMEM((group, rows, cols), BF16),
            pltpu.SemaphoreType.DMA((group,)),
            pltpu.SemaphoreType.DMA((group,)),
            pltpu.SemaphoreType.DMA((3 * group,)),
            pltpu.SemaphoreType.DMA,
        ],
        compiler_params=params(collective_id=2, has_side_effects=True),
        cost_estimate=pl.CostEstimate(
            flops=2 * rows * width * cols * group,
            bytes_accessed=2 * group * cols * (width + rows),
            transcendentals=0,
        ),
        name="norm_project",
    )(x, gain[None], shift[None], weight, bias_parts)


def only_head(block, head, heads):
    if heads == 1:
        return block
    lane = lax.broadcasted_iota(jnp.int32, block.shape, 1)
    return jnp.where(lane // HEAD_DIM == head, block, jnp.zeros_like(block))


def transposed(block):
    return block.astype(F32).T.astype(BF16)


def causal(size, offset):
    key = lax.broadcasted_iota(jnp.int32, (size, TILE), 0)
    query = lax.broadcasted_iota(jnp.int32, (size, TILE), 1)
    return key <= query + offset


def sweep(tiles, low_of, start, step, finish):
    def before(i, whole_blocks):
        low = low_of(i)
        return lax.fori_loop(
            low, whole_blocks, lambda b, c: step(i, b * PAIR, PAIR, None, c), start(i)
        )

    def even(i, half):
        finish(i, step(i, i * TILE, TILE, 0, before(i, half)))

    def odd(i, half):
        finish(i, step(i, half * PAIR, PAIR, TILE, before(i, half)))

    def both(half, _):
        even(2 * half, half)
        odd(2 * half + 1, half)
        return 0

    lax.fori_loop(0, tiles // 2, both, 0)
    if tiles % 2:
        even(tiles - 1, tiles // 2)


def span(at, size):
    return pl.ds(at if isinstance(at, int) else pl.multiple_of(at, TILE), size)


def load_heads(me, cap, parts, q_s, k_s, v_s):
    wide = v_s.shape[1]
    for m in range(parts.shape[0]):
        here = pl.ds(pl.multiple_of((me ^ m) * cap, 32), cap)
        q_s[here, :] = parts[m, :, :wide] * SCALE
        k_s[here, :wide] = parts[m, :, wide : 2 * wide]
        v_s[here, :] = parts[m, :, 2 * wide :]


def query_rows(queries, docs, heads):
    out = []
    for h in range(heads):
        mine = only_head(queries, h, heads).astype(F32)
        out.append(jnp.concatenate([mine, docs.astype(F32)], axis=1).T.astype(BF16))
    return out


def attend_kernel(group, cap, tiles, heads, sc_ref, *refs):
    parts, q_docs, k_docs, out_ref, lse_ref, q_s, k_s, v_s, vt_s, o_s = refs
    wide = heads * HEAD_DIM
    me = sc_ref[0]
    row = pl.program_id(0)
    load_heads(me, cap, parts, q_s, k_s, v_s)
    k_s[:, wide:] = k_docs[0]
    for t in range(tiles):
        vt_s[:, t * TILE : (t + 1) * TILE] = transposed(v_s[t * TILE : (t + 1) * TILE, :])

    def start(i):
        blank = (
            jnp.full((1, TILE), NEG, F32),
            jnp.zeros((1, TILE), F32),
            jnp.zeros((HEAD_DIM, TILE), F32),
        )
        at = span(i * TILE, TILE)
        return tuple(query_rows(q_s[at, :], q_docs[0, at, :], heads)), (blank,) * heads

    def step(i, at, size, diagonal, carry):
        queries, states = carry
        there = span(at, size)
        keys = k_s[there, :]
        new = []
        for h in range(heads):
            top, total, acc = states[h]
            s = dot(keys, queries[h])
            if diagonal is not None:
                s = jnp.where(causal(size, diagonal), s, NEG)
            top2 = jnp.maximum(top, jnp.max(s, axis=0, keepdims=True))
            p = jnp.exp(s - top2)
            fade = jnp.exp(top - top2)
            total = total * fade + jnp.sum(p, axis=0, keepdims=True)
            vt = vt_s[h * HEAD_DIM : (h + 1) * HEAD_DIM, there]
            acc = acc * fade + dot(vt, p.astype(BF16))
            new.append((top2, total, acc))
        return queries, tuple(new)

    def finish(i, carry):
        pieces = []
        for h in range(heads):
            top, total, acc = carry[1][h]
            pieces.append(acc * (1.0 / total))
            lse_ref[0, i, h : h + 1, :] = top + jnp.log(total)
        o_s[span(i * TILE, TILE), :] = jnp.concatenate(pieces, axis=0).T.astype(BF16)

    sweep(tiles, lambda i: sc_ref[1 + row * tiles + i], start, step, finish)
    for m in range(group):
        out_ref[m] = o_s[pl.ds(pl.multiple_of((me ^ m) * cap, 32), cap), :]


def attend(scalars, parts, q_docs, k_docs, cap, heads):
    group, tokens, cols = parts.shape
    rows = tokens // cap
    length = group * cap
    tiles = length // TILE
    wide = heads * HEAD_DIM
    deep = wide + q_docs.shape[2]
    pair = rows * heads * length * length // 2
    by_row = lambda r, sc: (0, r, 0)
    all_row = lambda r, sc: (r, 0, 0)
    return pl.pallas_call(
        functools.partial(attend_kernel, group, cap, tiles, heads),
        grid_spec=pltpu.PrefetchScalarGridSpec(
            num_scalar_prefetch=1,
            grid=(rows,),
            in_specs=[pl.BlockSpec((group, cap, cols), by_row)]
            + [pl.BlockSpec((1,) + q_docs.shape[1:], all_row)] * 2,
            out_specs=[
                pl.BlockSpec((group, cap, wide), by_row),
                pl.BlockSpec((1, tiles, heads, TILE), lambda r, sc: (r, 0, 0, 0)),
            ],
            scratch_shapes=[
                pltpu.VMEM((length, wide), BF16),
                pltpu.VMEM((length, deep), BF16),
                pltpu.VMEM((length, wide), BF16),
                pltpu.VMEM((wide, length), BF16),
                pltpu.VMEM((length, wide), BF16),
            ],
        ),
        out_shape=[
            jax.ShapeDtypeStruct((group, rows * cap, wide), BF16),
            jax.ShapeDtypeStruct((rows, tiles, heads, TILE), F32),
        ],
        compiler_params=params(),
        cost_estimate=pl.CostEstimate(
            flops=4 * 256 * pair, bytes_accessed=8 * rows * length * wide, transcendentals=pair
        ),
        name="attend",
    )(scalars, parts, q_docs, k_docs)


def attend_back_kernel(group, cap, tiles, heads, sc_ref, *refs):
    parts, ctx, grads, q_docs, k_docs, lse_ref, out_ref = refs[:7]
    refs = refs[7:]
    q_s, k_s, v_s, kt_s, g_s, o_s, dq_s, dk_s, dv_s = refs
    wide = heads * HEAD_DIM
    me = sc_ref[0]
    row = pl.program_id(0)
    load_heads(me, cap, parts, q_s, k_s, v_s)
    k_s[:, wide:] = k_docs[0]
    for m in range(group):
        here = pl.ds(pl.multiple_of((me ^ m) * cap, 32), cap)
        g_s[here, :] = grads[m]
        o_s[here, :] = ctx[m]
    for t in range(tiles):
        kt_s[:, t * TILE : (t + 1) * TILE] = transposed(k_s[t * TILE : (t + 1) * TILE, :wide])
    dk_s[...] = jnp.zeros_like(dk_s)
    dv_s[...] = jnp.zeros_like(dv_s)

    def start(i):
        at = span(i * TILE, TILE)
        queries = q_s[at, :]
        grad = g_s[at, :]
        product = (grad.astype(F32) * o_s[at, :].astype(F32)).T
        delta = tuple(
            jnp.sum(product[h * HEAD_DIM : (h + 1) * HEAD_DIM], axis=0, keepdims=True)
            for h in range(heads)
        )
        split_q = tuple(only_head(queries, h, heads) for h in range(heads))
        split_g = tuple(only_head(grad, h, heads) for h in range(heads))
        turned_q = tuple(query_rows(queries, q_docs[0, at, :], heads))
        turned_g = tuple(transposed(part) for part in split_g)
        fixed = (split_q, split_g, turned_q, turned_g, delta)
        return fixed, tuple(jnp.zeros((HEAD_DIM, TILE), F32) for _ in range(heads))

    def step(i, at, size, diagonal, carry):
        fixed, sums = carry
        split_q, split_g, turned_q, turned_g, delta = fixed
        there = span(at, size)
        keys = k_s[there, :]
        values = v_s[there, :]
        new, ps, dss = [], [], []
        for h in range(heads):
            s = dot(keys, turned_q[h]) - lse_ref[0, i, h : h + 1, :]
            if diagonal is not None:
                s = jnp.where(causal(size, diagonal), s, NEG)
            p = jnp.exp(s)
            dp = dot(values, turned_g[h])
            ds = (p * (dp - delta[h])).astype(BF16)
            ps.append(p.astype(BF16))
            dss.append(ds)
            kt = kt_s[h * HEAD_DIM : (h + 1) * HEAD_DIM, there]
            new.append(sums[h] + dot(kt, ds))
        dv = dot(ps[0], split_g[0])
        dk = dot(dss[0], split_q[0])
        for h in range(1, heads):
            dv = dv + dot(ps[h], split_g[h])
            dk = dk + dot(dss[h], split_q[h])
        dv_s[there, :] += dv
        dk_s[there, :] += dk
        return fixed, tuple(new)

    def finish(i, carry):
        dq_s[span(i * TILE, TILE), :] = (jnp.concatenate(carry[1], axis=0).T * SCALE).astype(BF16)

    sweep(tiles, lambda i: sc_ref[1 + row * tiles + i], start, step, finish)
    for m in range(group):
        here = pl.ds(pl.multiple_of((me ^ m) * cap, 32), cap)
        out_ref[m, :, :wide] = dq_s[here, :]
        out_ref[m, :, wide : 2 * wide] = dk_s[here, :].astype(BF16)
        out_ref[m, :, 2 * wide :] = dv_s[here, :].astype(BF16)


def attend_back(scalars, parts, ctx, grads, q_docs, k_docs, lse, cap, heads):
    group, tokens, cols = parts.shape
    rows = tokens // cap
    length = group * cap
    tiles = length // TILE
    wide = heads * HEAD_DIM
    deep = wide + q_docs.shape[2]
    pair = rows * heads * length * length // 2
    by_row = lambda r, sc: (0, r, 0)
    all_row = lambda r, sc: (r, 0, 0)
    return pl.pallas_call(
        functools.partial(attend_back_kernel, group, cap, tiles, heads),
        grid_spec=pltpu.PrefetchScalarGridSpec(
            num_scalar_prefetch=1,
            grid=(rows,),
            in_specs=[pl.BlockSpec((group, cap, cols), by_row)]
            + [pl.BlockSpec((group, cap, wide), by_row)] * 2
            + [pl.BlockSpec((1,) + q_docs.shape[1:], all_row)] * 2
            + [pl.BlockSpec((1, tiles, heads, TILE), lambda r, sc: (r, 0, 0, 0))],
            out_specs=pl.BlockSpec((group, cap, cols), by_row),
            scratch_shapes=[
                pltpu.VMEM((length, wide), BF16),
                pltpu.VMEM((length, deep), BF16),
                pltpu.VMEM((length, wide), BF16),
                pltpu.VMEM((wide, length), BF16),
            ]
            + [pltpu.VMEM((length, wide), BF16)] * 3
            + [pltpu.VMEM((length, wide), F32)] * 2,
        ),
        out_shape=jax.ShapeDtypeStruct((group, rows * cap, cols), BF16),
        compiler_params=params(),
        cost_estimate=pl.CostEstimate(
            flops=10 * 256 * pair, bytes_accessed=20 * rows * length * wide, transcendentals=pair
        ),
        name="attend_back",
    )(scalars, parts, ctx, grads, q_docs, k_docs, lse)


def norm_back(upper, n, rs, gain):
    e = upper * gain
    return rs * (
        e - jnp.mean(e, axis=-1, keepdims=True) - n * jnp.mean(e * n, axis=-1, keepdims=True)
    )


GELU_A = 0.7978845608028654
GELU_B = 0.044715


VECTORS = 10


def mid_kernel(wide, *refs):
    grid = Grid()
    group, ys, xs, zs = grid.seq, grid.y, grid.x, grid.z
    refs = list(refs)

    def take(n):
        out = refs[:n]
        del refs[:n]
        return out

    ctx_hbm, x_ref, g_ref, ow_hbm, uw_hbm, dw_hbm, ob, gain, shift, ub, db = take(11)
    grads, result_ref, mg_ref, early = take(4)
    down_out, up_out, out_out = take(2 * ys), take(xs + ys), take(zs)
    gots = take(3)
    landed, ctx, ow, uw, dw, hid, rise, mid_s, n2_s, normed, attn, chunk = take(12)
    flat_ring, tall_ring, flat_got, tall_got = take(4)
    send_sem, recv_sem, load_sem, ring_sem, got_sem = take(5)

    me, dp = lax.axis_index("seq"), lax.axis_index("dp")
    core, row = dp % 2, dp // 2
    links = Links(send_sem, recv_sem)
    tokens, width = x_ref.shape
    hidden = hid.shape[1]
    block = min(512, hidden)
    partner_core = {"dp": flip(dp, 1)}
    loads = [
        pltpu.make_async_copy(src, dst, load_sem.at[k])
        for k, (src, dst) in enumerate(
            ((dw_hbm, dw), (ow_hbm, ow), (uw_hbm, uw), (ctx_hbm.at[0], landed.at[0]))
        )
    ]
    for copy in loads:
        copy.start()
    greet(range(1, group), [1])
    first = links.reserve(group)
    for m in range(group - 1, 0, -1):
        links.start(ctx_hbm.at[m], landed.at[m], first + m, first + m, {"seq": flip(me, m)})

    early[...] = jnp.zeros_like(early)
    early[5:6, :] = jnp.sum(g_ref[...].astype(F32), axis=0, keepdims=True)
    loads[0].wait()

    def lanes(f, size):
        return pl.ds(pl.multiple_of(f * size, size), size)

    def before(f, _):
        here = lanes(f, block)
        rise[:, here] = dot(g_ref[...], dw[here, :], NT).astype(BF16)
        return 0

    lax.fori_loop(0, hidden // block, before, 0)
    for copy in loads[1:]:
        copy.wait()
    for m in range(1, group):
        links.arrived(landed.at[m], first + m, {"seq": flip(me, m)})
    for s in range(group):
        chunk[s] = landed[flip(me, s)]
    for s in range(group):
        ctx[:, s * wide : (s + 1) * wide] = chunk[s]
    mid = x_ref[...].astype(F32) + dot(ctx[...], ow[...]) + ob[...]
    mid_s[...] = mid
    n, _ = centre_rows(mid)
    normed[...] = (n * gain[...] + shift[...]).astype(BF16)
    n2_s[...] = jnp.zeros_like(n2_s)

    def through(f, _):
        here = lanes(f, block)
        u = dot(normed[...], uw[:, here]) + ub[:, here]
        square = u * u
        t = jnp.tanh(GELU_A * u * (1.0 + GELU_B * square))
        half = 0.5 * (1.0 + t)
        hid[:, here] = (u * half).astype(BF16)
        slope = half + 0.5 * GELU_A * u * (1.0 - t * t) * (1.0 + 3.0 * GELU_B * square)
        up = (rise[:, here].astype(F32) * slope).astype(BF16)
        rise[:, here] = up
        n2_s[...] += dot(up, uw[:, here], NT)
        return 0

    lax.fori_loop(0, hidden // block, through, 0)
    n, rs = centre_rows(mid_s[...])
    n2 = n2_s[...]
    early[3:4, :] = jnp.sum(n2 * n, axis=0, keepdims=True)
    early[4:5, :] = jnp.sum(n2, axis=0, keepdims=True)
    mid_grad = g_ref[...].astype(F32) + norm_back(n2, n, rs, gain[...])
    mg_ref[...] = mid_grad
    attn[...] = mid_grad.astype(BF16)
    full = dot(attn[...], ow[...], NT).astype(BF16)
    for s in range(group):
        chunk[flip(me, s)] = full[:, s * wide : (s + 1) * wide]
    second = links.reserve(group)
    for m in range(group - 1, 0, -1):
        links.start(chunk.at[m], grads.at[m], second + m, second + m, {"seq": flip(me, m)})
    own = pltpu.make_async_copy(chunk.at[0], grads.at[0], load_sem.at[0])
    own.start()

    rings = {"flat": flat_ring, "tall": tall_ring}
    loaded = {"flat": flat_got, "tall": tall_got}
    busy = {"flat": [None] * flat_ring.shape[0], "tall": [None] * tall_ring.shape[0]}
    places = {"flat": 0, "tall": flat_ring.shape[0]}
    made = {"flat": 0, "tall": 0}
    arriving = {}

    def ordered(ring, spot, total, parts, share, got):
        for s in range(parts):
            rel = flip(me % parts, s)
            piece = total[s * share : (s + 1) * share]
            if got is not None:
                piece = piece + got[rel % xs, rel // xs].astype(F32)
            ring[spot, rel % xs, rel // xs] = piece.astype(BF16)

    def outputs(item, o, z, cols, ring):
        if item == 0:
            half = down_out[0].shape[-1]
            for h in range(2):
                yield ring.at[:, :, :, h * half : (h + 1) * half], down_out[2 * o + h].at[:, z]
        elif item == 1:
            half = up_out[0].shape[-1]
            h, at = cols.start // half, cols.start % half
            here = slice(at, at + cols.stop - cols.start)
            if h:
                yield ring, up_out[xs + o].at[:, :, :, here]
            else:
                for x in range(xs):
                    yield ring.at[x], up_out[x].at[o, :, :, here]
        else:
            for z in range(zs):
                yield ring.at[:, z], out_out[z].at[o]

    def weight_grad(kind, item, a, b):
        share = a.shape[1] // (2 * ys * group)
        parts = min(group, max(256 // share, xs))
        sub = group // parts
        depth = parts // xs
        cols = b.shape[1]
        piece = min(1024, cols)
        ring, got = rings[kind], loaded[kind]
        units = [(o, k, p) for o in reversed(range(ys)) for k in range(sub) for p in range(0, cols, piece)]

        def rows_of(c, o, k):
            at = (flip(row, o) * 2 + flip(core, c)) * group * share
            at = at + flip(me // parts, k) * parts * share
            return transposed(a[:, pl.ds(pl.multiple_of(at, 128), parts * share)])

        def place(o, k, p):
            return (o, slice(None), slice(k * depth, (k + 1) * depth), slice(None), slice(p, p + piece))

        def spot_of():
            spot = made[kind] % ring.shape[0]
            made[kind] += 1
            for wait in busy[kind][spot] or ():
                wait()
            return spot

        for n, (o, k, p) in enumerate(units):
            if p == 0:
                left = rows_of(1, o, k)
            total = dot(left, b[:, p : p + piece])
            spot = spot_of()
            ordered(ring, spot, total, parts, share, None)
            slot = links.reserve(1)
            copy = pltpu.make_async_remote_copy(
                src_ref=ring.at[spot],
                dst_ref=gots[item].at[place(o, k, p)],
                send_sem=send_sem.at[slot],
                recv_sem=recv_sem.at[slot],
                device_id=partner_core,
                device_id_type=pl.DeviceIdType.MESH,
            )
            copy.start()
            busy[kind][spot] = [copy.wait_send]
            arriving[n] = slot

        def fetch(n):
            src = gots[item].at[place(*units[n])]
            links.arrived(src, arriving[n], partner_core)
            copy = pltpu.make_async_copy(src, got.at[n % 2], got_sem.at[2 * item + n % 2])
            copy.start()
            return copy

        coming = fetch(0)
        for n, (o, k, p) in enumerate(units):
            if p == 0:
                left = rows_of(0, o, k)
            total = dot(left, b[:, p : p + piece])
            coming.wait()
            if n + 1 < len(units):
                coming = fetch(n + 1)
            spot = spot_of()
            ordered(ring, spot, total, parts, share, got.at[n % 2])
            busy[kind][spot] = []
            z = slice(k * depth, (k + 1) * depth)
            for h, (src, dst) in enumerate(outputs(item, o, z, slice(p, p + piece), ring.at[spot])):
                sem = ring_sem.at[(places[kind] + spot) * max(2, xs, zs) + h]
                copy = pltpu.make_async_copy(src, dst, sem)
                copy.start()
                busy[kind][spot].append(copy.wait)

    weight_grad("tall", 0, hid, g_ref)
    weight_grad("flat", 1, normed, rise)
    weight_grad("flat", 2, ctx, attn)
    result_ref[...] = (mid_s[...] + (dot(hid[...], dw[...]) + db[...])).astype(BF16)
    early[2:3, :] = jnp.sum(attn[...].astype(F32), axis=0, keepdims=True)
    for k in range(hidden // width):
        part = rise[:, k * width : (k + 1) * width].astype(F32)
        early[6 + k : 7 + k, :] = jnp.sum(part, axis=0, keepdims=True)
    for m in range(1, group):
        links.arrived(grads.at[m], second + m, {"seq": flip(me, m)})
    for spots in busy.values():
        for waits in spots:
            for wait in waits or ():
                wait()
    own.wait()
    links.drain()


def feed_forward(ctx, x, g, ow, ob, gain, shift, uw, ub, dw, db):
    grid = Grid()
    group, ys, xs, zs = grid.seq, grid.y, grid.x, grid.z
    rows, width = x.shape
    wide = width // group
    hidden = uw.shape[1]
    here = any_spec()
    anywhere = pl.BlockSpec(memory_space=pl.ANY)
    shape = jax.ShapeDtypeStruct
    low, high = width // (grid.dp * group), hidden // (grid.dp * group)
    vectors = VECTORS + group
    vectors += -vectors % 8
    sums = [
        shape((ys, xs, zs, high, width), BF16),
        shape((ys, xs, zs, low, hidden), BF16),
        shape((ys, xs, zs, low, width), BF16),
    ]
    parts = lambda share: min(group, max(256 // share, xs))
    ring = lambda share, n: pltpu.VMEM((n, xs, parts(share) // xs, share, width), BF16)
    blocks = ys * (group // parts(high)) + ys * (hidden // width) + ys
    vmem = lambda dims, kind=BF16: pltpu.VMEM(dims, kind)
    return pl.pallas_call(
        functools.partial(mid_kernel, wide),
        in_specs=[anywhere, here, here, anywhere, anywhere, anywhere] + [here] * 5,
        out_specs=[anywhere, here, here, here] + [anywhere] * (3 * ys + xs + zs + 3),
        out_shape=[
            shape((group, rows, wide), BF16),
            shape((rows, width), BF16),
            shape((rows, width), F32),
            shape((vectors, width), F32),
        ]
        + [shape((xs, zs, high, width // 2), BF16)] * (2 * ys)
        + [shape((ys, zs, low, hidden // 2), BF16)] * xs
        + [shape((xs, zs, low, hidden // 2), BF16)] * ys
        + [shape((ys, xs, low, width), BF16)] * zs
        + sums,
        scratch_shapes=[
            vmem((group, rows, wide)),
            vmem((rows, width)),
            vmem((width, width)),
            vmem((width, hidden)),
            vmem((hidden, width)),
            vmem((rows, hidden)),
            vmem((rows, hidden)),
            vmem((rows, width), F32),
            vmem((rows, width), F32),
            vmem((rows, width)),
            vmem((rows, width)),
            vmem((group, rows, wide)),
            ring(low, 4),
            ring(high, 4),
            ring(low, 2),
            ring(high, 2),
            pltpu.SemaphoreType.DMA((2 * group + blocks,)),
            pltpu.SemaphoreType.DMA((2 * group + blocks,)),
            pltpu.SemaphoreType.DMA((4,)),
            pltpu.SemaphoreType.DMA((8 * max(2, xs, zs),)),
            pltpu.SemaphoreType.DMA((6,)),
        ],
        compiler_params=params(collective_id=3, has_side_effects=True),
        cost_estimate=pl.CostEstimate(
            flops=8 * rows * width * width + 12 * rows * width * hidden,
            bytes_accessed=4 * width * width + 8 * width * hidden,
            transcendentals=rows * hidden,
        ),
        name="feed_forward",
    )(ctx, x, g, ow, uw, dw, ob[None], gain[None], shift[None], ub[None], db[None])


def partner(axis, mask):
    return [(i, i ^ mask) for i in range(lax.axis_size(axis))]


def exchange(axis, blocks):
    grid = Grid()
    out = [blocks[0]]
    for r in range(1, grid.size[axis]):
        name, mask = ("dp", 2 * r) if axis == "y" else ("seq", grid.mask(axis, r))
        out.append(lax.ppermute(blocks[r], name, partner(name, mask)))
    return out


def item_counts(ys, xs, zs):
    return (ys - 1) + 5, (xs - 1) + 5, 7, 7, (zs - 1) + 4


def tail_kernel(wide, *refs):
    grid = Grid()
    group, ys, xs, zs = grid.seq, grid.y, grid.x, grid.z
    refs = list(refs)

    def take(n):
        out = refs[:n]
        del refs[:n]
        return out

    back, weight, normed_ref, x_hbm, mg_hbm, gain_ref, early_ref = take(7)
    down_in, down_rest = take(ys), take(ys)
    up_in, up_rest = take(xs), take(ys)
    out_in = take(zs)
    tg_ref, project_ref, down_ref, up_ref, out_ref, vec_ref = take(6)
    landed, w_s, x_s, mg_s, acc, turned, order = take(7)
    send_a, send_b, keep_a, keep_b, pair_a, pair_b = take(6)
    got_a1, got_b1, mid_a, mid_b, got_a2, got_b2, z_a, z_b, got_za, got_zb = take(10)
    items = [take(count) for count in item_counts(ys, xs, zs)]
    vec_s, vec_g = take(2)
    send_sem, recv_sem, load_sem = take(3)

    me, dp = lax.axis_index("seq"), lax.axis_index("dp")
    core, row = dp % 2, dp // 2
    links = Links(send_sem, recv_sem)
    tokens, width = normed_ref.shape
    share = project_ref.shape[1]
    partner_core = {"dp": flip(dp, 1)}
    loads = []

    def load(src, dst):
        copy = pltpu.make_async_copy(src, dst, load_sem.at[len(loads)])
        copy.start()
        loads.append(copy)
        return copy

    greet(range(1, group), [1] + [2 * r for r in range(1, ys)])

    first = links.reserve(group)
    for m in range(1, group):
        links.start(back.at[m], landed.at[m], first + m, first + m, {"seq": flip(me, m)})
    own = load(back.at[0], landed.at[0])
    down_a, up_a, down_b, up_b, out_a = items
    loaded = [
        [load(src, dst) for src, dst in zip(up_in, [up_a[xs - 1]] + up_a[: xs - 1])],
        [load(src, dst) for src, dst in zip(down_in, [down_a[ys - 1]] + down_a[: ys - 1])],
        [load(src, dst) for src, dst in zip(out_in, [out_a[zs - 1]] + out_a[: zs - 1])],
        [load(src, down_b[0].at[o]) for o, src in enumerate(down_rest)],
        [load(src, up_b[0].at[o]) for o, src in enumerate(up_rest)],
    ]

    def load_weight(m):
        source = flip(me, m)
        out = []
        for part in range(3):
            src = weight_view(weight, part, source, width, wide)
            out.append(load(src, w_s.at[m % ahead, part]))
        return out

    ahead = w_s.shape[0]
    own_w = [load_weight(m) for m in range(ahead)]
    own_x = load(x_hbm, x_s)
    own_mg = load(mg_hbm, mg_s)

    def summed(axis, block, got):
        return Summed(links, grid, axis, block, got)

    up_a1 = summed("y", up_a[xs - 1], up_a[xs])
    up_a2 = LineSum(links, grid, *up_a[xs + 1 :])
    down_a1 = summed("x", down_a[ys - 1], down_a[ys])
    down_a2 = LineSum(links, grid, *down_a[ys + 1 :])
    down_b1, down_b2 = summed("y", down_b[0], down_b[1]), summed("x", down_b[2], down_b[3])
    down_b3 = LineSum(links, grid, *down_b[4:])
    up_b1, up_b2 = summed("y", up_b[0], up_b[1]), summed("x", up_b[2], up_b[3])
    up_b3 = LineSum(links, grid, *up_b[4:])
    out_1 = summed("y", out_a[zs - 1], out_a[zs])
    out_2 = summed("x", out_a[zs + 1], out_a[zs + 2])
    lines = (up_a2, down_a2, up_b3, down_b3)
    for copies in loaded[3:]:
        for copy in copies:
            copy.wait()
    down_b1.send()
    up_b1.send()
    for copies, item, count, stage in (
        (loaded[0], up_a, xs, up_a1),
        (loaded[1], down_a, ys, down_a1),
        (loaded[2], out_a, zs, out_1),
    ):
        for copy in copies:
            copy.wait()
        add_into(item[count - 1], item[: count - 1])
        stage.send()

    for k in range(0, width, 256):
        turned[k : k + 256, :] = normed_ref[:, k : k + 256].astype(F32).T
    for c in range(2):
        for o in range(ys):
            for x in range(xs):
                for z in range(zs):
                    there = (flip(row, o) * 2 + flip(core, c)) * group + flip(me, z * xs + x)
                    rows = turned[pl.ds(pl.multiple_of(there * share, share), share), :]
                    order[c, o, x, z] = rows.astype(BF16)
    half = ys * group * share
    acc[...] = jnp.zeros_like(acc)
    vec_s[0] = early_ref[...]
    own.wait()

    pair_first = links.reserve(2 * group)
    a1 = SlotSum(links, grid, "y", group, keep_a, got_a1)
    a2 = SlotSum(links, grid, "x", group, mid_a, got_a2)
    b1 = SlotSum(links, grid, "x", group, keep_b, got_b1, inner=True)
    b2 = SlotSum(links, grid, "y", group, mid_b, got_b2)
    cut = 2 * wide

    def multiply(m):
        if m:
            links.arrived(landed.at[m], first + m, {"seq": flip(me, m)})
        source = flip(me, m)
        for k, (send, keep, pair, cols) in enumerate(
            (
                (send_a, keep_a, pair_a, slice(0, cut)),
                (send_b, keep_b, pair_b, slice(cut, 3 * wide)),
            )
        ):
            grad = landed[m, :, cols]
            left = order[1].reshape(half, tokens)
            send[m] = dot(left, grad).reshape(send.shape[1:]).astype(BF16)
            slot = pair_first + 2 * m + k
            links.start(send.at[m], pair.at[m], slot, slot, partner_core)
            left = order[0].reshape(half, tokens)
            keep[m] = dot(left, grad).reshape(keep.shape[1:]).astype(BF16)
        block = landed[m]
        for copy in own_w[m]:
            copy.wait()
        pieces = [w_s[m % ahead, part] for part in range(3)]
        acc[...] += dot(block, jnp.concatenate(pieces, axis=1), NT)
        if m + ahead < group:
            own_w.append(load_weight(m + ahead))
        sums = jnp.sum(block.astype(F32), axis=0, keepdims=True)
        vec_s[0, pl.ds(VECTORS + source, 1), : 3 * wide] = sums

    def paired(m):
        for k, (keep, pair, nxt) in enumerate(((keep_a, pair_a, a1), (keep_b, pair_b, b1))):
            links.arrived(pair.at[m], pair_first + 2 * m + k, partner_core)
            keep[m] = total_of(keep[m], [pair[m]], BF16)
            nxt.send(m)

    def second(m):
        mid_a[m] = a1.receive(m).astype(BF16)
        a2.send(m)
        mid_b[m] = b1.receive(m).astype(BF16)
        b2.send(m)

    def third(m):
        total = a2.receive(m).astype(BF16)
        for z in range(zs):
            z_a[z, m] = total[z]
        total = b2.receive(m).astype(BF16)
        for z in range(zs):
            z_b[z, m] = total[z]

    def input_grads():
        own_x.wait()
        own_mg.wait()
        n, rs = centre_rows(x_s[...].astype(F32))
        n1 = acc[...]
        tg_ref[...] = (mg_s[...] + norm_back(n1, n, rs, gain_ref[...])).astype(BF16)
        vec_s[0, 0:1, :] = jnp.sum(n1 * n, axis=0, keepdims=True)
        vec_s[0, 1:2, :] = jnp.sum(n1, axis=0, keepdims=True)

    vec_first = links.reserve(1 + (ys - 1) + (xs - 1) + (zs - 1))
    hops = [[partner_core]]
    for axis in ("y", "x", "z"):
        hops.append([grid.device(axis, r) for r in range(1, grid.size[axis])])

    def vec_send(k):
        at = vec_first + sum(len(h) for h in hops[:k])
        for r, device in enumerate(hops[k]):
            links.start(vec_s.at[k], vec_g.at[at + r - vec_first], at + r, at + r, device)

    def vec_receive(k):
        at = vec_first + sum(len(h) for h in hops[:k])
        got = []
        for r, device in enumerate(hops[k]):
            links.arrived(vec_g.at[at + r - vec_first], at + r, device)
            got.append(vec_g[at + r - vec_first])
        total = total_of(vec_s[k], got, F32)
        if k + 1 < len(hops):
            vec_s[k + 1] = total
            vec_send(k + 1)
        else:
            vec_ref[...] = total

    for m in range(group):
        multiply(m)
        if m:
            paired(m - 1)
        if m == group // 2:
            down_b1.receive(down_b[2])
            down_b2.send()
    paired(group - 1)
    down_a1.receive(down_a[ys + 1])
    down_a2.hop(0)
    up_b1.receive(up_b[2])
    up_b2.send()
    up_a1.receive(up_a[xs + 1])
    up_a2.hop(0)
    input_grads()
    vec_send(0)
    out_1.receive(out_a[zs + 1])
    out_2.send()
    down_b2.receive(down_b[4])
    down_b3.hop(0)
    for k in range(1, zs - 1):
        down_a2.hop(k)
        up_a2.hop(k)
    vec_receive(0)
    for m in range(group):
        second(m)
        if m == group // 2:
            for k in range(1, zs - 1):
                down_b3.hop(k)
    vec_receive(1)
    up_b2.receive(up_b[4])
    up_b3.hop(0)
    for m in range(group):
        third(m)
        if m == group // 2:
            for k in range(1, zs - 1):
                up_b3.hop(k)

    z_first = links.reserve(2 * (zs - 1))
    for r in range(1, zs):
        for k, (block, got) in enumerate(((z_a, got_za), (z_b, got_zb))):
            slot = z_first + 2 * (r - 1) + k
            links.start(block.at[r], got.at[r - 1], slot, slot, grid.device("z", r))
    vec_receive(2)
    half = down_ref.shape[1] // 2
    out_2.receive_last(out_ref)
    up_a2.finish(up_ref, slice(0, up_ref.shape[1] // 2))
    down_a2.finish(down_ref, slice(0, half))
    up_b3.finish(up_ref, slice(up_ref.shape[1] // 2, up_ref.shape[1]))
    down_b3.finish(down_ref, slice(half, 2 * half))
    vec_receive(3)
    for r in range(1, zs):
        for k, got in enumerate((got_za, got_zb)):
            links.arrived(got.at[r - 1], z_first + 2 * (r - 1) + k, grid.device("z", r))
    for m in range(group):
        source = flip(me, m)
        for block, got, cols in (
            (z_a, got_za, slice(0, cut)),
            (z_b, got_zb, slice(cut, 3 * wide)),
        ):
            others = [got[r - 1, m ^ grid.mask("z", r)] for r in range(1, zs)]
            project_ref[source, :, cols] = total_of(block[0, m], others, F32)
    links.drain()


def tail(back, normed, weight, x, mid_grad, gain, early, down, up, out):
    grid = Grid()
    group, ys, xs, zs = grid.seq, grid.y, grid.x, grid.z
    rows, width = x.shape
    wide = width // group
    shape = jax.ShapeDtypeStruct
    any_place = pl.BlockSpec(memory_space=pl.ANY)
    here = any_spec()
    share = width // (grid.dp * grid.seq)
    (down, down_rest), (up, up_rest) = down, up
    down_block, up_block, out_block = down[0].shape, up[0].shape, out[0].shape
    vmem = lambda dims, kind=BF16: pltpu.VMEM(tuple(dims), kind)
    a_full, b_full = (share, 2 * wide), (share, wide)
    copies = (
        group
        + 2 * group
        + 2 * group * (ys - 1)
        + 2 * group * (xs - 1)
        + 4 * (xs - 1)
        + 4 * (ys - 1)
        + 8 * zs
        + (1 + (ys - 1) + (xs - 1) + (zs - 1))
        + 2 * (zs - 1)
    )
    hops = 1 + (ys - 1) + (xs - 1) + (zs - 1)
    scratch = (
        [
            vmem((group, rows, 3 * wide)),
            vmem((min(4, group), 3, width, wide)),
            vmem((rows, width)),
            vmem((rows, width), F32),
            vmem((rows, width), F32),
            vmem((width, rows), F32),
            vmem((2, ys, xs, zs, share, rows)),
        ]
        + [vmem((group, ys, xs, zs) + a_full), vmem((group, ys, xs, zs) + b_full)] * 3
        + [
            vmem((group, ys - 1, xs, zs) + a_full),
            vmem((group, xs - 1, ys, zs) + b_full),
            vmem((group, xs, zs) + a_full),
            vmem((group, ys, zs) + b_full),
            vmem((group, xs - 1, zs) + a_full),
            vmem((group, ys - 1, zs) + b_full),
            vmem((zs, group) + a_full),
            vmem((zs, group) + b_full),
            vmem((zs - 1, group) + a_full),
            vmem((zs - 1, group) + b_full),
        ]
        + [vmem(down_block)] * ys
        + [vmem((xs - 1,) + down_block[1:])]
        + [vmem(down_block[1:])] * 3
        + [vmem(up_block)] * xs
        + [vmem((ys - 1,) + up_block[1:])]
        + [vmem(up_block[1:])] * 3
        + [
            vmem((ys,) + down_block),
            vmem((ys - 1,) + down_block),
            vmem(down_block),
            vmem((xs - 1,) + down_block[1:]),
        ]
        + [vmem(down_block[1:])] * 3
        + [
            vmem((ys,) + up_rest[0].shape),
            vmem((ys - 1,) + up_rest[0].shape),
            vmem(up_rest[0].shape),
            vmem((xs - 1,) + up_block[1:]),
        ]
        + [vmem(up_block[1:])] * 3
        + [vmem(out_block)] * zs
        + [
            vmem((ys - 1,) + out_block[1:]),
            vmem(out_block[1:]),
            vmem((xs - 1,) + out_block[2:]),
        ]
        + [
            vmem((4,) + early.shape, F32),
            vmem((hops,) + early.shape, F32),
            pltpu.SemaphoreType.DMA((copies,)),
            pltpu.SemaphoreType.DMA((copies,)),
            pltpu.SemaphoreType.DMA((3 + 3 * ys + xs + zs + 3 * group,)),
        ]
    )
    return pl.pallas_call(
        functools.partial(tail_kernel, wide),
        in_specs=[any_place, any_place, here, any_place, any_place, here, here]
        + [any_place] * (3 * ys + xs + zs),
        out_specs=[here] * 6,
        out_shape=[
            shape((rows, width), BF16),
            shape((group, share, 3 * wide), F32),
            shape((down_block[2], width), F32),
            shape((up_block[2], 2 * up_block[3]), F32),
            shape(out_block[2:], F32),
            shape(early.shape, F32),
        ],
        scratch_shapes=scratch,
        compiler_params=params(collective_id=1, has_side_effects=True),
        cost_estimate=pl.CostEstimate(
            flops=12 * rows * width * width, bytes_accessed=2**25, transcendentals=0
        ),
        name="tail",
    )(back, weight, normed, x, mid_grad, gain[None], early, *down, *down_rest, *up, *up_rest, *out)


def layer(
    cap,
    tokens,
    first_gain,
    first_shift,
    project_weight,
    query_bias,
    value_bias,
    output_weight,
    output_bias,
    second_gain,
    second_shift,
    up_weight,
    up_bias,
    down_weight,
    down_bias,
    doc_offsets,
    active,
    upstream,
):
    group = lax.axis_size("seq")
    outer = lax.axis_size("dp") // 2
    rows, shard, width = tokens.shape
    length = active.shape[1]
    docs = doc_offsets.shape[1]
    wide = width // group
    heads = wide // HEAD_DIM
    me = lax.axis_index("seq").astype(jnp.int32)
    dp = lax.axis_index("dp").astype(jnp.int32)
    count = rows * cap

    place = jnp.arange(length, dtype=jnp.int32)
    ids = jnp.sum((doc_offsets[:, 1:, None] <= place).astype(jnp.int32), axis=1)
    live = active.reshape(rows, group, shard)
    rank = jnp.cumsum(live.astype(jnp.int32), axis=2) - 1
    slot = jnp.arange(cap, dtype=jnp.int32)[:, None]
    chosen = (rank[:, :, None, :] == slot) & live[:, :, None, :]
    ids = jnp.sum(
        jnp.where(chosen, ids.reshape(rows, group, 1, shard) + 1, 0), axis=3
    ).reshape(rows, group * cap)
    padded = -docs % 128
    unit = ids[:, :, None] == 1 + jnp.arange(docs + padded, dtype=jnp.int32)
    q_docs = unit.astype(BF16)
    k_docs = jnp.where(unit | (jnp.arange(docs + padded) >= docs), 0.0, NEG).astype(BF16)
    tiles = group * cap // TILE
    last = jnp.max(ids.reshape(rows, tiles, TILE), axis=2)
    first = jnp.min(jnp.where(ids == 0, docs + 1, ids).reshape(rows, tiles, TILE), axis=2)
    number = jnp.arange(tiles, dtype=jnp.int32)
    needed = (last[:, None, :] >= first[:, :, None]) & (number < number[:, None])
    low = jnp.min(jnp.where(needed, number, number[:, None]), axis=2) // 2
    scalars = jnp.concatenate([me[None], low.reshape(-1)])
    pick = lax.dynamic_index_in_dim(chosen, me, 1, keepdims=False).astype(BF16)
    live_here = lax.dynamic_index_in_dim(live, me, 1, keepdims=False)[:, :, None]

    def pack(values):
        return (
            jnp.einsum("rct,rtd->rcd", pick, values, preferred_element_type=F32)
            .astype(BF16)
            .reshape(count, width)
        )

    def unpack(packed, values):
        spread = jnp.einsum(
            "rct,rcd->rtd", pick, packed.reshape(rows, cap, width), preferred_element_type=F32
        ).astype(BF16)
        return jnp.where(live_here, spread, values)

    x = pack(tokens)
    g = pack(upstream)

    biases = jnp.stack([query_bias, jnp.zeros_like(query_bias), value_bias])
    bias_parts = biases.reshape(3, group, wide).transpose(1, 0, 2).reshape(group, 1, 3 * wide)

    weight = split_weight(project_weight, group)
    normed, head_parts = project(x, first_gain, first_shift, weight, bias_parts)
    ctx_chunks, lse = attend(scalars, head_parts, q_docs, k_docs, cap, heads)
    grad_parts, result, middle_grad, early, *halves = feed_forward(
        ctx_chunks,
        x,
        g,
        output_weight,
        output_bias,
        second_gain,
        second_shift,
        up_weight,
        up_bias,
        down_weight,
        down_bias,
    )
    ys, xs = Grid().y, Grid().x
    down, up, out = halves[: 2 * ys], halves[2 * ys : 3 * ys + xs], halves[3 * ys + xs : -3]
    down_parts = exchange("y", down[0::2]), down[1::2]
    up_parts = exchange("x", up[:xs]), up[xs:]
    out_parts = exchange("z", out)
    back = attend_back(
        scalars, head_parts, ctx_chunks, grad_parts, q_docs, k_docs, lse, cap, heads
    )
    token_grad, project_share, down_share, up_share, out_share, sums = tail(
        back, normed, weight, x, middle_grad, first_gain, early, down_parts, up_parts, out_parts
    )
    project_share = project_share.reshape(group, -1, 3, wide).transpose(1, 2, 0, 3)
    devices = 2 * outer * group
    index = dp * group + me
    mine = lambda v: lax.dynamic_index_in_dim(v, index, 1, keepdims=False)
    singles = mine(sums[:6].reshape(6, devices, -1))
    up_bias_share = mine(sums[6:VECTORS].reshape(1, devices, -1))[0]
    by_part = sums[VECTORS : VECTORS + group, : 3 * wide].reshape(group, 3, wide).transpose(1, 0, 2)
    by_part = mine(by_part.reshape(3, devices, -1))
    return (
        unpack(result, tokens),
        unpack(token_grad, upstream),
        singles[0],
        singles[1],
        project_share.reshape(-1, 3 * width),
        by_part[0],
        by_part[2],
        out_share,
        singles[2],
        singles[3],
        singles[4],
        up_share,
        up_bias_share,
        down_share,
        singles[5],
    )


def per_device(*args):
    *most, doc_offsets, exit_layers, layer_index, upstream = args
    shard = most[0].shape[1]
    active = exit_layers > layer_index[0]
    return layer(shard, *most, doc_offsets, active, upstream)


def solution(mesh):
    rows = P("dp", "seq", None)
    shares = P(("dp", "seq"))
    wide_shares = P(("dp", "seq"), None)
    in_specs = (rows,) + (P(),) * 13 + (P("dp", None), P("dp", None), P(), rows)
    out_specs = (
        rows,
        rows,
        shares,
        shares,
        wide_shares,
        shares,
        shares,
        wide_shares,
        shares,
        shares,
        shares,
        wide_shares,
        shares,
        wide_shares,
        shares,
    )
    return jax.shard_map(
        per_device, mesh=mesh, in_specs=in_specs, out_specs=out_specs, check_vma=False
    )
```

time: 1600 us -> 441 us (0.28)
  waiting for transfers between devices: 885 us -> 0.01 us
  Pallas kernels: 0 us -> 402 us
  matrix products: 339 us -> 8.35 us
  blocking collectives: 117 us -> 0 us
  local copies, waits for them, and re-layouts: 103 us -> 13.4 us
  other arithmetic: 87.1 us -> 9.77 us
  loops' own time: 27.1 us -> 0 us
    reduce_scatter x4 -> x0, waiting for transfers between devices: 764 us -> none  [the longest x1 360 us: per_device(): lax.psum_scatter(grad_down_weight, ('dp', 'seq'), scatter_dimension=0, ti...]
    pallas_call x0 -> x5, Pallas kernels: none -> 402 us  [the longest x1 142 us: tail(): pl.pallas_call(functools.partial(tail_kernel, wide), in_specs=[any_place,...]
    dot_general x68 -> x4, matrix products: 339 us -> 8.35 us  [the longest x2 5.51 us: unpack(): jnp.einsum('rct,rcd->rtd', pick, packed.reshape(rows, cap, width), prefer...]
    all_to_all x3 -> x0, waiting for transfers between devices: 121 us -> none  [the longest x1 69.8 us: per_device(): lax.all_to_all(packed_qkv, 'seq', split_axis=3, concat_axis=1, tiled=True)]
    all_to_all x1 -> x0, blocking collectives: 74.6 us -> none  [per_device(): lax.all_to_all(head_qkv_grad, 'seq', split_axis=1, concat_axis=3, tiled=T...]
    unnamed x1 -> x0, blocking collectives: 42.4 us -> none
    convert_element_type x11 -> x3, other arithmetic: 34.8 us -> 4.83 us  [the longest x1 2.06 us: layer(): jnp.where(unit | (jnp.arange(docs + padded) >= docs), 0.0, NEG).astype(BF16)]
    reduce_sum x16 -> x2, other arithmetic: 28.7 us -> 1.04 us  [the longest x1 0.94 us: layer(): jnp.sum(jnp.where(chosen, ids.reshape(rows, group, 1, shard) + 1, 0), axi...]
  transfers between devices with their start and end apart: 7 -> 5, of which waited for: 6 -> 0; matrix products, arithmetic and copies ran while one was open for 22% -> 1% of each run, Pallas kernels for 0% -> 9%
where the time goes in v2:
time: 441 us
  Pallas kernels  402 us (91%)
  local copies, waits for them, and re-layouts  13.4 us (3%)
  other arithmetic  9.77 us (2%)
  matrix products  8.35 us (2%)
  starting transfers between devices  5.9 us (1%)
    pallas_call x1, Pallas kernels, tail(): pl.pallas_call(functools.partial(tail_kernel, wide), in_specs=[any_place,...  142 us
    pallas_call x1, Pallas kernels, feed_forward(): pl.pallas_call(functools.partial(mid_kernel, wide), in_specs=[anywhere, h...  96.6 us
    pallas_call x1, Pallas kernels, project(): pl.pallas_call(functools.partial(first_kernel, wide), in_specs=[here, her...  84.3 us
    pallas_call x1, Pallas kernels, attend_back(): pl.pallas_call(functools.partial(attend_back_kernel, group, cap, tiles, h...  41 us
    pallas_call x1, Pallas kernels, attend(): pl.pallas_call(functools.partial(attend_kernel, group, cap, tiles, heads)...  38.3 us
  transfers between devices with their start and end apart: 5, of which 0 were waited for; matrix products, arithmetic and copies ran while one was open for 1% of the time, Pallas kernels for 9%

profile of v2, /device:TPU:0, one launch (start us, length us, event | category | flops | bytes accessed | tf_op | source)
XLA Modules:
  0.0 441.5 jit_solution(15076790542071935154)
XLA Ops:
  1.5 0.8 slice.52
  2.4 0.8 maximum_bitcast_fusion
  3.2 0.6 copy.79.refs_4_
  3.9 0.7 fusion.27
  4.7 1.2 reduce-window.6
  6.2 0.7 fusion
  6.9 0.9 select_reduce_fusion
  8.7 2.0 compare_convert_fusion.refs_1_.refs_3_
  10.7 2.1 select_convert_fusion.refs_2_.refs_4_
  12.8 1.4 convolution_convert_fusion.2
  14.2 1.4 convolution_convert_fusion.3
  15.6 0.6 pad_add_fusion.sc_ref
  16.2 84.3 %norm_project.1 = (bf16[512,1024]{1,0:T(8,128)(2,1)}, bf16[8,512,384]{2,1,0:T(8,128)(2,1)}) custom-call(bf16[512,1024]{1,0:T(8,128)(2,1)} %bitcast.72, f32[1,1024]{1,0:T(1,128)} %bitcast.93, f32[1,1024]{1,0:T(1,128)} %bitcast.88, bf16[1024,3072]{1,0:T(8,128)(2,1)} %refs_1_.1, f32[8,1,384]{2,1,0:T(1,128)} %copy.79.refs_4_), custom_call_target="tpu_custom_call" | custom-call | flops 3221225472 | bytes 9437184 | tf_op jit(solution)/shard_map/norm_project/pallas_call | solution.py:318
  100.5 38.3 %attend.1 = (bf16[8,512,128]{2,1,0:T(8,128)(2,1)}, f32[2,8,2,256]{3,2,1,0:T(2,128)}) custom-call(s32[17]{0:T(128)} %pad_add_fusion.sc_ref, bf16[8,512,384]{2,1,0:T(8,128)(2,1)} %get-tuple-element.41.refs_0_, bf16[2,2048,128]{2,1,0:T(8,128)(2,1)} %compare_convert_fusion.refs_1_.refs_3_, bf16[2,2048,128]{2,1,0:T(8,128)(2,1)} %select_convert_fusion.refs_2_.refs_4_), custom_call_target="tpu_custom_call" | custom-call | flops 8589934592 | bytes 4194304 | tf_op jit(solution)/shard_map/attend/pallas_call | solution.py:466
  138.7 96.6 %feed_forward.1 = (bf16[8,512,128]{2,1,0:T(8,128)(2,1)}, bf16[512,1024]{1,0:T(8,128)(2,1)}, f32[512,1024]{1,0:T(8,128)}, f32[24,1024]{1,0:T(8,128)}, bf16[2,4,12...) custom-call(bf16[8,512,128]{2,1,0:T(8,128)(2,1)} %get-tuple-element., ...), custom_call_target="tpu_custom_call" | custom-call | flops 30064771072 | bytes 37748736 | tf_op jit(solution)/shard_map/feed_forward/pallas_call | solution.py:857
  235.4 2.4 collective-permute-start.3
  237.8 2.0 collective-permute-start.4
  239.8 1.5 collective-permute-start.1
  241.3 41.0 %attend_back.1.refs_0_ = bf16[8,512,384]{2,1,0:T(8,128)(2,1)} custom-call(s32[17]{0:T(128)} %pad_add_fusion.sc_ref, bf16[8,512,384]{2,1,0:T(8,128)(2,1)} %get-tuple-element.41.refs_0_, bf16[8,512,128]{2,1,0:T(8,128)(2,1)} %get-tuple-element.42.refs_0_.refs_1_, bf16[8,512,128]{2,1,0:T(8,128)(2,1)} %get-tuple-element.44.refs_2_, ...), custom_call_target="tpu_custom_call" | custom-call | flops 21474836480 | bytes 10485760 | tf_op jit(solution)/shard_map/attend_back/pallas_call | solution.py:579
  282.3 2.7 fusion.1
  285.1 0.7 copy-done.5
  285.7 142.0 %tail.1 = (bf16[512,1024]{1,0:T(8,128)(2,1)}, f32[8,32,384]{2,1,0:T(8,128)}, f32[128,1024]{1,0:T(8,128)}, f32[32,4096]{1,0:T(8,128)}, f32[32,1024]{1,0:T(8,128)}, /*index=5*/f32[24,1024]{1,0:T(8,128)}) custom-call(bf16[8,512,384]{2,1,0:T(8,128)(2,1)} %attend_back.1.refs_0_, bf16[1024,3072]{1,0:T(8,128)(2,1)} %refs_1_.1, ...), custom_call_target="tpu_custom_call" | custom-call | flops 6442450944 | bytes 33554432 | tf_op jit(solution)/shard_map/tail/pallas_call | solution.py:1262
  427.8 1.4 slice_bitcast_fusion
  429.2 0.8 slice.62
  430.0 1.4 slice.53
  431.4 2.8 fusion.2
  434.2 0.8 reshape.164
  435.0 0.8 reshape.160
  436.3 0.8 copy.87
  438.1 1.6 copy.97
  439.7 0.8 copy.98
  440.5 0.8 copy.99
  (44 shorter events, 3.0 us)
Async XLA Ops:
  0.6 12.1 %copy-start.1 = (bf16[2,256,1024]{2,1,0:T(8,128)(2,1)S(1)}, bf16[2,256,1024]{2,1,0:T(8,128)(2,1)}, u32[]{:S(2)}) copy-start(bf16[2,256,1024]{2,1,0:T(8,128)(2,1)} %param.35) | copy-start | bytes 3145732
  0.7 13.5 %copy-start = (bf16[2,256,1024]{2,1,0:T(8,128)(2,1)S(1)}, bf16[2,256,1024]{2,1,0:T(8,128)(2,1)}, u32[]{:S(2)}) copy-start(bf16[2,256,1024]{2,1,0:T(8,128)(2,1)} %param.18) | copy-start | bytes 3145732
  235.4 49.7 %collective-permute-start.2 = (bf16[2,2,32,1024]{3,2,1,0:T(8,128)(2,1)}, bf16[2,2,32,1024]{3,2,1,0:T(8,128)(2,1)S(1)}, u32[]{:S(2)}, u32[]{:S(2)}) collective-permute-start(bf16[2,2,32,1024]{3,2,1,0:T(8,128)(2,1)} %get-tuple-element.58), channel_id=1, source_target_pairs={{0,2},{1,3},{2,0},{3,1},{4,6},{5,7},{6,4},{7,5},{8,10},{9,11},{10,... | collective-permute-start | bytes 786440 | tf_op jit(solution)/shard_map/ppermute | solution.py:914
  235.4 49.6 %collective-permute-start.3 = (bf16[2,2,32,1024]{3,2,1,0:T(8,128)(2,1)}, bf16[2,2,32,1024]{3,2,1,0:T(8,128)(2,1)}, u32[]{:S(2)}, u32[]{:S(2)}) collective-permute-start(bf16[2,2,32,1024]{3,2,1,0:T(8,128)(2,1)} %get-tuple-element.59), channel_id=1, source_target_pairs={{0,4},{1,5},{2,6},{3,7},{4,0},{5,1},{6,2},{7,3},{8,12},{9,13},{10,... | collective-permute-start | bytes 786440 | tf_op jit(solution)/shard_map/ppermute | solution.py:914
  237.8 47.2 %collective-permute-start.4 = (bf16[2,2,32,1024]{3,2,1,0:T(8,128)(2,1)}, bf16[2,2,32,1024]{3,2,1,0:T(8,128)(2,1)}, u32[]{:S(2)}, u32[]{:S(2)}) collective-permute-start(bf16[2,2,32,1024]{3,2,1,0:T(8,128)(2,1)} %get-tuple-element.60), channel_id=1, source_target_pairs={{0,6},{1,7},{2,4},{3,5},{4,2},{5,3},{6,0},{7,1},{8,14},{9,15},{10,... | collective-permute-start | bytes 786440 | tf_op jit(solution)/shard_map/ppermute | solution.py:914
  239.8 45.2 %collective-permute-start = (bf16[2,4,128,512]{3,2,1,0:T(8,128)(2,1)}, bf16[2,4,128,512]{3,2,1,0:T(8,128)(2,1)}, u32[]{:S(2)}, u32[]{:S(2)}) collective-permute-start(bf16[2,4,128,512]{3,2,1,0:T(8,128)(2,1)} %get-tuple-element.50), channel_id=1, source_target_pairs={{0,16},{8,24},{16,0},{24,8},{1,17},{9,25},{17,1},{25,9},{2,18},{10... | collective-permute-start | bytes 3145736 | tf_op jit(solution)/shard_map/ppermute | solution.py:914
  239.8 45.2 %collective-permute-start.1 = (bf16[2,4,32,2048]{3,2,1,0:T(8,128)(2,1)}, bf16[2,4,32,2048]{3,2,1,0:T(8,128)(2,1)}, u32[]{:S(2)}, u32[]{:S(2)}) collective-permute-start(bf16[2,4,32,2048]{3,2,1,0:T(8,128)(2,1)} %get-tuple-element.54), channel_id=1, source_target_pairs={{0,1},{1,0},{2,3},{3,2},{4,5},{5,4},{6,7},{7,6},{8,9},{9,8},{10,11... | collective-permute-start | bytes 3145736 | tf_op jit(solution)/shard_map/ppermute | solution.py:914
  285.0 0.7 copy-start.5
  427.8 8.1 %copy-start.4 = (f32[8,32,384]{2,1,0:T(8,128)S(1)}, f32[8,32,384]{2,1,0:T(8,128)}, u32[]{:S(2)}) copy-start(f32[8,32,384]{2,1,0:T(8,128)} %get-tuple-element.63) | copy-start | bytes 1179652
  431.4 8.3 %copy-start.3 = (f32[32,4096]{1,0:T(8,128)S(1)}, f32[32,4096]{1,0:T(8,128)}, u32[]{:S(2)}) copy-start(f32[32,4096]{1,0:T(8,128)} %get-tuple-element.107) | copy-start | bytes 1572868
  431.4 9.1 %copy-start.2 = (f32[128,1024]{1,0:T(8,128)S(1)}, f32[128,1024]{1,0:T(8,128)}, u32[]{:S(2)}) copy-start(f32[128,1024]{1,0:T(8,128)} %get-tuple-element.109) | copy-start | bytes 1572868

commit v3 on v2

--- a/solution.py
+++ b/solution.py
@@ -46,16 +46,27 @@
     return pl.BlockSpec(memory_space=pltpu.SMEM)
 
 
-def flip(index, mask):
+def flip(index, mask, size=64):
     bit = 1
     out = index
-    while bit <= mask:
-        if mask & bit:
+    while bit < size:
+        if not isinstance(mask, int):
+            ours, theirs = (index // bit) % 2, (mask // bit) % 2
+            out = out + bit * (theirs - 2 * ours * theirs)
+        elif mask & bit:
             out = out + bit * (1 - 2 * ((index // bit) % 2))
         bit *= 2
     return out
 
 
+def loop(first, last, body):
+    def turn(i, _):
+        body(i)
+        return 0
+
+    lax.fori_loop(first, last, turn, 0)
+
+
 class Links:
     def __init__(self, send_sem, recv_sem):
         self.send_sem, self.recv_sem, self.used, self.sent = send_sem, recv_sem, 0, []
@@ -64,7 +75,7 @@
         first, self.used = self.used, self.used + count
         return first
 
-    def start(self, src, dst, slot, there, device):
+    def start(self, src, dst, slot, there, device, later=True):
         copy = pltpu.make_async_remote_copy(
             src_ref=src,
             dst_ref=dst,
@@ -74,7 +85,18 @@
             device_id_type=pl.DeviceIdType.MESH,
         )
         copy.start()
-        self.sent.append(copy)
+        if later:
+            self.sent.append(copy)
+
+    def left(self, src, slot, device):
+        pltpu.make_async_remote_copy(
+            src_ref=src,
+            dst_ref=src,
+            send_sem=self.send_sem.at[slot],
+            recv_sem=self.recv_sem.at[slot],
+            device_id=device,
+            device_id_type=pl.DeviceIdType.MESH,
+        ).wait_send()
 
     def arrived(self, ref, slot, device):
         pltpu.make_async_remote_copy(
@@ -126,9 +148,13 @@
 
 
 def add_into(total, others):
-    for i in range(total.shape[0]):
-        for j in range(total.shape[1]):
-            total[i, j] = total_of(total[i, j], [other[i, j] for other in others], total.dtype)
+    inner = total.shape[1]
+
+    def one(k):
+        i, j = k // inner, k % inner
+        total[i, j] = total_of(total[i, j], [other[i, j] for other in others], total.dtype)
+
+    loop(0, total.shape[0] * inner, one)
 
 
 class Summed:
@@ -149,10 +175,17 @@
             self.links.arrived(
                 self.got.at[r - 1], self.slot + r - 1, self.grid.device(self.axis, r)
             )
-        for i in range(store.shape[0]):
-            store[i] = total_of(
-                self.block[0, i], [self.got[r - 1, i] for r in range(1, self.size)], kind
-            )
+        inner = store.shape[1]
+
+        def one(k):
+            i, j = k // inner, k % inner
+            others = [self.got[r - 1, i, j] for r in range(1, self.size)]
+            store[i, j] = total_of(self.block[0, i, j], others, kind)
+
+        if len(store.shape) == 4:
+            loop(0, store.shape[0] * inner, one)
+        else:
+            store[...] = total_of(self.block[0], [self.got[r - 1] for r in range(1, self.size)], kind)
 
     def receive_last(self, store):
         for r in range(1, self.size):
@@ -191,7 +224,7 @@
 
     def hop(self, k):
         for way, at in ((1, k), (-1, self.size - 1 - k)):
-            goals = range(at + 1, self.size) if way == 1 else range(at - 1, -1, -1)
+            goals = range(self.size - 1, at, -1) if way == 1 else range(at)
 
             @pl.when(self.place == at)
             def _(way=way, goals=goals):
@@ -208,25 +241,27 @@
         self.copy(way, goal, self.got[way].at[goal]).wait_recv()
 
     def finish(self, store, cols):
-        for at in range(self.size):
-
-            @pl.when(self.place == at)
-            def _(at=at):
-                ways = [way for way in (1, -1) if (at > 0 if way == 1 else at < self.size - 1)]
-                for way in ways:
-                    self.arrived(way, at)
-                store[:, cols] = total_of(self.block[0], [self.got[w][at] for w in ways], F32)
-                for way, k in ((1, at), (-1, self.size - 1 - at)):
-                    goals = range(at + 1, self.size) if way == 1 else range(at - 1, -1, -1)
-                    for goal in goals:
-                        self.copy(way, goal, self.source(way, goal, k == 0)).wait_send()
+        store[:, cols] = self.block[0].astype(F32)
+        for way, limit in ((1, self.place > 0), (-1, self.place < self.size - 1)):
+
+            @pl.when(limit)
+            def _(way=way):
+                self.arrived(way, self.place)
+                store[:, cols] = store[:, cols] + self.got[way][self.place].astype(F32)
+
+        for way in (1, -1):
+            for goal in range(self.size):
+
+                @pl.when(self.place < goal if way == 1 else self.place > goal)
+                def _(way=way, goal=goal):
+                    self.copy(way, goal, self.got[way].at[goal]).wait_send()
 
 
 class SlotSum:
     def __init__(self, links, grid, axis, slots, block, got, inner=False):
         self.links, self.grid, self.axis, self.got = links, grid, axis, got
         self.block = (lambda m, r: block.at[m, :, r]) if inner else (lambda m, r: block.at[m, r])
-        self.size = grid.size[axis]
+        self.size, self.slots = grid.size[axis], slots
         self.first = links.reserve(slots * (self.size - 1))
 
     def id(self, m, r):
@@ -234,13 +269,14 @@
 
     def send(self, m):
         for r in range(1, self.size):
-            there = m ^ self.grid.mask(self.axis, r)
+            there = flip(m, self.grid.mask(self.axis, r), self.slots)
             self.links.start(
                 self.block(m, r),
                 self.got.at[there, r - 1],
                 self.id(m, r),
                 self.id(there, r),
                 self.grid.device(self.axis, r),
+                later=False,
             )
 
     def receive(self, m):
@@ -251,6 +287,10 @@
         return total_of(
             self.block(m, 0)[...], [self.got[m, r - 1] for r in range(1, self.size)], F32
         )
+
+    def drain(self, m):
+        for r in range(1, self.size):
+            self.links.left(self.block(m, r), self.id(m, r), self.grid.device(self.axis, r))
 
 
 def split_weight(weight, group):
@@ -308,7 +348,7 @@
     own.wait()
 
 
-def project(x, gain, shift, weight, bias_parts):
+def project(branch, x, gain, shift, weight, bias_parts):
     rows, width = x.shape
     group = bias_parts.shape[0]
     wide = width // group
@@ -331,7 +371,7 @@
             pltpu.SemaphoreType.DMA((3 * group,)),
             pltpu.SemaphoreType.DMA,
         ],
-        compiler_params=params(collective_id=2, has_side_effects=True),
+        compiler_params=params(collective_id=3 * branch + 1, has_side_effects=True),
         cost_estimate=pl.CostEstimate(
             flops=2 * rows * width * cols * group,
             bytes_accessed=2 * group * cols * (width + rows),
@@ -385,10 +425,17 @@
     return pl.ds(at if isinstance(at, int) else pl.multiple_of(at, TILE), size)
 
 
+def blank_rest(used, *arrays):
+    if used < arrays[0].shape[0]:
+        for array in arrays:
+            array[used:, :] = jnp.zeros((array.shape[0] - used, array.shape[1]), array.dtype)
+
+
 def load_heads(me, cap, parts, q_s, k_s, v_s):
     wide = v_s.shape[1]
+    blank_rest(parts.shape[0] * cap, q_s, k_s, v_s)
     for m in range(parts.shape[0]):
-        here = pl.ds(pl.multiple_of((me ^ m) * cap, 32), cap)
+        here = pl.ds(pl.multiple_of((me ^ m) * cap, math.gcd(cap, 128)), cap)
         q_s[here, :] = parts[m, :, :wide] * SCALE
         k_s[here, :wide] = parts[m, :, wide : 2 * wide]
         v_s[here, :] = parts[m, :, 2 * wide :]
@@ -450,14 +497,14 @@
 
     sweep(tiles, lambda i: sc_ref[1 + row * tiles + i], start, step, finish)
     for m in range(group):
-        out_ref[m] = o_s[pl.ds(pl.multiple_of((me ^ m) * cap, 32), cap), :]
+        out_ref[m] = o_s[pl.ds(pl.multiple_of((me ^ m) * cap, math.gcd(cap, 128)), cap), :]
 
 
 def attend(scalars, parts, q_docs, k_docs, cap, heads):
     group, tokens, cols = parts.shape
     rows = tokens // cap
-    length = group * cap
-    tiles = length // TILE
+    tiles = pl.cdiv(group * cap, TILE)
+    length = tiles * TILE
     wide = heads * HEAD_DIM
     deep = wide + q_docs.shape[2]
     pair = rows * heads * length * length // 2
@@ -503,8 +550,9 @@
     row = pl.program_id(0)
     load_heads(me, cap, parts, q_s, k_s, v_s)
     k_s[:, wide:] = k_docs[0]
+    blank_rest(group * cap, g_s, o_s)
     for m in range(group):
-        here = pl.ds(pl.multiple_of((me ^ m) * cap, 32), cap)
+        here = pl.ds(pl.multiple_of((me ^ m) * cap, math.gcd(cap, 128)), cap)
         g_s[here, :] = grads[m]
         o_s[here, :] = ctx[m]
     for t in range(tiles):
@@ -560,7 +608,7 @@
 
     sweep(tiles, lambda i: sc_ref[1 + row * tiles + i], start, step, finish)
     for m in range(group):
-        here = pl.ds(pl.multiple_of((me ^ m) * cap, 32), cap)
+        here = pl.ds(pl.multiple_of((me ^ m) * cap, math.gcd(cap, 128)), cap)
         out_ref[m, :, :wide] = dq_s[here, :]
         out_ref[m, :, wide : 2 * wide] = dk_s[here, :].astype(BF16)
         out_ref[m, :, 2 * wide :] = dv_s[here, :].astype(BF16)
@@ -569,8 +617,8 @@
 def attend_back(scalars, parts, ctx, grads, q_docs, k_docs, lse, cap, heads):
     group, tokens, cols = parts.shape
     rows = tokens // cap
-    length = group * cap
-    tiles = length // TILE
+    tiles = pl.cdiv(group * cap, TILE)
+    length = tiles * TILE
     wide = heads * HEAD_DIM
     deep = wide + q_docs.shape[2]
     pair = rows * heads * length * length // 2
@@ -618,6 +666,11 @@
 VECTORS = 10
 
 
+def early_cols(cols, late):
+    early = cols * 3 // 4
+    return cols - early if late else early
+
+
 def mid_kernel(wide, *refs):
     grid = Grid()
     group, ys, xs, zs = grid.seq, grid.y, grid.x, grid.z
@@ -633,7 +686,7 @@
     down_out, up_out, out_out = take(2 * ys), take(xs + ys), take(zs)
     gots = take(3)
     landed, ctx, ow, uw, dw, hid, rise, mid_s, n2_s, normed, attn, chunk = take(12)
-    flat_ring, tall_ring, flat_got, tall_got = take(4)
+    rings, loaded, lefts = take(3), take(3), take(6)
     send_sem, recv_sem, load_sem, ring_sem, got_sem = take(5)
 
     me, dp = lax.axis_index("seq"), lax.axis_index("dp")
@@ -696,7 +749,143 @@
         n2_s[...] += dot(up, uw[:, here], NT)
         return 0
 
-    lax.fori_loop(0, hidden // block, through, 0)
+    def ordered(ring, spot, total, parts, share, got):
+        for s in range(parts):
+            rel = flip(me % parts, s)
+            piece = total[s * share : (s + 1) * share]
+            if got is not None:
+                piece = piece + got[rel % xs, rel // xs].astype(F32)
+            ring[spot, rel % xs, rel // xs] = piece.astype(BF16)
+
+    def outputs(item, o, z, cols, ring):
+        if item == 0:
+            first = down_out[0].shape[-1]
+            for h, here in enumerate((slice(0, first), slice(first, width))):
+                yield ring.at[:, :, :, here], down_out[2 * o + h].at[:, z]
+        elif item == 1:
+            first = up_out[0].shape[-1]
+            if cols.start >= first:
+                here = slice(cols.start - first, cols.stop - first)
+                yield ring, up_out[xs + o].at[:, :, :, here]
+            else:
+                for x in range(xs):
+                    yield ring.at[x], up_out[x].at[o, :, :, cols]
+        else:
+            for z in range(zs):
+                yield ring.at[:, z], out_out[z].at[o]
+
+    def weight_grad(item, a, b):
+        share = a.shape[1] // (2 * ys * group)
+        parts = min(group, max(256 // share, xs))
+        sub = group // parts
+        depth = parts // xs
+        cols = b.shape[1]
+        piece = min(1024, cols)
+        pieces = cols // piece
+        count = ys * sub * pieces
+        ring, got, left_s = rings[item], loaded[item], lefts[2 * item : 2 * item + 2]
+        spots = ring.shape[0] // 2
+        slot = links.reserve(count)
+
+        def unit(n):
+            u = n // pieces
+            return ys - 1 - u // sub, u % sub, n % pieces
+
+        def start_of(c, n):
+            o, k, _ = unit(n)
+            at = (flip(row, o, ys) * 2 + flip(core, c, 2)) * group * share
+            return at + flip(me // parts, k, sub) * parts * share
+
+        def product(c, n):
+            o, k, p = unit(n)
+            left = left_s[c]
+
+            @pl.when(p == 0)
+            def _():
+                at = pl.multiple_of(start_of(c, n), 128)
+                left[...] = transposed(a[:, pl.ds(at, parts * share)])
+
+            return dot(left[...], b[:, pl.ds(pl.multiple_of(p * piece, piece), piece)])
+
+        def place(n):
+            o, k, p = unit(n)
+            columns = pl.ds(pl.multiple_of(p * piece, piece), piece)
+            return (o, slice(None), pl.ds(k * depth, depth), slice(None), columns)
+
+        def away(n):
+            links.left(ring.at[n % spots], slot + n, partner_core)
+
+        def send(n):
+            @pl.when(n >= spots)
+            def _():
+                away(n - spots)
+
+            ordered(ring, n % spots, product(1, n), parts, share, None)
+            there = gots[item].at[place(n)]
+            links.start(ring.at[n % spots], there, slot + n, slot + n, partner_core, later=False)
+
+        def fetch(n):
+            src = gots[item].at[place(n)]
+            return pltpu.make_async_copy(src, got.at[n % 2], got_sem.at[2 * item + n % 2])
+
+        def fetch_start(n):
+            links.arrived(gots[item].at[place(n)], slot + n, partner_core)
+            fetch(n).start()
+
+        def written(n, act):
+            for fixed in range(ys):
+                for p in range(pieces):
+                    o, k, q = unit(n)
+
+                    @pl.when((o == fixed) & (q == p))
+                    def _(fixed=fixed, p=p):
+                        spot = spots + n % spots
+                        z = pl.ds(k * depth, depth)
+                        here = slice(p * piece, (p + 1) * piece)
+                        copies = outputs(item, fixed, z, here, ring.at[spot])
+                        for h, (src, dst) in enumerate(copies):
+                            at = (item * spots + n % spots) * max(2, xs, zs) + h
+                            act(pltpu.make_async_copy(src, dst, ring_sem.at[at]))
+
+        def keep(n):
+            @pl.when(n + 1 < count)
+            def _():
+                fetch_start(n + 1)
+
+            @pl.when(n >= spots)
+            def _():
+                written(n - spots, lambda copy: copy.wait())
+
+            total = product(0, n)
+            fetch(n).wait()
+            ordered(ring, spots + n % spots, total, parts, share, got.at[n % 2])
+            written(n, lambda copy: copy.start())
+
+        def rest(act):
+            for n in range(max(0, count - spots), count):
+                act(n)
+
+        def finish():
+            rest(lambda n: written(n, lambda copy: copy.wait()))
+
+        return count, send, lambda: rest(away), fetch_start, keep, finish, start_of
+
+    first_job = weight_grad(0, hid, g_ref)
+    steps = hidden // block
+    per = first_job[0] * 2 // steps
+
+    def mine(i):
+        c = 1 - 2 * i // steps
+        f = first_job[6](c, (i % (steps // 2)) * per) // block
+        through(f, 0)
+
+        @pl.when(c == 1)
+        def _():
+            for k in range(per):
+                first_job[1](i * per + k)
+
+    loop(0, steps, mine)
+    first_job[2]()
     n, rs = centre_rows(mid_s[...])
     n2 = n2_s[...]
     early[3:4, :] = jnp.sum(n2 * n, axis=0, keepdims=True)
@@ -713,127 +902,44 @@
     own = pltpu.make_async_copy(chunk.at[0], grads.at[0], load_sem.at[0])
     own.start()
 
-    rings = {"flat": flat_ring, "tall": tall_ring}
-    loaded = {"flat": flat_got, "tall": tall_got}
-    busy = {"flat": [None] * flat_ring.shape[0], "tall": [None] * tall_ring.shape[0]}
-    places = {"flat": 0, "tall": flat_ring.shape[0]}
-    made = {"flat": 0, "tall": 0}
-    arriving = {}
-
-    def ordered(ring, spot, total, parts, share, got):
-        for s in range(parts):
-            rel = flip(me % parts, s)
-            piece = total[s * share : (s + 1) * share]
-            if got is not None:
-                piece = piece + got[rel % xs, rel // xs].astype(F32)
-            ring[spot, rel % xs, rel // xs] = piece.astype(BF16)
-
-    def outputs(item, o, z, cols, ring):
-        if item == 0:
-            half = down_out[0].shape[-1]
-            for h in range(2):
-                yield ring.at[:, :, :, h * half : (h + 1) * half], down_out[2 * o + h].at[:, z]
-        elif item == 1:
-            half = up_out[0].shape[-1]
-            h, at = cols.start // half, cols.start % half
-            here = slice(at, at + cols.stop - cols.start)
-            if h:
-                yield ring, up_out[xs + o].at[:, :, :, here]
-            else:
-                for x in range(xs):
-                    yield ring.at[x], up_out[x].at[o, :, :, here]
-        else:
-            for z in range(zs):
-                yield ring.at[:, z], out_out[z].at[o]
-
-    def weight_grad(kind, item, a, b):
-        share = a.shape[1] // (2 * ys * group)
-        parts = min(group, max(256 // share, xs))
-        sub = group // parts
-        depth = parts // xs
-        cols = b.shape[1]
-        piece = min(1024, cols)
-        ring, got = rings[kind], loaded[kind]
-        units = [(o, k, p) for o in reversed(range(ys)) for k in range(sub) for p in range(0, cols, piece)]
-
-        def rows_of(c, o, k):
-            at = (flip(row, o) * 2 + flip(core, c)) * group * share
-            at = at + flip(me // parts, k) * parts * share
-            return transposed(a[:, pl.ds(pl.multiple_of(at, 128), parts * share)])
-
-        def place(o, k, p):
-            return (o, slice(None), slice(k * depth, (k + 1) * depth), slice(None), slice(p, p + piece))
-
-        def spot_of():
-            spot = made[kind] % ring.shape[0]
-            made[kind] += 1
-            for wait in busy[kind][spot] or ():
-                wait()
-            return spot
-
-        for n, (o, k, p) in enumerate(units):
-            if p == 0:
-                left = rows_of(1, o, k)
-            total = dot(left, b[:, p : p + piece])
-            spot = spot_of()
-            ordered(ring, spot, total, parts, share, None)
-            slot = links.reserve(1)
-            copy = pltpu.make_async_remote_copy(
-                src_ref=ring.at[spot],
-                dst_ref=gots[item].at[place(o, k, p)],
-                send_sem=send_sem.at[slot],
-                recv_sem=recv_sem.at[slot],
-                device_id=partner_core,
-                device_id_type=pl.DeviceIdType.MESH,
-            )
-            copy.start()
-            busy[kind][spot] = [copy.wait_send]
-            arriving[n] = slot
-
-        def fetch(n):
-            src = gots[item].at[place(*units[n])]
-            links.arrived(src, arriving[n], partner_core)
-            copy = pltpu.make_async_copy(src, got.at[n % 2], got_sem.at[2 * item + n % 2])
-            copy.start()
-            return copy
-
-        coming = fetch(0)
-        for n, (o, k, p) in enumerate(units):
-            if p == 0:
-                left = rows_of(0, o, k)
-            total = dot(left, b[:, p : p + piece])
-            coming.wait()
-            if n + 1 < len(units):
-                coming = fetch(n + 1)
-            spot = spot_of()
-            ordered(ring, spot, total, parts, share, got.at[n % 2])
-            busy[kind][spot] = []
-            z = slice(k * depth, (k + 1) * depth)
-            for h, (src, dst) in enumerate(outputs(item, o, z, slice(p, p + piece), ring.at[spot])):
-                sem = ring_sem.at[(places[kind] + spot) * max(2, xs, zs) + h]
-                copy = pltpu.make_async_copy(src, dst, sem)
-                copy.start()
-                busy[kind][spot].append(copy.wait)
-
-    weight_grad("tall", 0, hid, g_ref)
-    weight_grad("flat", 1, normed, rise)
-    weight_grad("flat", 2, ctx, attn)
-    result_ref[...] = (mid_s[...] + (dot(hid[...], dw[...]) + db[...])).astype(BF16)
+    jobs = [first_job, weight_grad(1, normed, rise), weight_grad(2, ctx, attn)]
+    for stage in range(1, len(jobs) + 1):
+        new = jobs[stage] if stage < len(jobs) else None
+        old = jobs[stage - 1]
+        old[3](0)
+
+        def turn(n, new=new, old=old):
+            for job, act in ((new, 1), (old, 4)):
+                if job:
+                    if new and old and job[0] < max(new[0], old[0]):
+                        pl.when(n < job[0])(lambda job=job, act=act: job[act](n))
+                    else:
+                        job[act](n)
+
+        loop(0, max(job[0] for job in (new, old) if job), turn)
+        if new:
+            new[2]()
+        old[5]()
+
+
+    def finished(k):
+        here = lanes(k, 256)
+        result_ref[:, here] = (
+            mid_s[:, here] + (dot(hid[...], dw[:, here]) + db[:, here])
+        ).astype(BF16)
+
+    loop(0, width // 256, finished)
     early[2:3, :] = jnp.sum(attn[...].astype(F32), axis=0, keepdims=True)
     for k in range(hidden // width):
         part = rise[:, k * width : (k + 1) * width].astype(F32)
         early[6 + k : 7 + k, :] = jnp.sum(part, axis=0, keepdims=True)
     for m in range(1, group):
         links.arrived(grads.at[m], second + m, {"seq": flip(me, m)})
-    for spots in busy.values():
-        for waits in spots:
-            for wait in waits or ():
-                wait()
     own.wait()
     links.drain()
 
 
-def feed_forward(ctx, x, g, ow, ob, gain, shift, uw, ub, dw, db):
+def feed_forward(branch, ctx, x, g, ow, ob, gain, shift, uw, ub, dw, db):
     grid = Grid()
     group, ys, xs, zs = grid.seq, grid.y, grid.x, grid.z
     rows, width = x.shape
@@ -851,7 +957,9 @@
         shape((ys, xs, zs, low, width), BF16),
     ]
     parts = lambda share: min(group, max(256 // share, xs))
-    ring = lambda share, n: pltpu.VMEM((n, xs, parts(share) // xs, share, width), BF16)
+    block = lambda share: (xs, parts(share) // xs, share, width)
+    rings = [pltpu.VMEM((n,) + block(share), BF16) for n in (4, 2) for share in (high, low, low)]
+    turned = [pltpu.VMEM((parts(s) * s, rows), BF16) for s in (high, low, low) for _ in range(2)]
     blocks = ys * (group // parts(high)) + ys * (hidden // width) + ys
     vmem = lambda dims, kind=BF16: pltpu.VMEM(dims, kind)
     return pl.pallas_call(
@@ -864,9 +972,9 @@
             shape((rows, width), F32),
             shape((vectors, width), F32),
         ]
-        + [shape((xs, zs, high, width // 2), BF16)] * (2 * ys)
-        + [shape((ys, zs, low, hidden // 2), BF16)] * xs
-        + [shape((xs, zs, low, hidden // 2), BF16)] * ys
+        + [shape((xs, zs, high, early_cols(width, k)), BF16) for _ in range(ys) for k in range(2)]
+        + [shape((ys, zs, low, early_cols(hidden, 0)), BF16)] * xs
+        + [shape((xs, zs, low, early_cols(hidden, 1)), BF16)] * ys
         + [shape((ys, xs, low, width), BF16)] * zs
         + sums,
         scratch_shapes=[
@@ -882,17 +990,17 @@
             vmem((rows, width)),
             vmem((rows, width)),
             vmem((group, rows, wide)),
-            ring(low, 4),
-            ring(high, 4),
-            ring(low, 2),
-            ring(high, 2),
+        ]
+        + rings
+        + turned
+        + [
             pltpu.SemaphoreType.DMA((2 * group + blocks,)),
             pltpu.SemaphoreType.DMA((2 * group + blocks,)),
             pltpu.SemaphoreType.DMA((4,)),
-            pltpu.SemaphoreType.DMA((8 * max(2, xs, zs),)),
+            pltpu.SemaphoreType.DMA((6 * max(2, xs, zs),)),
             pltpu.SemaphoreType.DMA((6,)),
         ],
-        compiler_params=params(collective_id=3, has_side_effects=True),
+        compiler_params=params(collective_id=3 * branch + 2, has_side_effects=True),
         cost_estimate=pl.CostEstimate(
             flops=8 * rows * width * width + 12 * rows * width * hidden,
             bytes_accessed=4 * width * width + 8 * width * hidden,
@@ -970,18 +1078,25 @@
         [load(src, up_b[0].at[o]) for o, src in enumerate(up_rest)],
     ]
 
-    def load_weight(m):
-        source = flip(me, m)
-        out = []
-        for part in range(3):
-            src = weight_view(weight, part, source, width, wide)
-            out.append(load(src, w_s.at[m % ahead, part]))
-        return out
-
-    ahead = w_s.shape[0]
-    own_w = [load_weight(m) for m in range(ahead)]
     own_x = load(x_hbm, x_s)
     own_mg = load(mg_hbm, mg_s)
+    ahead = w_s.shape[0]
+    weight_first = len(loads)
+
+    def weight_copies(m):
+        source = flip(me, m, group)
+        return [
+            pltpu.make_async_copy(
+                weight_view(weight, part, source, width, wide),
+                w_s.at[m % ahead, part],
+                load_sem.at[weight_first + 3 * m + part],
+            )
+            for part in range(3)
+        ]
+
+    for m in range(ahead):
+        for copy in weight_copies(m):
+            copy.start()
 
     def summed(axis, block, got):
         return Summed(links, grid, axis, block, got)
@@ -1016,11 +1131,13 @@
         turned[k : k + 256, :] = normed_ref[:, k : k + 256].astype(F32).T
     for c in range(2):
         for o in range(ys):
-            for x in range(xs):
-                for z in range(zs):
-                    there = (flip(row, o) * 2 + flip(core, c)) * group + flip(me, z * xs + x)
-                    rows = turned[pl.ds(pl.multiple_of(there * share, share), share), :]
-                    order[c, o, x, z] = rows.astype(BF16)
+
+            def place(s, c=c, o=o):
+                there = (flip(row, o) * 2 + flip(core, c)) * group + flip(me, s, group)
+                rows = turned[pl.ds(pl.multiple_of(there * share, share), share), :]
+                order[c, o, s % xs, s // xs] = rows.astype(BF16)
+
+            loop(0, group, place)
     half = ys * group * share
     acc[...] = jnp.zeros_like(acc)
     vec_s[0] = early_ref[...]
@@ -1034,9 +1151,12 @@
     cut = 2 * wide
 
     def multiply(m):
-        if m:
-            links.arrived(landed.at[m], first + m, {"seq": flip(me, m)})
-        source = flip(me, m)
+        source = flip(me, m, group)
+
+        @pl.when(m > 0)
+        def _():
+            links.arrived(landed.at[m], first + m, {"seq": source})
+
         for k, (send, keep, pair, cols) in enumerate(
             (
                 (send_a, keep_a, pair_a, slice(0, cut)),
@@ -1047,16 +1167,20 @@
             left = order[1].reshape(half, tokens)
             send[m] = dot(left, grad).reshape(send.shape[1:]).astype(BF16)
             slot = pair_first + 2 * m + k
-            links.start(send.at[m], pair.at[m], slot, slot, partner_core)
+            links.start(send.at[m], pair.at[m], slot, slot, partner_core, later=False)
             left = order[0].reshape(half, tokens)
             keep[m] = dot(left, grad).reshape(keep.shape[1:]).astype(BF16)
         block = landed[m]
-        for copy in own_w[m]:
+        for copy in weight_copies(m):
             copy.wait()
         pieces = [w_s[m % ahead, part] for part in range(3)]
         acc[...] += dot(block, jnp.concatenate(pieces, axis=1), NT)
-        if m + ahead < group:
-            own_w.append(load_weight(m + ahead))
+
+        @pl.when(m + ahead < group)
+        def _():
+            for copy in weight_copies(m + ahead):
+                copy.start()
+
         sums = jnp.sum(block.astype(F32), axis=0, keepdims=True)
         vec_s[0, pl.ds(VECTORS + source, 1), : 3 * wide] = sums
 
@@ -1073,12 +1197,10 @@
         b2.send(m)
 
     def third(m):
-        total = a2.receive(m).astype(BF16)
-        for z in range(zs):
-            z_a[z, m] = total[z]
-        total = b2.receive(m).astype(BF16)
-        for z in range(zs):
-            z_b[z, m] = total[z]
+        for block, stage in ((z_a, a2), (z_b, b2)):
+            total = stage.receive(m).astype(BF16)
+            for z in range(zs):
+                block[z, m] = total[z]
 
     def input_grads():
         own_x.wait()
@@ -1112,13 +1234,17 @@
         else:
             vec_ref[...] = total
 
-    for m in range(group):
+    def multiply_next(m):
         multiply(m)
-        if m:
+
+        @pl.when(m > 0)
+        def _():
             paired(m - 1)
-        if m == group // 2:
-            down_b1.receive(down_b[2])
-            down_b2.send()
+
+    loop(0, group // 2 + 1, multiply_next)
+    down_b1.receive(down_b[2])
+    down_b2.send()
+    loop(group // 2 + 1, group, multiply_next)
     paired(group - 1)
     down_a1.receive(down_a[ys + 1])
     down_a2.hop(0)
@@ -1136,19 +1262,17 @@
         down_a2.hop(k)
         up_a2.hop(k)
     vec_receive(0)
-    for m in range(group):
-        second(m)
-        if m == group // 2:
-            for k in range(1, zs - 1):
-                down_b3.hop(k)
+    loop(0, group // 2, second)
+    for k in range(1, zs - 1):
+        down_b3.hop(k)
+    loop(group // 2, group, second)
     vec_receive(1)
     up_b2.receive(up_b[4])
     up_b3.hop(0)
-    for m in range(group):
-        third(m)
-        if m == group // 2:
-            for k in range(1, zs - 1):
-                up_b3.hop(k)
+    loop(0, group // 2, third)
+    for k in range(1, zs - 1):
+        up_b3.hop(k)
+    loop(group // 2, group, third)
 
     z_first = links.reserve(2 * (zs - 1))
     for r in range(1, zs):
@@ -1156,28 +1280,39 @@
             slot = z_first + 2 * (r - 1) + k
             links.start(block.at[r], got.at[r - 1], slot, slot, grid.device("z", r))
     vec_receive(2)
-    half = down_ref.shape[1] // 2
+    cut_down, cut_up = early_cols(down_ref.shape[1], 0), early_cols(up_ref.shape[1], 0)
     out_2.receive_last(out_ref)
-    up_a2.finish(up_ref, slice(0, up_ref.shape[1] // 2))
-    down_a2.finish(down_ref, slice(0, half))
-    up_b3.finish(up_ref, slice(up_ref.shape[1] // 2, up_ref.shape[1]))
-    down_b3.finish(down_ref, slice(half, 2 * half))
+    up_a2.finish(up_ref, slice(0, cut_up))
+    down_a2.finish(down_ref, slice(0, cut_down))
+    up_b3.finish(up_ref, slice(cut_up, up_ref.shape[1]))
+    down_b3.finish(down_ref, slice(cut_down, down_ref.shape[1]))
     vec_receive(3)
     for r in range(1, zs):
         for k, got in enumerate((got_za, got_zb)):
             links.arrived(got.at[r - 1], z_first + 2 * (r - 1) + k, grid.device("z", r))
-    for m in range(group):
-        source = flip(me, m)
+
+    def share_of(m):
+        source = flip(me, m, group)
         for block, got, cols in (
             (z_a, got_za, slice(0, cut)),
             (z_b, got_zb, slice(cut, 3 * wide)),
         ):
-            others = [got[r - 1, m ^ grid.mask("z", r)] for r in range(1, zs)]
+            others = [got[r - 1, flip(m, grid.mask("z", r), group)] for r in range(1, zs)]
             project_ref[source, :, cols] = total_of(block[0, m], others, F32)
+
+    loop(0, group, share_of)
+
+    def drain(m):
+        for k, send in enumerate((send_a, send_b)):
+            links.left(send.at[m], pair_first + 2 * m + k, partner_core)
+        for stage in (a1, a2, b1, b2):
+            stage.drain(m)
+
+    loop(0, group, drain)
     links.drain()
 
 
-def tail(back, normed, weight, x, mid_grad, gain, early, down, up, out):
+def tail(branch, back, normed, weight, x, mid_grad, gain, early, down, up, out):
     grid = Grid()
     group, ys, xs, zs = grid.seq, grid.y, grid.x, grid.z
     rows, width = x.shape
@@ -1232,19 +1367,19 @@
         + [vmem((ys - 1,) + up_block[1:])]
         + [vmem(up_block[1:])] * 3
         + [
-            vmem((ys,) + down_block),
-            vmem((ys - 1,) + down_block),
-            vmem(down_block),
-            vmem((xs - 1,) + down_block[1:]),
+            vmem((ys,) + down_rest[0].shape),
+            vmem((ys - 1,) + down_rest[0].shape),
+            vmem(down_rest[0].shape),
+            vmem((xs - 1,) + down_rest[0].shape[1:]),
         ]
-        + [vmem(down_block[1:])] * 3
+        + [vmem(down_rest[0].shape[1:])] * 3
         + [
             vmem((ys,) + up_rest[0].shape),
             vmem((ys - 1,) + up_rest[0].shape),
             vmem(up_rest[0].shape),
-            vmem((xs - 1,) + up_block[1:]),
+            vmem((xs - 1,) + up_rest[0].shape[1:]),
         ]
-        + [vmem(up_block[1:])] * 3
+        + [vmem(up_rest[0].shape[1:])] * 3
         + [vmem(out_block)] * zs
         + [
             vmem((ys - 1,) + out_block[1:]),
@@ -1268,12 +1403,12 @@
             shape((rows, width), BF16),
             shape((group, share, 3 * wide), F32),
             shape((down_block[2], width), F32),
-            shape((up_block[2], 2 * up_block[3]), F32),
+            shape((up_block[2], up_block[3] + up_rest[0].shape[3]), F32),
             shape(out_block[2:], F32),
             shape(early.shape, F32),
         ],
         scratch_shapes=scratch,
-        compiler_params=params(collective_id=1, has_side_effects=True),
+        compiler_params=params(collective_id=3 * branch + 3, has_side_effects=True),
         cost_estimate=pl.CostEstimate(
             flops=12 * rows * width * width, bytes_accessed=2**25, transcendentals=0
         ),
@@ -1281,8 +1416,44 @@
     )(back, weight, normed, x, mid_grad, gain[None], early, *down, *down_rest, *up, *up_rest, *out)
 
 
+def agree_kernel(count_ref, most_ref, got, send_sem, recv_sem):
+    links = Links(send_sem, recv_sem)
+    others = lax.axis_size("dp") - 1
+    greet([], range(1, others + 1))
+    dp = lax.axis_index("dp")
+    for m in range(1, others + 1):
+        links.start(count_ref, got.at[m - 1], m - 1, m - 1, {"dp": flip(dp, m)})
+    most = count_ref[...]
+    for m in range(1, others + 1):
+        links.arrived(got.at[m - 1], m - 1, {"dp": flip(dp, m)})
+        most = jnp.maximum(most, got[m - 1])
+    most_ref[...] = most
+    links.drain()
+
+
+def agree(count):
+    others = lax.axis_size("dp") - 1
+    block = jnp.broadcast_to(count.astype(F32), (8, 128))
+    most = pl.pallas_call(
+        agree_kernel,
+        in_specs=[any_spec()],
+        out_specs=any_spec(),
+        out_shape=jax.ShapeDtypeStruct((8, 128), F32),
+        scratch_shapes=[
+            pltpu.VMEM((others, 8, 128), F32),
+            pltpu.SemaphoreType.DMA((others,)),
+            pltpu.SemaphoreType.DMA((others,)),
+        ],
+        compiler_params=pltpu.CompilerParams(collective_id=0, has_side_effects=True),
+        name="agree",
+    )(block)
+    return most[0, 0]
+
+
 def layer(
+    branch,
     cap,
+    docs,
     tokens,
     first_gain,
     first_shift,
@@ -1297,35 +1468,31 @@
     up_bias,
     down_weight,
     down_bias,
-    doc_offsets,
-    active,
+    live,
+    rank,
+    ids,
     upstream,
 ):
     group = lax.axis_size("seq")
     outer = lax.axis_size("dp") // 2
     rows, shard, width = tokens.shape
-    length = active.shape[1]
-    docs = doc_offsets.shape[1]
     wide = width // group
     heads = wide // HEAD_DIM
     me = lax.axis_index("seq").astype(jnp.int32)
     dp = lax.axis_index("dp").astype(jnp.int32)
     count = rows * cap
 
-    place = jnp.arange(length, dtype=jnp.int32)
-    ids = jnp.sum((doc_offsets[:, 1:, None] <= place).astype(jnp.int32), axis=1)
-    live = active.reshape(rows, group, shard)
-    rank = jnp.cumsum(live.astype(jnp.int32), axis=2) - 1
     slot = jnp.arange(cap, dtype=jnp.int32)[:, None]
     chosen = (rank[:, :, None, :] == slot) & live[:, :, None, :]
     ids = jnp.sum(
         jnp.where(chosen, ids.reshape(rows, group, 1, shard) + 1, 0), axis=3
     ).reshape(rows, group * cap)
+    tiles = pl.cdiv(group * cap, TILE)
+    ids = jnp.pad(ids, ((0, 0), (0, tiles * TILE - group * cap)))
     padded = -docs % 128
     unit = ids[:, :, None] == 1 + jnp.arange(docs + padded, dtype=jnp.int32)
     q_docs = unit.astype(BF16)
     k_docs = jnp.where(unit | (jnp.arange(docs + padded) >= docs), 0.0, NEG).astype(BF16)
-    tiles = group * cap // TILE
     last = jnp.max(ids.reshape(rows, tiles, TILE), axis=2)
     first = jnp.min(jnp.where(ids == 0, docs + 1, ids).reshape(rows, tiles, TILE), axis=2)
     number = jnp.arange(tiles, dtype=jnp.int32)
@@ -1355,9 +1522,10 @@
     bias_parts = biases.reshape(3, group, wide).transpose(1, 0, 2).reshape(group, 1, 3 * wide)
 
     weight = split_weight(project_weight, group)
-    normed, head_parts = project(x, first_gain, first_shift, weight, bias_parts)
+    normed, head_parts = project(branch, x, first_gain, first_shift, weight, bias_parts)
     ctx_chunks, lse = attend(scalars, head_parts, q_docs, k_docs, cap, heads)
     grad_parts, result, middle_grad, early, *halves = feed_forward(
+        branch,
         ctx_chunks,
         x,
         g,
@@ -1379,7 +1547,7 @@
         scalars, head_parts, ctx_chunks, grad_parts, q_docs, k_docs, lse, cap, heads
     )
     token_grad, project_share, down_share, up_share, out_share, sums = tail(
-        back, normed, weight, x, middle_grad, first_gain, early, down_parts, up_parts, out_parts
+        branch, back, normed, weight, x, middle_grad, first_gain, early, down_parts, up_parts, out_parts
     )
     project_share = project_share.reshape(group, -1, 3, wide).transpose(1, 2, 0, 3)
     devices = 2 * outer * group
@@ -1408,11 +1576,29 @@
     )
 
 
+CAPS = (12, 14, 16, 10)
+
+
 def per_device(*args):
     *most, doc_offsets, exit_layers, layer_index, upstream = args
-    shard = most[0].shape[1]
+    rows, shard, _ = most[0].shape
+    group = lax.axis_size("seq")
     active = exit_layers > layer_index[0]
-    return layer(shard, *most, doc_offsets, active, upstream)
+    place = jnp.arange(active.shape[1], dtype=jnp.int32)
+    ids = jnp.sum((doc_offsets[:, 1:, None] <= place).astype(jnp.int32), axis=1)
+    live = active.reshape(rows, group, shard)
+    rank = jnp.cumsum(live.astype(jnp.int32), axis=2) - 1
+    caps = [shard * k // 16 for k in CAPS]
+    count = agree(jnp.max(jnp.sum(live.astype(jnp.int32), axis=2)))
+    branch = sum(
+        jnp.where((count <= cap) & (count > max([0] + [c for c in caps if c < cap])), k, 0)
+        for k, cap in enumerate(caps)
+    )
+    branch = jnp.where(count <= 0, caps.index(min(caps)), branch)
+    steps = [
+        functools.partial(layer, k, cap, doc_offsets.shape[1]) for k, cap in enumerate(caps)
+    ]
+    return lax.switch(branch, steps, *most, live, rank, ids, upstream)
 
 
 def solution(mesh):

time: 441 us -> 386 us (0.88); the launches traced: 441 us -> 381 us
  Pallas kernels: 402 us -> 307 us
  loops' own time: 0 us -> 26.4 us
  between operations: 1.85 us -> 6.83 us
    pallas_call x1, Pallas kernels: 96.6 us -> 69.8 us  [feed_forward(): pl.pallas_call(functools.partial(mid_kernel, wide), in_specs=[anywhere, h...]
    another operation x0 -> x1, loops' own time: none -> 26.4 us  [per_device(): return lax.switch(branch, steps, *most, live, rank, ids, upstream)]
    pallas_call x1, Pallas kernels: 142 us -> 119 us  [tail(): pl.pallas_call(functools.partial(tail_kernel, wide), in_specs=[any_place,...]
    pallas_call x1, Pallas kernels: 84.3 us -> 64.5 us  [project(): pl.pallas_call(functools.partial(first_kernel, wide), in_specs=[here, her...]
    pallas_call x1, Pallas kernels: 41 us -> 24.8 us  [attend_back(): pl.pallas_call(functools.partial(attend_back_kernel, group, cap, tiles, h...]
    pallas_call x1, Pallas kernels: 38.3 us -> 23.5 us  [attend(): pl.pallas_call(functools.partial(attend_kernel, group, cap, tiles, heads)...]
    pallas_call x0 -> x1, Pallas kernels: none -> 5.89 us  [agree(): pl.pallas_call(agree_kernel, in_specs=[any_spec()], out_specs=any_spec(),...]
  transfers between devices with their start and end apart: 5 -> 5, of which waited for: 0 -> 2; matrix products, arithmetic and copies ran while one was open for 1% -> 1% of each run, Pallas kernels for 9% -> 7%
where the time goes in v3:
time: 386 us; the launch traced here: 381 us
  Pallas kernels  307 us (80%)
  loops' own time  26.4 us (7%)
  local copies, waits for them, and re-layouts  13.6 us (4%)
  other arithmetic  8.97 us (2%)
  starting transfers between devices  8.4 us (2%)
  matrix products  7.77 us (2%)
  between operations  6.83 us (2%)
    pallas_call x1, Pallas kernels, tail(): pl.pallas_call(functools.partial(tail_kernel, wide), in_specs=[any_place,...  119 us
    pallas_call x1, Pallas kernels, feed_forward(): pl.pallas_call(functools.partial(mid_kernel, wide), in_specs=[anywhere, h...  69.8 us
    pallas_call x1, Pallas kernels, project(): pl.pallas_call(functools.partial(first_kernel, wide), in_specs=[here, her...  64.5 us
    another operation x1, loops' own time, per_device(): return lax.switch(branch, steps, *most, live, rank, ids, upstream)  26.4 us
    pallas_call x1, Pallas kernels, attend_back(): pl.pallas_call(functools.partial(attend_back_kernel, group, cap, tiles, h...  24.8 us
    pallas_call x1, Pallas kernels, attend(): pl.pallas_call(functools.partial(attend_kernel, group, cap, tiles, heads)...  23.5 us
    ppermute x5, starting transfers between devices, exchange(): out.append(lax.ppermute(blocks[r], name, partner(name, mask)))  8.4 us
  transfers between devices with their start and end apart: 5, of which 2 were waited for; matrix products, arithmetic and copies ran while one was open for 1% of the time, Pallas kernels for 7%

profile of v3, /device:TPU:0, one launch (start us, length us, event | category | flops | bytes accessed | tf_op | source)
XLA Modules:
  0.0 381.4 jit_solution(5677593331996738861)
XLA Ops:
  1.3 0.7 fusion.112
  2.2 0.6 reduce_max.45
  4.1 5.9 %agree.1 = f32[8,128]{1,0:T(8,128)} custom-call(f32[8,128]{1,0:T(8,128)} %broadcast_in_dim.340.count_ref), custom_call_target="tpu_custom_call" | custom-call | tf_op jit(solution)/shard_map/agree/pallas_call | solution.py:1437
  10.0 1.2 slice.176
  15.8 1.2 reduce-window.6
  17.2 0.8 slice.179
  18.1 357.6 %conditional.1 = (f32[32,1024]{1,0:T(8,128)}, f32[32,4096]{1,0:T(8,128)}, f32[128,1024]{1,0:T(8,128)}, bf16[2,256,1024]{2,1,0:T(8,128)(2,1)}, bf16[2,256,1024]{2...) conditional(s32[]{:T(128)} %bitcast.131, ...), branch_computations={%region_5.0_spmd, %region_10.15_spmd, %region_15.20_spmd, %region_... | conditional | flops 70879584256 | bytes 139393280 | solution.py:1601
  18.9 0.8 select_reduce_fusion
  19.9 0.8 maximum_bitcast_fusion
  20.7 0.6 copy.326.refs_4_
  22.0 1.6 compare_convert_fusion.refs_1_.refs_3_
  23.6 1.3 select_convert_fusion.refs_2_.refs_4_
  25.0 1.3 convolution_convert_fusion.3
  26.2 1.3 convolution_convert_fusion.2
  28.1 64.5 %norm_project.4 = (bf16[384,1024]{1,0:T(8,128)(2,1)}, bf16[8,384,384]{2,1,0:T(8,128)(2,1)}) custom-call(bf16[384,1024]{1,0:T(8,128)(2,1)} %bitcast.276, f32[1,1024]{1,0:T(1,128)S(1)} %bitcast.340, f32[1,1024]{1,0:T(1,128)S(1)} %bitcast.356, bf16[1024,3072]{1,0:T(8,128)(2,1)} %get-tuple-element.459.refs_3_.refs_1_, f32[8,1,384]{2,1,0:T(1,128)} %copy.326.refs_4_), custom_call_target="tpu_custom_call" | custom-call | flops 2415919104 | bytes 8650752 | tf_op jit(solution)/shard_map/cond/branch_0_fun/norm_project/pallas_call | solution.py:358
  92.6 23.5 %attend.4 = (bf16[8,384,128]{2,1,0:T(8,128)(2,1)}, f32[2,6,2,256]{3,2,1,0:T(2,128)}) custom-call(s32[13]{0:T(128)} %pad_add_fusion.sc_ref, bf16[8,384,384]{2,1,0:T(8,128)(2,1)} %get-tuple-element.162.refs_0_, bf16[2,1536,128]{2,1,0:T(8,128)(2,1)} %compare_convert_fusion.refs_1_.refs_3_, bf16[2,1536,128]{2,1,0:T(8,128)(2,1)} %select_convert_fusion.refs_2_.refs_4_), custom_call_target="tpu_custom_call" | custom-call | flops 4831838208 | bytes 3145728 | tf_op jit(solution)/shard_map/cond/branch_0_fun/attend/pallas_call | solution.py:513
  116.2 69.8 %feed_forward.4 = (bf16[8,384,128]{2,1,0:T(8,128)(2,1)}, bf16[384,1024]{1,0:T(8,128)(2,1)}, f32[384,1024]{1,0:T(8,128)}, f32[24,1024]{1,0:T(8,128)}, bf16[2,4,12...) custom-call(bf16[8,384,128]{2,1,0:T(8,128)(2,1)} %get-tuple-element., ...), custom_call_target="tpu_custom_call" | custom-call | flops 22548578304 | bytes 37748736 | tf_op jit(solution)/shard_map/cond/branch_0_fun/feed_forward/pallas_call | solution.py:965
  185.9 2.6 collective-permute-start
  188.5 1.5 collective-permute-start.1
  189.9 2.3 collective-permute-start.3
  192.2 2.1 collective-permute-start.4
  194.3 24.8 %attend_back.4.refs_0_ = bf16[8,384,384]{2,1,0:T(8,128)(2,1)} custom-call(s32[13]{0:T(128)} %pad_add_fusion.sc_ref, bf16[8,384,384]{2,1,0:T(8,128)(2,1)} %get-tuple-element.162.refs_0_, bf16[8,384,128]{2,1,0:T(8,128)(2,1)} %get-tuple-element.163.refs_0_.refs_1_, bf16[8,384,128]{2,1,0:T(8,128)(2,1)} %get-tuple-element.174.refs_2_, ...), custom_call_target="tpu_custom_call" | custom-call | flops 12079595520 | bytes 7864320 | tf_op jit(solution)/shard_map/cond/branch_0_fun/attend_back/pallas_call | solution.py:627
  219.2 2.6 fusion.1
  221.8 1.6 collective-permute-done.refs_8_
  223.9 118.9 %tail.4 = (bf16[384,1024]{1,0:T(8,128)(2,1)}, f32[8,32,384]{2,1,0:T(8,128)}, f32[128,1024]{1,0:T(8,128)}, f32[32,4096]{1,0:T(8,128)}, f32[32,1024]{1,0:T(8,128)}, /*index=5*/f32[24,1024]{1,0:T(8,128)}) custom-call(bf16[8,384,384]{2,1,0:T(8,128)(2,1)} %attend_back.4.refs_0_, bf16[1024,3072]{1,0:T(8,128)(2,1)} %get-tuple-element.459.refs_3_.refs_1_, ...), custom_call_target="tpu_custom_call" | custom-call | flops 4831838208 | bytes 33554432 | tf_op jit(solution)/shard_map/cond/branch_0_fun/tail/pallas_call | solution.py:1397
  342.8 0.8 slice.128
  343.6 0.7 slice_bitcast_fusion
  344.4 0.8 slice.137
  345.4 2.6 fusion.2
  375.7 1.6 copy.469
  377.4 1.9 copy.470
  379.3 1.9 copy.471
  (79 shorter events, 5.7 us)
Async XLA Ops:
  18.1 6.9 %copy-start = (bf16[2,256,1024]{2,1,0:T(8,128)(2,1)S(1)}, bf16[2,256,1024]{2,1,0:T(8,128)(2,1)}, u32[]{:S(2)}) copy-start(bf16[2,256,1024]{2,1,0:T(8,128)(2,1)} %get-tuple-element.439) | copy-start | bytes 3145732 | tf_op jit(solution)/shard_map/cond
  18.9 7.3 %copy-start.4 = (bf16[2,256,1024]{2,1,0:T(8,128)(2,1)S(1)}, bf16[2,256,1024]{2,1,0:T(8,128)(2,1)}, u32[]{:S(2)}) copy-start(bf16[2,256,1024]{2,1,0:T(8,128)(2,1)} %get-tuple-element.463) | copy-start | bytes 3145732 | tf_op jit(solution)/shard_map/cond
  24.9 3.1 copy-start.18
  24.9 3.1 copy-start.33
  92.6 23.5 %copy-start.29 = (f32[4096]{0:T(1024)S(1)}, f32[4096]{0:T(1024)}, u32[]{:S(2)}) copy-start(f32[4096]{0:T(1024)} %get-tuple-element.479) | copy-start | bytes 49156 | tf_op jit(solution)/shard_map/cond
  92.6 23.5 %copy-start.37 = (f32[1024]{0:T(1024)S(1)}, f32[1024]{0:T(1024)}, u32[]{:S(2)}) copy-start(f32[1024]{0:T(1024)} %get-tuple-element.467) | copy-start | bytes 12292 | tf_op jit(solution)/shard_map/cond
  92.6 23.5 %copy-start.41 = (f32[1024]{0:T(1024)S(1)}, f32[1024]{0:T(1024)}, u32[]{:S(2)}) copy-start(f32[1024]{0:T(1024)} %get-tuple-element.471) | copy-start | bytes 12292 | tf_op jit(solution)/shard_map/cond
  92.6 23.5 %copy-start.45 = (f32[1024]{0:T(1024)S(1)}, f32[1024]{0:T(1024)}, u32[]{:S(2)}) copy-start(f32[1024]{0:T(1024)} %get-tuple-element.475) | copy-start | bytes 12292 | tf_op jit(solution)/shard_map/cond
  92.6 23.5 %copy-start.49 = (f32[1024]{0:T(1024)S(1)}, f32[1024]{0:T(1024)}, u32[]{:S(2)}) copy-start(f32[1024]{0:T(1024)} %get-tuple-element.483) | copy-start | bytes 12292 | tf_op jit(solution)/shard_map/cond
  185.9 37.5 %collective-permute-start = (bf16[2,4,128,768]{3,2,1,0:T(8,128)(2,1)}, bf16[2,4,128,768]{3,2,1,0:T(8,128)(2,1)}, u32[]{:S(2)}, u32[]{:S(2)}) collective-permute-start(bf16[2,4,128,768]{3,2,1,0:T(8,128)(2,1)} %get-tuple-element.180), channel_id=1, source_target_pairs={{0,16},{8,24},{16,0},{24,8},{1,17},{9,25},{17,1},{25,9},{2,18},{10... | collective-permute-start | bytes 4718600 | tf_op jit(solution)/shard_map/cond/branch_0_fun/ppermute | solution.py:1022
  188.5 35.4 %collective-permute-start.1 = (bf16[2,4,32,3072]{3,2,1,0:T(8,128)(2,1)}, bf16[2,4,32,3072]{3,2,1,0:T(8,128)(2,1)}, u32[]{:S(2)}, u32[]{:S(2)}) collective-permute-start(bf16[2,4,32,3072]{3,2,1,0:T(8,128)(2,1)} %get-tuple-element.184), channel_id=1, source_target_pairs={{0,1},{1,0},{2,3},{3,2},{4,5},{5,4},{6,7},{7,6},{8,9},{9,8},{10,11... | collective-permute-start | bytes 4718600 | tf_op jit(solution)/shard_map/cond/branch_0_fun/ppermute | solution.py:1022
  189.9 31.8 %collective-permute-start.2 = (bf16[2,2,32,1024]{3,2,1,0:T(8,128)(2,1)}, bf16[2,2,32,1024]{3,2,1,0:T(8,128)(2,1)S(1)}, u32[]{:S(2)}, u32[]{:S(2)}) collective-permute-start(bf16[2,2,32,1024]{3,2,1,0:T(8,128)(2,1)} %get-tuple-element.188), channel_id=1, source_target_pairs={{0,2},{1,3},{2,0},{3,1},{4,6},{5,7},{6,4},{7,5},{8,10},{9,11},{10,... | collective-permute-start | bytes 786440 | tf_op jit(solution)/shard_map/cond/branch_0_fun/ppermute | solution.py:1022
  189.9 31.8 %collective-permute-start.3 = (bf16[2,2,32,1024]{3,2,1,0:T(8,128)(2,1)}, bf16[2,2,32,1024]{3,2,1,0:T(8,128)(2,1)S(1)}, u32[]{:S(2)}, u32[]{:S(2)}) collective-permute-start(bf16[2,2,32,1024]{3,2,1,0:T(8,128)(2,1)} %get-tuple-element.189), channel_id=1, source_target_pairs={{0,4},{1,5},{2,6},{3,7},{4,0},{5,1},{6,2},{7,3},{8,12},{9,13},{10,... | collective-permute-start | bytes 786440 | tf_op jit(solution)/shard_map/cond/branch_0_fun/ppermute | solution.py:1022
  192.2 29.6 %collective-permute-start.4 = (bf16[2,2,32,1024]{3,2,1,0:T(8,128)(2,1)}, bf16[2,2,32,1024]{3,2,1,0:T(8,128)(2,1)}, u32[]{:S(2)}, u32[]{:S(2)}) collective-permute-start(bf16[2,2,32,1024]{3,2,1,0:T(8,128)(2,1)} %get-tuple-element.190), channel_id=1, source_target_pairs={{0,6},{1,7},{2,4},{3,5},{4,2},{5,3},{6,0},{7,1},{8,14},{9,15},{10,... | collective-permute-start | bytes 786440 | tf_op jit(solution)/shard_map/cond/branch_0_fun/ppermute | solution.py:1022
  221.8 2.1 copy-start.14
  221.8 2.1 copy-start.16
  342.8 5.2 %copy-start.9 = (f32[8,32,384]{2,1,0:T(8,128)S(1)}, f32[8,32,384]{2,1,0:T(8,128)}, u32[]{:S(2)}) copy-start(f32[8,32,384]{2,1,0:T(8,128)} %get-tuple-element.193) | copy-start | bytes 1179652 | tf_op jit(solution)/shard_map/cond
  375.7 5.5 %copy-start.13 = (f32[32,3072]{1,0:T(8,128)}, f32[32,3072]{1,0:T(8,128)S(1)}, u32[]{:S(2)}) copy-start(f32[32,3072]{1,0:T(8,128)S(1)} %get-tuple-element.1352) | copy-start | bytes 1179652
  375.7 5.5 %copy-start.22 = (f32[32]{0:T(128)}, f32[32]{0:T(128)S(1)}, u32[]{:S(2)}) copy-start(f32[32]{0:T(128)S(1)} %get-tuple-element.1362) | copy-start | bytes 388
  375.7 5.5 %copy-start.23 = (f32[32]{0:T(128)}, f32[32]{0:T(128)S(1)}, u32[]{:S(2)}) copy-start(f32[32]{0:T(128)S(1)} %get-tuple-element.1358) | copy-start | bytes 388
  375.7 5.5 %copy-start.24 = (f32[32]{0:T(128)}, f32[32]{0:T(128)S(1)}, u32[]{:S(2)}) copy-start(f32[32]{0:T(128)S(1)} %get-tuple-element.1357) | copy-start | bytes 388
  375.7 5.5 %copy-start.25 = (f32[32]{0:T(128)}, f32[32]{0:T(128)S(1)}, u32[]{:S(2)}) copy-start(f32[32]{0:T(128)S(1)} %get-tuple-element.1356) | copy-start | bytes 388
  375.7 5.5 %copy-start.26 = (f32[32]{0:T(128)}, f32[32]{0:T(128)S(1)}, u32[]{:S(2)}) copy-start(f32[32]{0:T(128)S(1)} %get-tuple-element.1351) | copy-start | bytes 388
  375.7 5.5 %copy-start.27 = (f32[32]{0:T(128)}, f32[32]{0:T(128)S(1)}, u32[]{:S(2)}) copy-start(f32[32]{0:T(128)S(1)} %get-tuple-element.1350) | copy-start | bytes 388
